TPU v7x, 256 devices: a whole 4x4x8 slice. The times are simulated.
256 devices in a mesh: dp: 128 (over x_hi, y, z, core), sub: 2 (over x_lo).
Axes of the slice: x: 4 (x_hi: 2, x_lo: 2; x = x_hi * 2 + x_lo), y: 4, z: 8, core: 2. Of those that a mesh axis runs over, the one named last changes fastest.
Arguments:
- views: float32 [131072, 512], P(('dp', 'sub')), may hold values from -1 to 1
- log_sum_exp: float32 [131072], P(('dp', 'sub')), may hold values from 9.5 to 11.5
- loss_weight: float32 [131072], P(('dp', 'sub')), may hold values from 0.5 to 2
- partner: int32 [131072], P(('dp', 'sub')), may hold values from 0 to 131071, as said below
Outputs:
- grad_views: float32 [131072, 512], P(('dp', 'sub'))
Inputs may be any that keep to these rules, and one draw needn't show every extreme that they name: partner is an involution without fixed points (partner[partner[i]] = i); the views of blocks 2k and 2k + 1, 1024 views each, are partners only among themselves.
All inputs are finite; a program needn't handle non-finite values.
Results may differ from a plain program's by a relative error of at most 0.0039.
Values may be sent and summed in bfloat16 or wider, within the bound.
No kernel may reach another device: no remote copies, remote signals or barrier semaphores. Data moves between devices by JAX's collectives and lax.ppermute only.
A program may use at most 128 MiB of HBM per device.

v0:
```python
import functools
import math

import jax
import jax.numpy as jnp
from jax import lax
from jax.experimental import pallas as pl
from jax.experimental.pallas import tpu as pltpu
from jax.sharding import PartitionSpec as P

STEPS = 8
TEMPER = 0.07
SHIFT = 11.5
SCALE = math.log2(math.e) / TEMPER
OFFSET = SHIFT * math.log2(math.e)
EXTRA = 16
TILE = 256


def split3(value):
    high = value.astype(jnp.bfloat16)
    rest = value - high.astype(jnp.float32)
    mid = rest.astype(jnp.bfloat16)
    low = (rest - mid.astype(jnp.float32)).astype(jnp.bfloat16)
    return [high.astype(jnp.float32), mid.astype(jnp.float32), low.astype(jnp.float32)]


def pack_kernel(place_ref, views_ref, lse_ref, weight_ref, partner_ref, pack_ref):
    rows = views_ref.shape[0]
    pack_ref[:rows, :] = views_ref[...].astype(jnp.bfloat16)
    weight = weight_ref[...]
    strength = weight * jnp.exp(SHIFT - lse_ref[...])
    local = partner_ref[...] & 2047
    place = jnp.full(weight.shape, place_ref[0], jnp.int32).astype(jnp.float32)
    lines = split3(strength) + split3(weight)
    lines += [(local >> 8).astype(jnp.float32), (local & 255).astype(jnp.float32), place]
    lines += [jnp.zeros_like(weight)] * (EXTRA - len(lines))
    pack_ref[rows:, :] = jnp.concatenate(lines, axis=0).astype(jnp.bfloat16)


def pack_views(place, views, lse, weight, partner):
    rows, width = views.shape
    whole = pl.BlockSpec(memory_space=pltpu.VMEM)
    return pl.pallas_call(
        pack_kernel,
        out_shape=jax.ShapeDtypeStruct((rows + EXTRA, width), jnp.bfloat16),
        in_specs=[pl.BlockSpec(memory_space=pltpu.SMEM)] + [whole] * 4,
        out_specs=whole,
        name="pack",
    )(place, views, lse.reshape(1, rows), weight.reshape(1, rows), partner.reshape(1, rows))


def statistics(pack_ref):
    rows = pack_ref.shape[0] - EXTRA
    lines = pack_ref[rows:, :].astype(jnp.float32)
    strength = lines[0:1] + lines[1:2] + lines[2:3]
    weight = lines[3:4] + lines[4:5] + lines[5:6]
    partner = lines[6:7] * 256.0 + lines[7:8]
    place = lines[8:9] * float(rows)
    return strength, weight, partner, place


def spread(line):
    return jnp.broadcast_to(line, (128, line.shape[1])).T


def wide(column, width):
    return jnp.concatenate([column] * (width // 128), axis=1)


def scores_of(rows, cols):
    return lax.dot_general(rows, cols, (((1,), (1,)), ((), ())), preferred_element_type=jnp.float32)


def own_kernel(own_ref, other_ref, core_ref, rows_ref, strength_ref, total_ref):
    size = own_ref.shape[0] - EXTRA
    for half, row_pack in enumerate((other_ref, own_ref)):
        row_strength, row_weight, _, row_place = statistics(row_pack)
        row_strength, row_weight = spread(row_strength), spread(row_weight)
        strength_ref[half * size : (half + 1) * size, :] = row_strength
        rows_ref[half * size : (half + 1) * size, :] = row_pack[:size, :]
        for start in range(0, size, TILE):
            here = slice(start, start + TILE)
            rows = row_pack[here, :]
            total = None
            for which, col_pack in enumerate((own_ref, core_ref)):
                strength, weight, partner, _ = statistics(col_pack)
                cols = col_pack[:size, :]
                row_at = lax.broadcasted_iota(jnp.int32, (TILE, size), 0) + start
                raised = jnp.exp2(scores_of(rows, cols) * SCALE - OFFSET)
                value = raised * (wide(row_strength[here], size) + strength)
                pair = partner == row_at.astype(jnp.float32) + row_place
                value = value - jnp.where(pair, wide(row_weight[here], size) + weight, 0.0)
                if half == 1 and which == 0:
                    col_at = lax.broadcasted_iota(jnp.int32, (TILE, size), 1)
                    value = jnp.where(row_at == col_at, 0.0, value)
                term = jnp.dot(value.astype(jnp.bfloat16), cols, preferred_element_type=jnp.float32)
                total = term if total is None else total + term
            total_ref[half * size + start : half * size + start + TILE, :] = total


def own_terms(own, other, core):
    size, width = own.shape[0] - EXTRA, own.shape[1]
    whole = pl.BlockSpec(memory_space=pltpu.VMEM)
    return pl.pallas_call(
        own_kernel,
        out_shape=(
            jax.ShapeDtypeStruct((2 * size, width), jnp.bfloat16),
            jax.ShapeDtypeStruct((2 * size, 128), jnp.float32),
            jax.ShapeDtypeStruct((2 * size, width), jnp.float32),
        ),
        in_specs=[whole] * 3,
        out_specs=(whole,) * 3,
        compiler_params=pltpu.CompilerParams(vmem_limit_bytes=40 * 2**20),
        cost_estimate=pl.CostEstimate(flops=8 * size**2 * width, bytes_accessed=6 * 2**20, transcendentals=0),
        name="own",
    )(own, other, core)


def window_kernel(count, rows_ref, strength_ref, total_ref, *refs):
    col_packs, out_ref = refs[:count], refs[count]
    size = col_packs[0].shape[0] - EXTRA
    rows = rows_ref[...]
    row_strength = wide(strength_ref[...], size)
    total = total_ref[...]
    for col_pack in col_packs:
        lines = col_pack[size:, :].astype(jnp.float32)
        strength = lines[0:1] + lines[1:2] + lines[2:3]
        cols = col_pack[:size, :]
        raised = jnp.exp2(scores_of(rows, cols) * SCALE - OFFSET)
        value = (raised * (row_strength + strength)).astype(jnp.bfloat16)
        total = total + jnp.dot(value, cols, preferred_element_type=jnp.float32)
    out_ref[...] = total.astype(out_ref.dtype)


def window_terms(rows, strength, total, packs, first, tiles, dtype=jnp.float32):
    width = rows.shape[1]
    offset = 0 if total.shape[0] == tiles * TILE else first
    size = packs[0].shape[0] - EXTRA
    whole = pl.BlockSpec(packs[0].shape, lambda i: (0, 0))
    return pl.pallas_call(
        functools.partial(window_kernel, len(packs)),
        grid=(tiles,),
        out_shape=jax.ShapeDtypeStruct((tiles * TILE, width), dtype),
        in_specs=[
            pl.BlockSpec((TILE, width), lambda i: (i + first, 0)),
            pl.BlockSpec((TILE, 128), lambda i: (i + first, 0)),
            pl.BlockSpec((TILE, width), lambda i: (i + offset, 0)),
        ]
        + [whole] * len(packs),
        out_specs=pl.BlockSpec((TILE, width), lambda i: (i, 0)),
        compiler_params=pltpu.CompilerParams(vmem_limit_bytes=40 * 2**20),
        cost_estimate=pl.CostEstimate(
            flops=4 * len(packs) * tiles * TILE * size * width,
            bytes_accessed=tiles * TILE * width * 10 + len(packs) * size * width * 2,
            transcendentals=0,
        ),
        name="window",
    )(rows, strength, total, *packs)


def per_device(lines, views, log_sum_exp, loss_weight, partner):
    dp_place, sub_place = lax.axis_index("dp"), lax.axis_index("sub")
    loop_size = lax.axis_size("dp")
    chips = loop_size // 2

    onward = []
    for place in range(chips):
        turn = 1 if (place + 1) % (chips // lines) == 0 else 0
        later = (place + 1) % chips
        for sub in range(2):
            onward.append(((2 * place) * 2 + sub, (2 * later) * 2 + (sub ^ turn)))
            onward.append(((2 * later + 1) * 2 + (sub ^ turn), (2 * place + 1) * 2 + sub))
    cores = [(place, place ^ 1) for place in range(loop_size)]

    def chip_next(value):
        return lax.ppermute(value, ("dp", "sub"), onward)

    def core_swap(value):
        return lax.ppermute(value, "dp", cores)

    def sub_swap(value):
        return lax.ppermute(value, "sub", [(0, 1), (1, 0)])

    place = ((dp_place % 2) * 2 + sub_place).astype(jnp.int32).reshape(1)
    own = pack_views(place, views, log_sum_exp, loss_weight, partner)
    core = core_swap(own)
    same, cross = chip_next(own), chip_next(core)
    other = sub_swap(own)
    rows, strength, total = own_terms(own, other, core)
    tiles = rows.shape[0] // TILE
    reach = STEPS // 2
    for step in range(1, reach):
        next_same, next_cross = (chip_next(same) if step < reach - 1 else None), chip_next(cross)
        same_over, cross_over = core_swap(same), core_swap(cross)
        total = window_terms(rows, strength, total, (same, same_over), 0, tiles)
        total = window_terms(rows, strength, total, (cross, cross_over), 0, tiles)
        same, cross = next_same, next_cross
    away = sub_swap(window_terms(rows, strength, total, (cross,), 0, tiles // 2, jnp.bfloat16))
    here = window_terms(rows, strength, total, (cross,), tiles // 2, tiles // 2)
    return (here + away.astype(jnp.float32)) * (1.0 / TEMPER)


def solution(mesh):
    in_specs = (P(("dp", "sub"), None), P(("dp", "sub")), P(("dp", "sub")), P(("dp", "sub")))
    out_specs = P(("dp", "sub"), None)
    return jax.shard_map(
        functools.partial(per_device, 2), mesh=mesh, in_specs=in_specs, out_specs=out_specs, check_vma=False
    )
```

profile of v0, /device:TPU:2, one launch (start us, length us, event | category | flops | bytes accessed | tf_op | source)
XLA Modules:
  0.0 91.6 jit_solution(5194088774453093541)
XLA Ops:
  0.0 2.1 %pack.1.own_ref = bf16[528,512]{1,0:T(8,128)(2,1)} custom-call(s32[1]{0:T(128)} %bitcast.place_ref, f32[512,512]{1,0:T(8,128)} %views_ref.1, f32[1,512]{1,0:T(1,128)} %bitcast.4, f32[1,512]{1,0:T(1,128)} %bitcast.5, s32[1,512]{1,0:T(1,128)} %bitcast.6), custom_call_target="tpu_custom_call" | custom-call | tf_op jit(solution)/shard_map/pack/pallas_call | solution.py:44
  2.1 0.0 collective-permute-start.1
  2.1 1.9 %collective-permute-start.2 = (bf16[528,512]{1,0:T(8,128)(2,1)}, bf16[528,512]{1,0:T(8,128)(2,1)S(1)}, u32[]{:S(2)}, u32[]{:S(2)}) collective-permute-start(bf16[528,512]{1,0:T(8,128)(2,1)} %pack.1.own_ref), channel_id=1, source_target_pairs={{0,4},{6,2},{1,5},{7,3},{4,8},{10,6},{5,9},{11,7},{8,12},{14,10},{... | collective-permute-start | bytes 1622024 | tf_op jit(solution)/shard_map/ppermute | solution.py:177
  4.1 0.2 collective-permute-done.1.core_ref
  4.3 1.9 %collective-permute-start.4 = (bf16[528,512]{1,0:T(8,128)(2,1)S(1)}, bf16[528,512]{1,0:T(8,128)(2,1)S(1)}, u32[]{:S(2)}, u32[]{:S(2)}) collective-permute-start(bf16[528,512]{1,0:T(8,128)(2,1)S(1)} %collective-permute-done.1.core_ref), channel_id=1, source_target_pairs={{0,4},{6,2},{1,5},{7,3},{4,8},{10,6},{5,9},{11,7},{8,12},{14,10},{... | collective-permute-start | bytes 1622024 | tf_op jit(solution)/shard_map/ppermute | solution.py:177
  6.2 12.7 %collective-permute-done.2.refs_0_ = bf16[528,512]{1,0:T(8,128)(2,1)S(1)} collective-permute-done((bf16[528,512]{1,0:T(8,128)(2,1)}, bf16[528,512]{1,0:T(8,128)(2,1)S(1)}, u32[]{:S(2)}, u32[]{:S(2)}) %collective-permute-start.2) | collective-permute-done | bytes 540704 | tf_op jit(solution)/shard_map/ppermute | solution.py:177
  18.9 5.8 %collective-permute-done.4.refs_0_ = bf16[528,512]{1,0:T(8,128)(2,1)S(1)} collective-permute-done((bf16[528,512]{1,0:T(8,128)(2,1)S(1)}, bf16[528,512]{1,0:T(8,128)(2,1)S(1)}, u32[]{:S(2)}, u32[]{:S(2)}) %collective-permute-start.4) | collective-permute-done | bytes 540704 | tf_op jit(solution)/shard_map/ppermute | solution.py:177
  24.7 1.8 %collective-permute-start = (bf16[528,512]{1,0:T(8,128)(2,1)}, bf16[528,512]{1,0:T(8,128)(2,1)S(1)}, u32[]{:S(2)}, u32[]{:S(2)}) collective-permute-start(bf16[528,512]{1,0:T(8,128)(2,1)} %pack.1.own_ref), channel_id=1, source_target_pairs={{0,1},{1,0},{2,3},{3,2},{4,5},{5,4},{6,7},{7,6},{8,9},{9,8},{10,11... | collective-permute-start | bytes 1622024 | tf_op jit(solution)/shard_map/ppermute | solution.py:183
  26.5 6.2 %collective-permute-start.3 = (bf16[528,512]{1,0:T(8,128)(2,1)S(1)}, bf16[528,512]{1,0:T(8,128)(2,1)S(1)}, u32[]{:S(2)}, u32[]{:S(2)}) collective-permute-start(bf16[528,512]{1,0:T(8,128)(2,1)S(1)} %collective-permute-done.2.refs_0_), channel_id=1, source_target_pairs={{0,2},{2,0},{4,6},{6,4},{8,10},{10,8},{12,14},{14,12},{16,18},{18,... | collective-permute-start | bytes 1622024 | tf_op jit(solution)/shard_map/ppermute | solution.py:180
  32.8 3.9 %collective-permute-start.5 = (bf16[528,512]{1,0:T(8,128)(2,1)S(1)}, bf16[528,512]{1,0:T(8,128)(2,1)S(1)}, u32[]{:S(2)}, u32[]{:S(2)}) collective-permute-start(bf16[528,512]{1,0:T(8,128)(2,1)S(1)} %collective-permute-done.4.refs_0_), channel_id=1, source_target_pairs={{0,2},{2,0},{4,6},{6,4},{8,10},{10,8},{12,14},{14,12},{16,18},{18,... | collective-permute-start | bytes 1622024 | tf_op jit(solution)/shard_map/ppermute | solution.py:180
  36.7 1.6 %collective-permute-done.8.refs_0_ = bf16[528,512]{1,0:T(8,128)(2,1)S(1)} collective-permute-done((bf16[528,512]{1,0:T(8,128)(2,1)S(1)}, bf16[528,512]{1,0:T(8,128)(2,1)S(1)}, u32[]{:S(2)}, u32[]{:S(2)}) %collective-permute-start.8) | collective-permute-done | bytes 540704 | tf_op jit(solution)/shard_map/ppermute | solution.py:177
  38.3 0.0 collective-permute-start.12
  38.3 0.0 collective-permute-done.other_ref
  38.3 4.2 %collective-permute-start.7 = (bf16[528,512]{1,0:T(8,128)(2,1)S(1)}, bf16[528,512]{1,0:T(8,128)(2,1)S(1)}, u32[]{:S(2)}, u32[]{:S(2)}) collective-permute-start(bf16[528,512]{1,0:T(8,128)(2,1)S(1)} %collective-permute-done.6.refs_0_), channel_id=1, source_target_pairs={{0,2},{2,0},{4,6},{6,4},{8,10},{10,8},{12,14},{14,12},{16,18},{18,... | collective-permute-start | bytes 1622024 | tf_op jit(solution)/shard_map/ppermute | solution.py:180
  42.5 1.0 %copy-done = bf16[528,512]{1,0:T(8,128)(2,1)S(1)} copy-done((bf16[528,512]{1,0:T(8,128)(2,1)S(1)}, bf16[528,512]{1,0:T(8,128)(2,1)}, u32[]{:S(2)}) %copy-start) | copy-done | bytes 540696
  43.5 3.1 %own.1 = (bf16[1024,512]{1,0:T(8,128)(2,1)S(1)}, f32[1024,128]{1,0:T(8,128)S(1)}, f32[1024,512]{1,0:T(8,128)S(1)}) custom-call(bf16[528,512]{1,0:T(8,128)(2,1)S(1)} %copy-done, bf16[528,512]{1,0:T(8,128)(2,1)S(1)} %collective-permute-done.other_ref, bf16[528,512]{1,0:T(8,128)(2,1)S(1)} %collective-permute-done.1.core_ref), custom_call_target="tpu_custom_call" | custom-call | flops 1073741824 | bytes 6291456 | tf_op jit(solution)/shard_map/own/pallas_call | solution.py:105
  46.6 0.1 collective-permute-start.9
  46.7 3.8 %window.8.total_ref = f32[1024,512]{1,0:T(8,128)S(1)} custom-call(bf16[1024,512]{1,0:T(8,128)(2,1)S(1)} %get-tuple-element.8.rows_ref, f32[1024,128]{1,0:T(8,128)S(1)} %get-tuple-element.9.strength_ref, f32[1024,512]{1,0:T(8,128)S(1)} %get-tuple-element.10.total_ref, bf16[528,512]{1,0:T(8,128)(2,1)S(1)} %collective-permute-done.2.refs_0_, ...), custom_call_target="tpu_custom_call" | custom-call | flops 2147483648 | bytes 6291456 | tf_op jit(solution)/shard_map/window/pallas_call | solution.py:141
  50.6 0.8 collective-permute-start.11
  51.3 3.8 %window.9.total_ref = f32[1024,512]{1,0:T(8,128)S(1)} custom-call(bf16[1024,512]{1,0:T(8,128)(2,1)S(1)} %get-tuple-element.8.rows_ref, f32[1024,128]{1,0:T(8,128)S(1)} %get-tuple-element.9.strength_ref, f32[1024,512]{1,0:T(8,128)S(1)} %window.8.total_ref, bf16[528,512]{1,0:T(8,128)(2,1)S(1)} %collective-permute-done.4.refs_0_, ...), custom_call_target="tpu_custom_call" | custom-call | flops 2147483648 | bytes 6291456 | tf_op jit(solution)/shard_map/window/pallas_call | solution.py:141
  55.1 0.1 collective-permute-start.13
  55.2 3.8 %window.10.total_ref = f32[1024,512]{1,0:T(8,128)S(1)} custom-call(bf16[1024,512]{1,0:T(8,128)(2,1)S(1)} %get-tuple-element.8.rows_ref, f32[1024,128]{1,0:T(8,128)S(1)} %get-tuple-element.9.strength_ref, f32[1024,512]{1,0:T(8,128)S(1)} %window.9.total_ref, bf16[528,512]{1,0:T(8,128)(2,1)S(1)} %collective-permute-done.6.refs_0_, ...), custom_call_target="tpu_custom_call" | custom-call | flops 2147483648 | bytes 6291456 | tf_op jit(solution)/shard_map/window/pallas_call | solution.py:141
  59.0 0.1 collective-permute-start.14
  59.1 3.8 %window.11.total_ref = f32[1024,512]{1,0:T(8,128)S(1)} custom-call(bf16[1024,512]{1,0:T(8,128)(2,1)S(1)} %get-tuple-element.8.rows_ref, f32[1024,128]{1,0:T(8,128)S(1)} %get-tuple-element.9.strength_ref, f32[1024,512]{1,0:T(8,128)S(1)} %window.10.total_ref, bf16[528,512]{1,0:T(8,128)(2,1)S(1)} %collective-permute-done.8.refs_0_, ...), custom_call_target="tpu_custom_call" | custom-call | flops 2147483648 | bytes 6291456 | tf_op jit(solution)/shard_map/window/pallas_call | solution.py:141
  63.0 3.8 %window.12.total_ref = f32[1024,512]{1,0:T(8,128)S(1)} custom-call(bf16[1024,512]{1,0:T(8,128)(2,1)S(1)} %get-tuple-element.8.rows_ref, f32[1024,128]{1,0:T(8,128)S(1)} %get-tuple-element.9.strength_ref, f32[1024,512]{1,0:T(8,128)S(1)} %window.11.total_ref, bf16[528,512]{1,0:T(8,128)(2,1)S(1)} %collective-permute-done.10.refs_0_, ...), custom_call_target="tpu_custom_call" | custom-call | flops 2147483648 | bytes 6291456 | tf_op jit(solution)/shard_map/window/pallas_call | solution.py:141
  66.8 3.8 %window.13.total_ref = f32[1024,512]{1,0:T(8,128)S(1)} custom-call(bf16[1024,512]{1,0:T(8,128)(2,1)S(1)} %get-tuple-element.8.rows_ref, f32[1024,128]{1,0:T(8,128)S(1)} %get-tuple-element.9.strength_ref, f32[1024,512]{1,0:T(8,128)S(1)} %window.12.total_ref, bf16[528,512]{1,0:T(8,128)(2,1)S(1)} %collective-permute-done.12.refs_0_, ...), custom_call_target="tpu_custom_call" | custom-call | flops 2147483648 | bytes 6291456 | tf_op jit(solution)/shard_map/window/pallas_call | solution.py:141
  70.6 2.1 %collective-permute-done.14.refs_0_ = bf16[528,512]{1,0:T(8,128)(2,1)S(1)} collective-permute-done((bf16[528,512]{1,0:T(8,128)(2,1)S(1)}, bf16[528,512]{1,0:T(8,128)(2,1)S(1)}, u32[]{:S(2)}, u32[]{:S(2)}) %collective-permute-start.14) | collective-permute-done | bytes 540704 | tf_op jit(solution)/shard_map/ppermute | solution.py:177
  72.7 1.2 %window.15 = bf16[512,512]{1,0:T(8,128)(2,1)S(1)} custom-call(bf16[1024,512]{1,0:T(8,128)(2,1)S(1)} %get-tuple-element.8.rows_ref, f32[1024,128]{1,0:T(8,128)S(1)} %get-tuple-element.9.strength_ref, f32[1024,512]{1,0:T(8,128)S(1)} %window.13.total_ref, bf16[528,512]{1,0:T(8,128)(2,1)S(1)} %collective-permute-done.14.refs_0_), custom_call_target="tpu_custom_call" | custom-call | flops 536870912 | bytes 3145728 | tf_op jit(solution)/shard_map/window/pallas_call | solution.py:141
  73.9 5.5 %collective-permute-start.15 = (bf16[512,512]{1,0:T(8,128)(2,1)S(1)}, bf16[512,512]{1,0:T(8,128)(2,1)S(1)}, u32[]{:S(2)}, u32[]{:S(2)}) collective-permute-start(bf16[512,512]{1,0:T(8,128)(2,1)S(1)} %window.15), channel_id=1, source_target_pairs={{0,1},{1,0},{2,3},{3,2},{4,5},{5,4},{6,7},{7,6},{8,9},{9,8},{10,11... | collective-permute-start | bytes 1572872 | tf_op jit(solution)/shard_map/ppermute | solution.py:183
  79.4 1.2 %window.14 = f32[512,512]{1,0:T(8,128)S(1)} custom-call(bf16[1024,512]{1,0:T(8,128)(2,1)S(1)} %get-tuple-element.8.rows_ref, f32[1024,128]{1,0:T(8,128)S(1)} %get-tuple-element.9.strength_ref, f32[1024,512]{1,0:T(8,128)S(1)} %window.13.total_ref, bf16[528,512]{1,0:T(8,128)(2,1)S(1)} %collective-permute-done.14.refs_0_), custom_call_target="tpu_custom_call" | custom-call | flops 536870912 | bytes 3145728 | tf_op jit(solution)/shard_map/window/pallas_call | solution.py:141
  80.6 9.9 %collective-permute-done.15 = bf16[512,512]{1,0:T(8,128)(2,1)S(1)} collective-permute-done((bf16[512,512]{1,0:T(8,128)(2,1)S(1)}, bf16[512,512]{1,0:T(8,128)(2,1)S(1)}, u32[]{:S(2)}, u32[]{:S(2)}) %collective-permute-start.15) | collective-permute-done | bytes 524320 | tf_op jit(solution)/shard_map/ppermute | solution.py:183
  90.4 1.1 %add_multiply_fusion = f32[512,512]{1,0:T(8,128)} fusion(f32[512,512]{1,0:T(8,128)S(1)} %window.14, bf16[512,512]{1,0:T(8,128)(2,1)S(1)} %collective-permute-done.15), kind=kLoop, calls=%fused_computation | loop fusion | flops 786432 | bytes 2621440 | tf_op jit(solution)/shard_map/mul | solution.py:201
  (13 shorter events, 0.0 us)
Async XLA Ops:
  2.1 2.1 %collective-permute-start.1 = (bf16[528,512]{1,0:T(8,128)(2,1)}, bf16[528,512]{1,0:T(8,128)(2,1)S(1)}, u32[]{:S(2)}, u32[]{:S(2)}) collective-permute-start(bf16[528,512]{1,0:T(8,128)(2,1)} %pack.1.own_ref), channel_id=1, source_target_pairs={{0,2},{2,0},{4,6},{6,4},{8,10},{10,8},{12,14},{14,12},{16,18},{18,... | collective-permute-start | bytes 1622024 | tf_op jit(solution)/shard_map/ppermute | solution.py:180
  2.1 16.8 %collective-permute-start.2 = (bf16[528,512]{1,0:T(8,128)(2,1)}, bf16[528,512]{1,0:T(8,128)(2,1)S(1)}, u32[]{:S(2)}, u32[]{:S(2)}) collective-permute-start(bf16[528,512]{1,0:T(8,128)(2,1)} %pack.1.own_ref), channel_id=1, source_target_pairs={{0,4},{6,2},{1,5},{7,3},{4,8},{10,6},{5,9},{11,7},{8,12},{14,10},{... | collective-permute-start | bytes 1622024 | tf_op jit(solution)/shard_map/ppermute | solution.py:177
  4.3 20.4 %collective-permute-start.4 = (bf16[528,512]{1,0:T(8,128)(2,1)S(1)}, bf16[528,512]{1,0:T(8,128)(2,1)S(1)}, u32[]{:S(2)}, u32[]{:S(2)}) collective-permute-start(bf16[528,512]{1,0:T(8,128)(2,1)S(1)} %collective-permute-done.1.core_ref), channel_id=1, source_target_pairs={{0,4},{6,2},{1,5},{7,3},{4,8},{10,6},{5,9},{11,7},{8,12},{14,10},{... | collective-permute-start | bytes 1622024 | tf_op jit(solution)/shard_map/ppermute | solution.py:177
  18.9 13.8 %collective-permute-start.6 = (bf16[528,512]{1,0:T(8,128)(2,1)S(1)}, bf16[528,512]{1,0:T(8,128)(2,1)S(1)}, u32[]{:S(2)}, u32[]{:S(2)}) collective-permute-start(bf16[528,512]{1,0:T(8,128)(2,1)S(1)} %collective-permute-done.2.refs_0_), channel_id=1, source_target_pairs={{0,4},{6,2},{1,5},{7,3},{4,8},{10,6},{5,9},{11,7},{8,12},{14,10},{... | collective-permute-start | bytes 1622024 | tf_op jit(solution)/shard_map/ppermute | solution.py:177
  24.7 13.6 %collective-permute-start.8 = (bf16[528,512]{1,0:T(8,128)(2,1)S(1)}, bf16[528,512]{1,0:T(8,128)(2,1)S(1)}, u32[]{:S(2)}, u32[]{:S(2)}) collective-permute-start(bf16[528,512]{1,0:T(8,128)(2,1)S(1)} %collective-permute-done.4.refs_0_), channel_id=1, source_target_pairs={{0,4},{6,2},{1,5},{7,3},{4,8},{10,6},{5,9},{11,7},{8,12},{14,10},{... | collective-permute-start | bytes 1622024 | tf_op jit(solution)/shard_map/ppermute | solution.py:177
  24.7 13.6 %collective-permute-start = (bf16[528,512]{1,0:T(8,128)(2,1)}, bf16[528,512]{1,0:T(8,128)(2,1)S(1)}, u32[]{:S(2)}, u32[]{:S(2)}) collective-permute-start(bf16[528,512]{1,0:T(8,128)(2,1)} %pack.1.own_ref), channel_id=1, source_target_pairs={{0,1},{1,0},{2,3},{3,2},{4,5},{5,4},{6,7},{7,6},{8,9},{9,8},{10,11... | collective-permute-start | bytes 1622024 | tf_op jit(solution)/shard_map/ppermute | solution.py:183
  26.5 20.1 %collective-permute-start.3 = (bf16[528,512]{1,0:T(8,128)(2,1)S(1)}, bf16[528,512]{1,0:T(8,128)(2,1)S(1)}, u32[]{:S(2)}, u32[]{:S(2)}) collective-permute-start(bf16[528,512]{1,0:T(8,128)(2,1)S(1)} %collective-permute-done.2.refs_0_), channel_id=1, source_target_pairs={{0,2},{2,0},{4,6},{6,4},{8,10},{10,8},{12,14},{14,12},{16,18},{18,... | collective-permute-start | bytes 1622024 | tf_op jit(solution)/shard_map/ppermute | solution.py:180
  32.8 17.8 %collective-permute-start.10 = (bf16[528,512]{1,0:T(8,128)(2,1)S(1)}, bf16[528,512]{1,0:T(8,128)(2,1)S(1)}, u32[]{:S(2)}, u32[]{:S(2)}) collective-permute-start(bf16[528,512]{1,0:T(8,128)(2,1)S(1)} %collective-permute-done.6.refs_0_), channel_id=1, source_target_pairs={{0,4},{6,2},{1,5},{7,3},{4,8},{10,6},{5,9},{11,7},{8,12},{14,10},{... | collective-permute-start | bytes 1622024 | tf_op jit(solution)/shard_map/ppermute | solution.py:177
  32.8 18.5 %collective-permute-start.5 = (bf16[528,512]{1,0:T(8,128)(2,1)S(1)}, bf16[528,512]{1,0:T(8,128)(2,1)S(1)}, u32[]{:S(2)}, u32[]{:S(2)}) collective-permute-start(bf16[528,512]{1,0:T(8,128)(2,1)S(1)} %collective-permute-done.4.refs_0_), channel_id=1, source_target_pairs={{0,2},{2,0},{4,6},{6,4},{8,10},{10,8},{12,14},{14,12},{16,18},{18,... | collective-permute-start | bytes 1622024 | tf_op jit(solution)/shard_map/ppermute | solution.py:180
  38.3 16.8 %collective-permute-start.12 = (bf16[528,512]{1,0:T(8,128)(2,1)S(1)}, bf16[528,512]{1,0:T(8,128)(2,1)S(1)}, u32[]{:S(2)}, u32[]{:S(2)}) collective-permute-start(bf16[528,512]{1,0:T(8,128)(2,1)S(1)} %collective-permute-done.8.refs_0_), channel_id=1, source_target_pairs={{0,4},{6,2},{1,5},{7,3},{4,8},{10,6},{5,9},{11,7},{8,12},{14,10},{... | collective-permute-start | bytes 1622024 | tf_op jit(solution)/shard_map/ppermute | solution.py:177
  38.3 17.0 %collective-permute-start.7 = (bf16[528,512]{1,0:T(8,128)(2,1)S(1)}, bf16[528,512]{1,0:T(8,128)(2,1)S(1)}, u32[]{:S(2)}, u32[]{:S(2)}) collective-permute-start(bf16[528,512]{1,0:T(8,128)(2,1)S(1)} %collective-permute-done.6.refs_0_), channel_id=1, source_target_pairs={{0,2},{2,0},{4,6},{6,4},{8,10},{10,8},{12,14},{14,12},{16,18},{18,... | collective-permute-start | bytes 1622024 | tf_op jit(solution)/shard_map/ppermute | solution.py:180
  42.5 1.0 %copy-start = (bf16[528,512]{1,0:T(8,128)(2,1)S(1)}, bf16[528,512]{1,0:T(8,128)(2,1)}, u32[]{:S(2)}) copy-start(bf16[528,512]{1,0:T(8,128)(2,1)} %pack.1.own_ref) | copy-start | bytes 1622020
  46.6 12.5 %collective-permute-start.9 = (bf16[528,512]{1,0:T(8,128)(2,1)S(1)}, bf16[528,512]{1,0:T(8,128)(2,1)S(1)}, u32[]{:S(2)}, u32[]{:S(2)}) collective-permute-start(bf16[528,512]{1,0:T(8,128)(2,1)S(1)} %collective-permute-done.8.refs_0_), channel_id=1, source_target_pairs={{0,2},{2,0},{4,6},{6,4},{8,10},{10,8},{12,14},{14,12},{16,18},{18,... | collective-permute-start | bytes 1622024 | tf_op jit(solution)/shard_map/ppermute | solution.py:180
  50.6 12.4 %collective-permute-start.11 = (bf16[528,512]{1,0:T(8,128)(2,1)S(1)}, bf16[528,512]{1,0:T(8,128)(2,1)S(1)}, u32[]{:S(2)}, u32[]{:S(2)}) collective-permute-start(bf16[528,512]{1,0:T(8,128)(2,1)S(1)} %collective-permute-done.10.refs_0_), channel_id=1, source_target_pairs={{0,2},{2,0},{4,6},{6,4},{8,10},{10,8},{12,14},{14,12},{16,18},{18,... | collective-permute-start | bytes 1622024 | tf_op jit(solution)/shard_map/ppermute | solution.py:180
  55.1 11.7 %collective-permute-start.13 = (bf16[528,512]{1,0:T(8,128)(2,1)S(1)}, bf16[528,512]{1,0:T(8,128)(2,1)S(1)}, u32[]{:S(2)}, u32[]{:S(2)}) collective-permute-start(bf16[528,512]{1,0:T(8,128)(2,1)S(1)} %collective-permute-done.12.refs_0_), channel_id=1, source_target_pairs={{0,2},{2,0},{4,6},{6,4},{8,10},{10,8},{12,14},{14,12},{16,18},{18,... | collective-permute-start | bytes 1622024 | tf_op jit(solution)/shard_map/ppermute | solution.py:180
  59.0 13.7 %collective-permute-start.14 = (bf16[528,512]{1,0:T(8,128)(2,1)S(1)}, bf16[528,512]{1,0:T(8,128)(2,1)S(1)}, u32[]{:S(2)}, u32[]{:S(2)}) collective-permute-start(bf16[528,512]{1,0:T(8,128)(2,1)S(1)} %collective-permute-done.12.refs_0_), channel_id=1, source_target_pairs={{0,4},{6,2},{1,5},{7,3},{4,8},{10,6},{5,9},{11,7},{8,12},{14,10},{... | collective-permute-start | bytes 1622024 | tf_op jit(solution)/shard_map/ppermute | solution.py:177
  73.9 16.6 %collective-permute-start.15 = (bf16[512,512]{1,0:T(8,128)(2,1)S(1)}, bf16[512,512]{1,0:T(8,128)(2,1)S(1)}, u32[]{:S(2)}, u32[]{:S(2)}) collective-permute-start(bf16[512,512]{1,0:T(8,128)(2,1)S(1)} %window.15), channel_id=1, source_target_pairs={{0,1},{1,0},{2,3},{3,2},{4,5},{5,4},{6,7},{7,6},{8,9},{9,8},{10,11... | collective-permute-start | bytes 1572872 | tf_op jit(solution)/shard_map/ppermute | solution.py:183
where the time goes:
time: 92 us; the launch traced here: 91.6 us
  waiting for transfers between devices  32.3 us (35%)
  Pallas kernels  30.4 us (33%)
  starting transfers between devices  26.5 us (29%)
  other arithmetic  1.15 us (1%)
  local copies, waits for them, and re-layouts  1.05 us (1%)
    pallas_call x8, Pallas kernels, window_terms(): pl.pallas_call(functools.partial(window_kernel, len(packs)), grid=(tiles,...  25.1 us
    ppermute x7, waiting for transfers between devices, chip_next(): return lax.ppermute(value, ('dp', 'sub'), onward)  22.2 us
    ppermute x7, starting transfers between devices, core_swap(): return lax.ppermute(value, 'dp', cores)  15.3 us
    ppermute x2, waiting for transfers between devices, sub_swap(): return lax.ppermute(value, 'sub', [(0, 1), (1, 0)])  9.87 us
    ppermute x2, starting transfers between devices, sub_swap(): return lax.ppermute(value, 'sub', [(0, 1), (1, 0)])  7.31 us
    ppermute x7, starting transfers between devices, chip_next(): return lax.ppermute(value, ('dp', 'sub'), onward)  3.93 us
    pallas_call x1, Pallas kernels, own_terms(): pl.pallas_call(own_kernel, out_shape=(jax.ShapeDtypeStruct((2 * size, wid...  3.11 us
    pallas_call x1, Pallas kernels, pack_views(): pl.pallas_call(pack_kernel, out_shape=jax.ShapeDtypeStruct((rows + EXTRA,...  2.13 us
  transfers between devices with their start and end apart: 16, of which 6 were waited for; matrix products, arithmetic and copies ran while one was open for 0% of the time, Pallas kernels for 30%

commit v1 on v0

v1 whole, which is shorter than its diff:
```python
import functools
import math

import jax
import jax.numpy as jnp
from jax import lax
from jax.experimental import pallas as pl
from jax.experimental.pallas import tpu as pltpu
from jax.sharding import PartitionSpec as P

STEPS = 8
TEMPER = 0.07
SHIFT = 11.5
SCALE = math.log2(math.e) / TEMPER
OFFSET = SHIFT * math.log2(math.e)
EXTRA = 16
VMEM = 24 * 2**20


def hold(value, token):
    return lax.optimization_barrier((value, token))[0]


def split3(value):
    high = value.astype(jnp.bfloat16)
    rest = value - high.astype(jnp.float32)
    mid = rest.astype(jnp.bfloat16)
    low = (rest - mid.astype(jnp.float32)).astype(jnp.bfloat16)
    return [high.astype(jnp.float32), mid.astype(jnp.float32), low.astype(jnp.float32)]


def pack_kernel(place_ref, views_ref, lse_ref, weight_ref, partner_ref, pack_ref):
    rows = views_ref.shape[0]
    pack_ref[:rows, :] = views_ref[...].astype(jnp.bfloat16)
    weight = weight_ref[...]
    strength = weight * jnp.exp(SHIFT - lse_ref[...])
    local = partner_ref[...] & 2047
    place = jnp.full(weight.shape, place_ref[0], jnp.int32).astype(jnp.float32)
    lines = split3(strength) + split3(weight)
    lines += [(local >> 8).astype(jnp.float32), (local & 255).astype(jnp.float32), place]
    lines += [jnp.zeros_like(weight)] * (EXTRA - len(lines))
    pack_ref[rows:, :] = jnp.concatenate(lines, axis=0).astype(jnp.bfloat16)


def pack_views(place, views, lse, weight, partner):
    rows, width = views.shape
    whole = pl.BlockSpec(memory_space=pltpu.VMEM)
    return pl.pallas_call(
        pack_kernel,
        out_shape=jax.ShapeDtypeStruct((rows + EXTRA, width), jnp.bfloat16),
        in_specs=[pl.BlockSpec(memory_space=pltpu.SMEM)] + [whole] * 4,
        out_specs=whole,
        name="pack",
    )(place, views, lse.reshape(1, rows), weight.reshape(1, rows), partner.reshape(1, rows))


def statistics(pack_ref):
    rows = pack_ref.shape[0] - EXTRA
    lines = pack_ref[rows:, :].astype(jnp.float32)
    strength = lines[0:1] + lines[1:2] + lines[2:3]
    weight = lines[3:4] + lines[4:5] + lines[5:6]
    partner = lines[6:7] * 256.0 + lines[7:8]
    place = lines[8:9] * float(rows)
    return strength, weight, partner, place


def spread(line):
    return jnp.broadcast_to(line, (128, line.shape[1])).T


def wide(column, width):
    return jnp.concatenate([column] * (width // 128), axis=1)


def scores_of(rows, cols):
    return lax.dot_general(rows, cols, (((1,), (1,)), ((), ())), preferred_element_type=jnp.float32)


def own_kernel(diagonal, row_pack, own_ref, core_ref, strength_ref, total_ref):
    size = own_ref.shape[0] - EXTRA
    row_strength, row_weight, _, row_place = statistics(row_pack)
    row_strength, row_weight = spread(row_strength), spread(row_weight)
    strength_ref[...] = row_strength
    rows = row_pack[:size, :]
    row_at = lax.broadcasted_iota(jnp.int32, (size, size), 0)
    total = None
    for which, col_pack in enumerate((own_ref, core_ref)):
        strength, weight, partner, _ = statistics(col_pack)
        cols = col_pack[:size, :]
        raised = jnp.exp2(scores_of(rows, cols) * SCALE - OFFSET)
        value = raised * (wide(row_strength, size) + strength)
        pair = partner == row_at.astype(jnp.float32) + row_place
        value = value - jnp.where(pair, wide(row_weight, size) + weight, 0.0)
        if diagonal and which == 0:
            col_at = lax.broadcasted_iota(jnp.int32, (size, size), 1)
            value = jnp.where(row_at == col_at, 0.0, value)
        term = jnp.dot(value.astype(jnp.bfloat16), cols, preferred_element_type=jnp.float32)
        total = term if total is None else total + term
    total_ref[...] = total


def own_terms(diagonal, rows, own, core):
    size, width = own.shape[0] - EXTRA, own.shape[1]
    whole = pl.BlockSpec(memory_space=pltpu.VMEM)
    return pl.pallas_call(
        functools.partial(own_kernel, diagonal),
        out_shape=(
            jax.ShapeDtypeStruct((size, 128), jnp.float32),
            jax.ShapeDtypeStruct((size, width), jnp.float32),
        ),
        in_specs=[whole] * 3,
        out_specs=(whole,) * 2,
        compiler_params=pltpu.CompilerParams(vmem_limit_bytes=VMEM),
        cost_estimate=pl.CostEstimate(flops=8 * size**2 * width, bytes_accessed=3 * 2**20, transcendentals=0),
        name="own_rows" if diagonal else "other_rows",
    )(rows, own, core)


def window_kernel(halves, count, *refs):
    row_packs, strengths, totals = refs[:halves], refs[halves : 2 * halves], refs[2 * halves : 3 * halves]
    col_packs, outs = refs[3 * halves : 3 * halves + count], refs[3 * halves + count :]
    size = col_packs[0].shape[0] - EXTRA
    for row_pack, row_strength, total_ref, out_ref in zip(row_packs, strengths, totals, outs, strict=True):
        total = total_ref[...]
        for col_pack in col_packs:
            lines = col_pack[size:, :].astype(jnp.float32)
            strength = lines[0:1] + lines[1:2] + lines[2:3]
            cols = col_pack[:size, :]
            raised = jnp.exp2(scores_of(row_pack[:size, :], cols) * SCALE - OFFSET)
            value = (raised * (wide(row_strength[...], size) + strength)).astype(jnp.bfloat16)
            total = total + jnp.dot(value, cols, preferred_element_type=jnp.float32)
        out_ref[...] = total.astype(out_ref.dtype)


def window_terms(row_packs, strengths, totals, col_packs, dtype=jnp.float32):
    halves, count = len(row_packs), len(col_packs)
    size, width = totals[0].shape
    whole = pl.BlockSpec(memory_space=pltpu.VMEM)
    return pl.pallas_call(
        functools.partial(window_kernel, halves, count),
        out_shape=(jax.ShapeDtypeStruct((size, width), dtype),) * halves,
        in_specs=[whole] * (3 * halves + count),
        out_specs=(whole,) * halves,
        input_output_aliases={2 * halves + i: i for i in range(halves)} if dtype == jnp.float32 else {},
        compiler_params=pltpu.CompilerParams(vmem_limit_bytes=VMEM),
        cost_estimate=pl.CostEstimate(
            flops=4 * count * halves * size**2 * width,
            bytes_accessed=halves * size * width * 10 + count * size * width * 2,
            transcendentals=0,
        ),
        name="window",
    )(*row_packs, *strengths, *totals, *col_packs)


def per_device(lines, views, log_sum_exp, loss_weight, partner):
    dp_place, sub_place = lax.axis_index("dp"), lax.axis_index("sub")
    loop_size = lax.axis_size("dp")
    chips = loop_size // 2

    onward = []
    for place in range(chips):
        turn = 1 if (place + 1) % (chips // lines) == 0 else 0
        later = (place + 1) % chips
        for sub in range(2):
            onward.append(((2 * place) * 2 + sub, (2 * later) * 2 + (sub ^ turn)))
            onward.append(((2 * later + 1) * 2 + (sub ^ turn), (2 * place + 1) * 2 + sub))
    cores = [(place, place ^ 1) for place in range(loop_size)]

    def chip_next(value):
        return lax.ppermute(value, ("dp", "sub"), onward)

    def core_swap(value):
        return lax.ppermute(value, "dp", cores)

    def sub_swap(value):
        return lax.ppermute(value, "sub", [(0, 1), (1, 0)])

    place = ((dp_place % 2) * 2 + sub_place).astype(jnp.int32).reshape(1)
    own = pack_views(place, views, log_sum_exp, loss_weight, partner)
    core = core_swap(own)
    same, cross = chip_next(own), chip_next(core)
    other = sub_swap(own)
    own_strength, own_total = own_terms(True, own, own, core)
    same = hold(same, own_total)
    other_strength, other_total = own_terms(False, other, own, core)
    cross = hold(cross, other_total)
    row_packs, strengths, totals = (other, own), (other_strength, own_strength), (other_total, own_total)
    reach = STEPS // 2
    for step in range(1, reach):
        next_same = chip_next(same) if step < reach - 1 else None
        same_over = core_swap(same)
        next_cross, cross_over = chip_next(cross), core_swap(cross)
        totals = window_terms(row_packs, strengths, totals, (same, same_over))
        next_same = hold(next_same, totals[0]) if step < reach - 1 else None
        totals = window_terms(row_packs, strengths, totals, (cross, cross_over))
        next_cross = hold(next_cross, totals[0])
        same, cross = next_same, next_cross
    away = sub_swap(window_terms(row_packs[:1], strengths[:1], totals[:1], (cross,), jnp.bfloat16)[0])
    here = window_terms(row_packs[1:], strengths[1:], totals[1:], (cross,))[0]
    return (here + away.astype(jnp.float32)) * (1.0 / TEMPER)


def solution(mesh):
    in_specs = (P(("dp", "sub"), None), P(("dp", "sub")), P(("dp", "sub")), P(("dp", "sub")))
    out_specs = P(("dp", "sub"), None)
    return jax.shard_map(
        functools.partial(per_device, 2), mesh=mesh, in_specs=in_specs, out_specs=out_specs, check_vma=False
    )
```

time: 92 us -> 82.6 us (0.90)
  waiting for transfers between devices: 32.3 us -> 46.4 us
  starting transfers between devices: 26.5 us -> 12.4 us
  Pallas kernels: 30.4 us -> 21.3 us
    ppermute x7, waiting for transfers between devices: 22.2 us -> 40 us  [chip_next(): return lax.ppermute(value, ('dp', 'sub'), onward)]
    ppermute x7, starting transfers between devices: 15.3 us -> 1.27 us  [core_swap(): return lax.ppermute(value, 'dp', cores)]
    pallas_call x9 -> x10, Pallas kernels: 28.3 us -> 19.2 us  [the longest x8 16.1 us: window_terms(): pl.pallas_call(functools.partial(window_kernel, halves, count), out_shape...]
    ppermute x2, waiting for transfers between devices: 9.87 us -> 6.41 us  [sub_swap(): return lax.ppermute(value, 'sub', [(0, 1), (1, 0)])]
  transfers between devices with their start and end apart: 16 -> 16, of which waited for: 6 -> 8; matrix products, arithmetic and copies ran while one was open for 0% -> 0% of each run, Pallas kernels for 30% -> 22%
where the time goes in v1:
time: 82.6 us; the launch traced here: 82.4 us
  waiting for transfers between devices  46.4 us (56%)
  Pallas kernels  21.3 us (26%)
  starting transfers between devices  12.4 us (15%)
  other arithmetic  1.15 us (1%)
  local copies, waits for them, and re-layouts  1.05 us (1%)
    ppermute x7, waiting for transfers between devices, chip_next(): return lax.ppermute(value, ('dp', 'sub'), onward)  40 us
    pallas_call x8, Pallas kernels, window_terms(): pl.pallas_call(functools.partial(window_kernel, halves, count), out_shape...  16.1 us
    ppermute x2, starting transfers between devices, sub_swap(): return lax.ppermute(value, 'sub', [(0, 1), (1, 0)])  7.26 us
    ppermute x2, waiting for transfers between devices, sub_swap(): return lax.ppermute(value, 'sub', [(0, 1), (1, 0)])  6.41 us
    ppermute x7, starting transfers between devices, chip_next(): return lax.ppermute(value, ('dp', 'sub'), onward)  3.85 us
    pallas_call x2, Pallas kernels, own_terms(): pl.pallas_call(functools.partial(own_kernel, diagonal), out_shape=(jax.Sh...  3.07 us
    pallas_call x1, Pallas kernels, pack_views(): pl.pallas_call(pack_kernel, out_shape=jax.ShapeDtypeStruct((rows + EXTRA,...  2.13 us
  transfers between devices with their start and end apart: 16, of which 8 were waited for; matrix products, arithmetic and copies ran while one was open for 0% of the time, Pallas kernels for 22%

profile of v1, /device:TPU:2, one launch (start us, length us, event | category | flops | bytes accessed | tf_op | source)
XLA Modules:
  0.0 82.4 jit_solution(3074248191927020946)
XLA Ops:
  0.0 2.1 %pack.1.row_pack.own_ref.refs_1_.refs_0_ = bf16[528,512]{1,0:T(8,128)(2,1)} custom-call(s32[1]{0:T(128)} %bitcast.place_ref, f32[512,512]{1,0:T(8,128)} %views_ref.1, f32[1,512]{1,0:T(1,128)} %bitcast.4, f32[1,512]{1,0:T(1,128)} %bitcast.5, s32[1,512]{1,0:T(1,128)} %bitcast.6), custom_call_target="tpu_custom_call" | custom-call | tf_op jit(solution)/shard_map/pack/pallas_call | solution.py:48
  2.1 1.9 %collective-permute-start.2 = (bf16[528,512]{1,0:T(8,128)(2,1)}, bf16[528,512]{1,0:T(8,128)(2,1)S(1)}, u32[]{:S(2)}, u32[]{:S(2)}) collective-permute-start(bf16[528,512]{1,0:T(8,128)(2,1)} %pack.1.row_pack.own_ref.refs_1_.refs_0_), channel_id=1, source_target_pairs={{0,4},{6,2},{1,5},{7,3},{4,8},{10,6},{5,9},{11,7},{8,12},{14,10},{... | collective-permute-start | bytes 1622024 | tf_op jit(solution)/shard_map/ppermute | solution.py:170
  4.1 0.5 collective-permute-start.1
  4.6 1.9 %collective-permute-start.4 = (bf16[528,512]{1,0:T(8,128)(2,1)S(1)}, bf16[528,512]{1,0:T(8,128)(2,1)S(1)}, u32[]{:S(2)}, u32[]{:S(2)}) collective-permute-start(bf16[528,512]{1,0:T(8,128)(2,1)S(1)} %collective-permute-done.core_ref), channel_id=1, source_target_pairs={{0,4},{6,2},{1,5},{7,3},{4,8},{10,6},{5,9},{11,7},{8,12},{14,10},{... | collective-permute-start | bytes 1622024 | tf_op jit(solution)/shard_map/ppermute | solution.py:170
  6.5 1.0 %copy-done = bf16[528,512]{1,0:T(8,128)(2,1)S(1)} copy-done((bf16[528,512]{1,0:T(8,128)(2,1)S(1)}, bf16[528,512]{1,0:T(8,128)(2,1)}, u32[]{:S(2)}) %copy-start) | copy-done | bytes 540696
  7.6 1.5 %own_rows.1 = (f32[512,128]{1,0:T(8,128)S(1)}, f32[512,512]{1,0:T(8,128)S(1)}) custom-call(bf16[528,512]{1,0:T(8,128)(2,1)S(1)} %copy-done, bf16[528,512]{1,0:T(8,128)(2,1)S(1)} %copy-done, bf16[528,512]{1,0:T(8,128)(2,1)S(1)} %collective-permute-done.core_ref), custom_call_target="tpu_custom_call" | custom-call | flops 1073741824 | bytes 3145728 | tf_op jit(solution)/shard_map/own_rows/pallas_call | solution.py:105
  9.1 9.8 %collective-permute-done.2.refs_6_ = bf16[528,512]{1,0:T(8,128)(2,1)S(1)} collective-permute-done((bf16[528,512]{1,0:T(8,128)(2,1)}, bf16[528,512]{1,0:T(8,128)(2,1)S(1)}, u32[]{:S(2)}, u32[]{:S(2)}) %collective-permute-start.2) | collective-permute-done | bytes 540704 | tf_op jit(solution)/shard_map/ppermute | solution.py:170
  18.9 0.0 collective-permute-start.3
  18.9 0.0 collective-permute-start.6
  18.9 0.0 collective-permute-done.1.row_pack.refs_0_
  18.9 1.5 %other_rows.1 = (f32[512,128]{1,0:T(8,128)S(1)}, f32[512,512]{1,0:T(8,128)S(1)}) custom-call(bf16[528,512]{1,0:T(8,128)(2,1)S(1)} %collective-permute-done.1.row_pack.refs_0_, bf16[528,512]{1,0:T(8,128)(2,1)S(1)} %copy-done.1, bf16[528,512]{1,0:T(8,128)(2,1)S(1)} %collective-permute-done.core_ref), custom_call_target="tpu_custom_call" | custom-call | flops 1073741824 | bytes 3145728 | tf_op jit(solution)/shard_map/other_rows/pallas_call | solution.py:105
  20.5 4.2 %collective-permute-done.4.refs_6_ = bf16[528,512]{1,0:T(8,128)(2,1)S(1)} collective-permute-done((bf16[528,512]{1,0:T(8,128)(2,1)S(1)}, bf16[528,512]{1,0:T(8,128)(2,1)S(1)}, u32[]{:S(2)}, u32[]{:S(2)}) %collective-permute-start.4) | collective-permute-done | bytes 540704 | tf_op jit(solution)/shard_map/ppermute | solution.py:170
  24.7 1.2 %collective-permute-start.5 = (bf16[528,512]{1,0:T(8,128)(2,1)S(1)}, bf16[528,512]{1,0:T(8,128)(2,1)S(1)}, u32[]{:S(2)}, u32[]{:S(2)}) collective-permute-start(bf16[528,512]{1,0:T(8,128)(2,1)S(1)} %collective-permute-done.4.refs_6_), channel_id=1, source_target_pairs={{0,2},{2,0},{4,6},{6,4},{8,10},{10,8},{12,14},{14,12},{16,18},{18,... | collective-permute-start | bytes 1622024 | tf_op jit(solution)/shard_map/ppermute | solution.py:173
  25.9 2.4 %window.8 = (f32[512,512]{1,0:T(8,128)S(1)}, f32[512,512]{1,0:T(8,128)S(1)}) custom-call(bf16[528,512]{1,0:T(8,128)(2,1)S(1)} %collective-permute-done.1.row_pack.refs_0_, bf16[528,512]{1,0:T(8,128)(2,1)S(1)} %copy-done.1, f32[512,128]{1,0:T(8,128)S(1)} %get-tuple-element.29.refs_2_.refs_1_, ...), custom_call_target="tpu_custom_call", output_to_operand_aliasing={{0}: (4, {}), {1}: (5, {})} | custom-call | flops 2147483648 | bytes 6291456 | tf_op jit(solution)/shard_map/window/pallas_call | solution.py:139
  28.3 4.2 %collective-permute-done.6.refs_6_ = bf16[528,512]{1,0:T(8,128)(2,1)S(1)} collective-permute-done((bf16[528,512]{1,0:T(8,128)(2,1)S(1)}, bf16[528,512]{1,0:T(8,128)(2,1)S(1)}, u32[]{:S(2)}, u32[]{:S(2)}) %collective-permute-start.6) | collective-permute-done | bytes 540704 | tf_op jit(solution)/shard_map/ppermute | solution.py:170
  32.5 0.1 collective-permute-start.7
  32.6 0.0 collective-permute-start.10
  32.6 2.4 %window.9 = (f32[512,512]{1,0:T(8,128)S(1)}, f32[512,512]{1,0:T(8,128)S(1)}) custom-call(bf16[528,512]{1,0:T(8,128)(2,1)S(1)} %collective-permute-done.1.row_pack.refs_0_, bf16[528,512]{1,0:T(8,128)(2,1)S(1)} %copy-done.1, f32[512,128]{1,0:T(8,128)S(1)} %get-tuple-element.29.refs_2_.refs_1_, ...), custom_call_target="tpu_custom_call", output_to_operand_aliasing={{0}: (4, {}), {1}: (5, {})} | custom-call | flops 2147483648 | bytes 6291456 | tf_op jit(solution)/shard_map/window/pallas_call | solution.py:139
  35.0 4.4 %collective-permute-done.8.refs_6_ = bf16[528,512]{1,0:T(8,128)(2,1)S(1)} collective-permute-done((bf16[528,512]{1,0:T(8,128)(2,1)S(1)}, bf16[528,512]{1,0:T(8,128)(2,1)S(1)}, u32[]{:S(2)}, u32[]{:S(2)}) %collective-permute-start.8) | collective-permute-done | bytes 540704 | tf_op jit(solution)/shard_map/ppermute | solution.py:170
  39.5 2.4 %window.10 = (f32[512,512]{1,0:T(8,128)S(1)}, f32[512,512]{1,0:T(8,128)S(1)}) custom-call(bf16[528,512]{1,0:T(8,128)(2,1)S(1)} %collective-permute-done.1.row_pack.refs_0_, bf16[528,512]{1,0:T(8,128)(2,1)S(1)} %copy-done.1, f32[512,128]{1,0:T(8,128)S(1)} %get-tuple-element.29.refs_2_.refs_1_, ...), custom_call_target="tpu_custom_call", output_to_operand_aliasing={{0}: (4, {}), {1}: (5, {})} | custom-call | flops 2147483648 | bytes 6291456 | tf_op jit(solution)/shard_map/window/pallas_call | solution.py:139
  41.9 4.2 %collective-permute-done.10.refs_6_ = bf16[528,512]{1,0:T(8,128)(2,1)S(1)} collective-permute-done((bf16[528,512]{1,0:T(8,128)(2,1)S(1)}, bf16[528,512]{1,0:T(8,128)(2,1)S(1)}, u32[]{:S(2)}, u32[]{:S(2)}) %collective-permute-start.10) | collective-permute-done | bytes 540704 | tf_op jit(solution)/shard_map/ppermute | solution.py:170
  46.2 2.4 %window.11 = (f32[512,512]{1,0:T(8,128)S(1)}, f32[512,512]{1,0:T(8,128)S(1)}) custom-call(bf16[528,512]{1,0:T(8,128)(2,1)S(1)} %collective-permute-done.1.row_pack.refs_0_, bf16[528,512]{1,0:T(8,128)(2,1)S(1)} %copy-done.1, f32[512,128]{1,0:T(8,128)S(1)} %get-tuple-element.29.refs_2_.refs_1_, ...), custom_call_target="tpu_custom_call", output_to_operand_aliasing={{0}: (4, {}), {1}: (5, {})} | custom-call | flops 2147483648 | bytes 6291456 | tf_op jit(solution)/shard_map/window/pallas_call | solution.py:139
  48.6 4.4 %collective-permute-done.12.refs_6_ = bf16[528,512]{1,0:T(8,128)(2,1)S(1)} collective-permute-done((bf16[528,512]{1,0:T(8,128)(2,1)S(1)}, bf16[528,512]{1,0:T(8,128)(2,1)S(1)}, u32[]{:S(2)}, u32[]{:S(2)}) %collective-permute-start.12) | collective-permute-done | bytes 540704 | tf_op jit(solution)/shard_map/ppermute | solution.py:170
  53.0 0.0 collective-permute-start.14
  53.1 2.4 %window.12 = (f32[512,512]{1,0:T(8,128)S(1)}, f32[512,512]{1,0:T(8,128)S(1)}) custom-call(bf16[528,512]{1,0:T(8,128)(2,1)S(1)} %collective-permute-done.1.row_pack.refs_0_, bf16[528,512]{1,0:T(8,128)(2,1)S(1)} %copy-done.1, f32[512,128]{1,0:T(8,128)S(1)} %get-tuple-element.29.refs_2_.refs_1_, ...), custom_call_target="tpu_custom_call", output_to_operand_aliasing={{0}: (4, {}), {1}: (5, {})} | custom-call | flops 2147483648 | bytes 6291456 | tf_op jit(solution)/shard_map/window/pallas_call | solution.py:139
  55.5 2.4 %window.13 = (f32[512,512]{1,0:T(8,128)S(1)}, f32[512,512]{1,0:T(8,128)S(1)}) custom-call(bf16[528,512]{1,0:T(8,128)(2,1)S(1)} %collective-permute-done.1.row_pack.refs_0_, bf16[528,512]{1,0:T(8,128)(2,1)S(1)} %copy-done.1, f32[512,128]{1,0:T(8,128)S(1)} %get-tuple-element.29.refs_2_.refs_1_, ...), custom_call_target="tpu_custom_call", output_to_operand_aliasing={{0}: (4, {}), {1}: (5, {})} | custom-call | flops 2147483648 | bytes 6291456 | tf_op jit(solution)/shard_map/window/pallas_call | solution.py:139
  58.0 8.7 %collective-permute-done.14.refs_3_ = bf16[528,512]{1,0:T(8,128)(2,1)S(1)} collective-permute-done((bf16[528,512]{1,0:T(8,128)(2,1)S(1)}, bf16[528,512]{1,0:T(8,128)(2,1)S(1)}, u32[]{:S(2)}, u32[]{:S(2)}) %collective-permute-start.14) | collective-permute-done | bytes 540704 | tf_op jit(solution)/shard_map/ppermute | solution.py:170
  66.6 0.7 window.15
  67.4 6.7 %collective-permute-start.15 = (bf16[512,512]{1,0:T(8,128)(2,1)S(1)}, bf16[512,512]{1,0:T(8,128)(2,1)S(1)}, u32[]{:S(2)}, u32[]{:S(2)}) collective-permute-start(bf16[512,512]{1,0:T(8,128)(2,1)S(1)} %window.15), channel_id=1, source_target_pairs={{0,1},{1,0},{2,3},{3,2},{4,5},{5,4},{6,7},{7,6},{8,9},{9,8},{10,11... | collective-permute-start | bytes 1572872 | tf_op jit(solution)/shard_map/ppermute | solution.py:176
  74.1 0.7 window.14
  74.9 6.4 %collective-permute-done.15 = bf16[512,512]{1,0:T(8,128)(2,1)S(1)} collective-permute-done((bf16[512,512]{1,0:T(8,128)(2,1)S(1)}, bf16[512,512]{1,0:T(8,128)(2,1)S(1)}, u32[]{:S(2)}, u32[]{:S(2)}) %collective-permute-start.15) | collective-permute-done | bytes 524320 | tf_op jit(solution)/shard_map/ppermute | solution.py:176
  81.3 1.1 %add_multiply_fusion = f32[512,512]{1,0:T(8,128)} fusion(f32[512,512]{1,0:T(8,128)S(1)} %window.14, bf16[512,512]{1,0:T(8,128)(2,1)S(1)} %collective-permute-done.15), kind=kLoop, calls=%fused_computation | loop fusion | flops 786432 | bytes 2621440 | tf_op jit(solution)/shard_map/mul | solution.py:200
  (16 shorter events, 0.0 us)
Async XLA Ops:
  2.1 2.5 %collective-permute-start = (bf16[528,512]{1,0:T(8,128)(2,1)}, bf16[528,512]{1,0:T(8,128)(2,1)S(1)}, u32[]{:S(2)}, u32[]{:S(2)}) collective-permute-start(bf16[528,512]{1,0:T(8,128)(2,1)} %pack.1.row_pack.own_ref.refs_1_.refs_0_), channel_id=1, source_target_pairs={{0,2},{2,0},{4,6},{6,4},{8,10},{10,8},{12,14},{14,12},{16,18},{18,... | collective-permute-start | bytes 1622024 | tf_op jit(solution)/shard_map/ppermute | solution.py:173
  2.1 16.8 %collective-permute-start.2 = (bf16[528,512]{1,0:T(8,128)(2,1)}, bf16[528,512]{1,0:T(8,128)(2,1)S(1)}, u32[]{:S(2)}, u32[]{:S(2)}) collective-permute-start(bf16[528,512]{1,0:T(8,128)(2,1)} %pack.1.row_pack.own_ref.refs_1_.refs_0_), channel_id=1, source_target_pairs={{0,4},{6,2},{1,5},{7,3},{4,8},{10,6},{5,9},{11,7},{8,12},{14,10},{... | collective-permute-start | bytes 1622024 | tf_op jit(solution)/shard_map/ppermute | solution.py:170
  4.1 14.9 %collective-permute-start.1 = (bf16[528,512]{1,0:T(8,128)(2,1)}, bf16[528,512]{1,0:T(8,128)(2,1)S(1)}, u32[]{:S(2)}, u32[]{:S(2)}) collective-permute-start(bf16[528,512]{1,0:T(8,128)(2,1)} %pack.1.row_pack.own_ref.refs_1_.refs_0_), channel_id=1, source_target_pairs={{0,1},{1,0},{2,3},{3,2},{4,5},{5,4},{6,7},{7,6},{8,9},{9,8},{10,11... | collective-permute-start | bytes 1622024 | tf_op jit(solution)/shard_map/ppermute | solution.py:176
  4.6 20.1 %collective-permute-start.4 = (bf16[528,512]{1,0:T(8,128)(2,1)S(1)}, bf16[528,512]{1,0:T(8,128)(2,1)S(1)}, u32[]{:S(2)}, u32[]{:S(2)}) collective-permute-start(bf16[528,512]{1,0:T(8,128)(2,1)S(1)} %collective-permute-done.core_ref), channel_id=1, source_target_pairs={{0,4},{6,2},{1,5},{7,3},{4,8},{10,6},{5,9},{11,7},{8,12},{14,10},{... | collective-permute-start | bytes 1622024 | tf_op jit(solution)/shard_map/ppermute | solution.py:170
  6.5 1.0 %copy-start = (bf16[528,512]{1,0:T(8,128)(2,1)S(1)}, bf16[528,512]{1,0:T(8,128)(2,1)}, u32[]{:S(2)}) copy-start(bf16[528,512]{1,0:T(8,128)(2,1)} %pack.1.row_pack.own_ref.refs_1_.refs_0_) | copy-start | bytes 1622020
  7.6 11.4 %copy-start.1 = (bf16[528,512]{1,0:T(8,128)(2,1)S(1)}, bf16[528,512]{1,0:T(8,128)(2,1)}, u32[]{:S(2)}) copy-start(bf16[528,512]{1,0:T(8,128)(2,1)} %pack.1.row_pack.own_ref.refs_1_.refs_0_) | copy-start | bytes 1622020
  18.9 7.0 %collective-permute-start.3 = (bf16[528,512]{1,0:T(8,128)(2,1)S(1)}, bf16[528,512]{1,0:T(8,128)(2,1)S(1)}, u32[]{:S(2)}, u32[]{:S(2)}) collective-permute-start(bf16[528,512]{1,0:T(8,128)(2,1)S(1)} %collective-permute-done.2.refs_6_), channel_id=1, source_target_pairs={{0,2},{2,0},{4,6},{6,4},{8,10},{10,8},{12,14},{14,12},{16,18},{18,... | collective-permute-start | bytes 1622024 | tf_op jit(solution)/shard_map/ppermute | solution.py:173
  18.9 13.6 %collective-permute-start.6 = (bf16[528,512]{1,0:T(8,128)(2,1)S(1)}, bf16[528,512]{1,0:T(8,128)(2,1)S(1)}, u32[]{:S(2)}, u32[]{:S(2)}) collective-permute-start(bf16[528,512]{1,0:T(8,128)(2,1)S(1)} %collective-permute-done.2.refs_6_), channel_id=1, source_target_pairs={{0,4},{6,2},{1,5},{7,3},{4,8},{10,6},{5,9},{11,7},{8,12},{14,10},{... | collective-permute-start | bytes 1622024 | tf_op jit(solution)/shard_map/ppermute | solution.py:170
  24.7 7.9 %collective-permute-start.5 = (bf16[528,512]{1,0:T(8,128)(2,1)S(1)}, bf16[528,512]{1,0:T(8,128)(2,1)S(1)}, u32[]{:S(2)}, u32[]{:S(2)}) collective-permute-start(bf16[528,512]{1,0:T(8,128)(2,1)S(1)} %collective-permute-done.4.refs_6_), channel_id=1, source_target_pairs={{0,2},{2,0},{4,6},{6,4},{8,10},{10,8},{12,14},{14,12},{16,18},{18,... | collective-permute-start | bytes 1622024 | tf_op jit(solution)/shard_map/ppermute | solution.py:173
  25.9 13.6 %collective-permute-start.8 = (bf16[528,512]{1,0:T(8,128)(2,1)S(1)}, bf16[528,512]{1,0:T(8,128)(2,1)S(1)}, u32[]{:S(2)}, u32[]{:S(2)}) collective-permute-start(bf16[528,512]{1,0:T(8,128)(2,1)S(1)} %collective-permute-done.4.refs_6_), channel_id=1, source_target_pairs={{0,4},{6,2},{1,5},{7,3},{4,8},{10,6},{5,9},{11,7},{8,12},{14,10},{... | collective-permute-start | bytes 1622024 | tf_op jit(solution)/shard_map/ppermute | solution.py:170
  32.5 7.0 %collective-permute-start.7 = (bf16[528,512]{1,0:T(8,128)(2,1)S(1)}, bf16[528,512]{1,0:T(8,128)(2,1)S(1)}, u32[]{:S(2)}, u32[]{:S(2)}) collective-permute-start(bf16[528,512]{1,0:T(8,128)(2,1)S(1)} %collective-permute-done.6.refs_6_), channel_id=1, source_target_pairs={{0,2},{2,0},{4,6},{6,4},{8,10},{10,8},{12,14},{14,12},{16,18},{18,... | collective-permute-start | bytes 1622024 | tf_op jit(solution)/shard_map/ppermute | solution.py:173
  32.6 13.6 %collective-permute-start.10 = (bf16[528,512]{1,0:T(8,128)(2,1)S(1)}, bf16[528,512]{1,0:T(8,128)(2,1)S(1)}, u32[]{:S(2)}, u32[]{:S(2)}) collective-permute-start(bf16[528,512]{1,0:T(8,128)(2,1)S(1)} %collective-permute-done.6.refs_6_), channel_id=1, source_target_pairs={{0,4},{6,2},{1,5},{7,3},{4,8},{10,6},{5,9},{11,7},{8,12},{14,10},{... | collective-permute-start | bytes 1622024 | tf_op jit(solution)/shard_map/ppermute | solution.py:170
  39.5 6.7 %collective-permute-start.9 = (bf16[528,512]{1,0:T(8,128)(2,1)S(1)}, bf16[528,512]{1,0:T(8,128)(2,1)S(1)}, u32[]{:S(2)}, u32[]{:S(2)}) collective-permute-start(bf16[528,512]{1,0:T(8,128)(2,1)S(1)} %collective-permute-done.8.refs_6_), channel_id=1, source_target_pairs={{0,2},{2,0},{4,6},{6,4},{8,10},{10,8},{12,14},{14,12},{16,18},{18,... | collective-permute-start | bytes 1622024 | tf_op jit(solution)/shard_map/ppermute | solution.py:173
  39.5 13.6 %collective-permute-start.12 = (bf16[528,512]{1,0:T(8,128)(2,1)S(1)}, bf16[528,512]{1,0:T(8,128)(2,1)S(1)}, u32[]{:S(2)}, u32[]{:S(2)}) collective-permute-start(bf16[528,512]{1,0:T(8,128)(2,1)S(1)} %collective-permute-done.8.refs_6_), channel_id=1, source_target_pairs={{0,4},{6,2},{1,5},{7,3},{4,8},{10,6},{5,9},{11,7},{8,12},{14,10},{... | collective-permute-start | bytes 1622024 | tf_op jit(solution)/shard_map/ppermute | solution.py:170
  46.1 6.9 %collective-permute-start.11 = (bf16[528,512]{1,0:T(8,128)(2,1)S(1)}, bf16[528,512]{1,0:T(8,128)(2,1)S(1)}, u32[]{:S(2)}, u32[]{:S(2)}) collective-permute-start(bf16[528,512]{1,0:T(8,128)(2,1)S(1)} %collective-permute-done.10.refs_6_), channel_id=1, source_target_pairs={{0,2},{2,0},{4,6},{6,4},{8,10},{10,8},{12,14},{14,12},{16,18},{18,... | collective-permute-start | bytes 1622024 | tf_op jit(solution)/shard_map/ppermute | solution.py:173
  53.0 2.5 %collective-permute-start.13 = (bf16[528,512]{1,0:T(8,128)(2,1)S(1)}, bf16[528,512]{1,0:T(8,128)(2,1)S(1)}, u32[]{:S(2)}, u32[]{:S(2)}) collective-permute-start(bf16[528,512]{1,0:T(8,128)(2,1)S(1)} %collective-permute-done.12.refs_6_), channel_id=1, source_target_pairs={{0,2},{2,0},{4,6},{6,4},{8,10},{10,8},{12,14},{14,12},{16,18},{18,... | collective-permute-start | bytes 1622024 | tf_op jit(solution)/shard_map/ppermute | solution.py:173
  53.0 13.6 %collective-permute-start.14 = (bf16[528,512]{1,0:T(8,128)(2,1)S(1)}, bf16[528,512]{1,0:T(8,128)(2,1)S(1)}, u32[]{:S(2)}, u32[]{:S(2)}) collective-permute-start(bf16[528,512]{1,0:T(8,128)(2,1)S(1)} %collective-permute-done.12.refs_6_), channel_id=1, source_target_pairs={{0,4},{6,2},{1,5},{7,3},{4,8},{10,6},{5,9},{11,7},{8,12},{14,10},{... | collective-permute-start | bytes 1622024 | tf_op jit(solution)/shard_map/ppermute | solution.py:170
  67.4 13.9 %collective-permute-start.15 = (bf16[512,512]{1,0:T(8,128)(2,1)S(1)}, bf16[512,512]{1,0:T(8,128)(2,1)S(1)}, u32[]{:S(2)}, u32[]{:S(2)}) collective-permute-start(bf16[512,512]{1,0:T(8,128)(2,1)S(1)} %window.15), channel_id=1, source_target_pairs={{0,1},{1,0},{2,3},{3,2},{4,5},{5,4},{6,7},{7,6},{8,9},{9,8},{10,11... | collective-permute-start | bytes 1572872 | tf_op jit(solution)/shard_map/ppermute | solution.py:176

commit v2 on v1

v2 whole, which is shorter than its diff:
```python
import functools
import math

import jax
import jax.numpy as jnp
from jax import lax
from jax.experimental import pallas as pl
from jax.experimental.pallas import tpu as pltpu
from jax.sharding import PartitionSpec as P

STEPS = 8
TEMPER = 0.07
SHIFT = 11.5
SCALE = math.log2(math.e) / TEMPER
OFFSET = SHIFT * math.log2(math.e)
EXTRA = 16
VMEM = 16 * 2**20
CHUNKS = 2
ROWS_AT = 4
PLAN = {
    5: [(["core1"], "mine")],
    6: [(["own1"], "mine")],
    7: [(["core1"], "theirs")],
    8: [(["own1"], "theirs"), (["core2"], "theirs")],
    9: [(["own2"], "theirs")],
    10: [(["core2"], "mine"), (["own2"], "mine")],
    11: [(["core3"], "theirs")],
    12: [(["own3"], "theirs"), (["core3"], "mine")],
    13: [(["own3"], "mine")],
}
WHOLE = pl.BlockSpec(memory_space=pltpu.VMEM)


def hold(value, token):
    return lax.optimization_barrier((value, token))[0]


def split3(value):
    high = value.astype(jnp.bfloat16)
    rest = value - high.astype(jnp.float32)
    mid = rest.astype(jnp.bfloat16)
    low = (rest - mid.astype(jnp.float32)).astype(jnp.bfloat16)
    return [high.astype(jnp.float32), mid.astype(jnp.float32), low.astype(jnp.float32)]


def pack_kernel(place_ref, views_ref, lse_ref, weight_ref, partner_ref, whole_ref, *chunk_refs):
    total = views_ref.shape[0]
    rows = total // len(chunk_refs)
    weight = weight_ref[...]
    strength = weight * jnp.exp(SHIFT - lse_ref[...])
    local = partner_ref[...] & 2047
    place = jnp.full(weight.shape, place_ref[0] * total, jnp.int32).astype(jnp.float32)
    lines = split3(strength) + split3(weight)
    lines += [(local >> 8).astype(jnp.float32), (local & 255).astype(jnp.float32), place]
    lines += [jnp.zeros_like(weight)] * (EXTRA - len(lines))
    extra = jnp.concatenate(lines, axis=0).astype(jnp.bfloat16)
    chunk_refs[0][rows:, :] = extra
    whole_ref[total:, :] = extra
    for i, chunk_ref in enumerate(chunk_refs):
        chunk = views_ref[i * rows : (i + 1) * rows, :].astype(jnp.bfloat16)
        chunk_ref[:rows, :] = chunk
        whole_ref[i * rows : (i + 1) * rows, :] = chunk


def pack_views(place, views, lse, weight, partner):
    rows, width = views.shape
    shapes = [rows + EXTRA] + [rows // CHUNKS + (EXTRA if i == 0 else 0) for i in range(CHUNKS)]
    return pl.pallas_call(
        pack_kernel,
        out_shape=[jax.ShapeDtypeStruct((size, width), jnp.bfloat16) for size in shapes],
        in_specs=[pl.BlockSpec(memory_space=pltpu.SMEM)] + [WHOLE] * 4,
        out_specs=[WHOLE] * (CHUNKS + 1),
        compiler_params=pltpu.CompilerParams(vmem_limit_bytes=VMEM),
        name="pack",
    )(place, views, lse.reshape(1, rows), weight.reshape(1, rows), partner.reshape(1, rows))


def statistics(first_ref):
    rows = first_ref.shape[0] - EXTRA
    lines = first_ref[rows:, :].astype(jnp.float32)
    strength = lines[0:1] + lines[1:2] + lines[2:3]
    weight = lines[3:4] + lines[4:5] + lines[5:6]
    partner = lines[6:7] * 256.0 + lines[7:8]
    return strength, weight, partner, lines[8:9]


def joined(chunk_refs):
    first = chunk_refs[0][: chunk_refs[0].shape[0] - EXTRA, :]
    rest = [ref[...] for ref in chunk_refs[1:]]
    return jnp.concatenate([first] + rest, axis=0) if rest else first


def spread(line):
    return jnp.broadcast_to(line, (128, line.shape[1])).T


def wide(column, width):
    return jnp.concatenate([column] * (width // 128), axis=1)


def scores_of(rows, cols):
    return lax.dot_general(rows, cols, (((1,), (1,)), ((), ())), preferred_element_type=jnp.float32)


def own_kernel(diagonal, row_ref, own_ref, *refs):
    row_refs, own_refs, core_refs = [row_ref], [own_ref], refs[:CHUNKS]
    strength_ref, total_ref = refs[CHUNKS:]
    size = total_ref.shape[0]
    row_strength, row_weight, _, row_place = statistics(row_refs[0])
    row_strength, row_weight = spread(row_strength), spread(row_weight)
    strength_ref[...] = row_strength
    rows = joined(row_refs)
    row_at = lax.broadcasted_iota(jnp.int32, (size, size), 0)
    total = None
    for which, col_refs in enumerate((own_refs, core_refs)):
        strength, weight, partner, _ = statistics(col_refs[0])
        cols = joined(col_refs)
        raised = jnp.exp2(scores_of(rows, cols) * SCALE - OFFSET)
        value = raised * (wide(row_strength, size) + strength)
        pair = partner == row_at.astype(jnp.float32) + row_place
        value = value - jnp.where(pair, wide(row_weight, size) + weight, 0.0)
        if diagonal and which == 0:
            col_at = lax.broadcasted_iota(jnp.int32, (size, size), 1)
            value = jnp.where(row_at == col_at, 0.0, value)
        term = jnp.dot(value.astype(jnp.bfloat16), cols, preferred_element_type=jnp.float32)
        total = term if total is None else total + term
    total_ref[...] = total


def own_terms(diagonal, rows, own, core):
    size, width = own.shape[0] - EXTRA, own.shape[1]
    return pl.pallas_call(
        functools.partial(own_kernel, diagonal),
        out_shape=(
            jax.ShapeDtypeStruct((size, 128), jnp.float32),
            jax.ShapeDtypeStruct((size, width), jnp.float32),
        ),
        in_specs=[WHOLE] * (2 + CHUNKS),
        out_specs=(WHOLE,) * 2,
        compiler_params=pltpu.CompilerParams(vmem_limit_bytes=VMEM),
        cost_estimate=pl.CostEstimate(flops=8 * size**2 * width, bytes_accessed=3 * 2**20, transcendentals=0),
        name="own_rows" if diagonal else "other_rows",
    )(rows, own, *core)


def spread_kernel(*refs):
    count = len(refs) // 2
    for first_ref, out_ref in zip(refs[:count], refs[count:], strict=True):
        out_ref[...] = spread(statistics(first_ref)[0])


def spread_strengths(packs):
    size = packs[1][0].shape[0] - EXTRA
    return pl.pallas_call(
        spread_kernel,
        out_shape=(jax.ShapeDtypeStruct((size, 128), jnp.float32),) * len(packs),
        in_specs=[WHOLE] * len(packs),
        out_specs=(WHOLE,) * len(packs),
        compiler_params=pltpu.CompilerParams(vmem_limit_bytes=VMEM),
        name="spread",
    )(*[pack[0] for pack in packs])


def window_kernel(row_counts, strides, count, *refs):
    refs = list(refs)
    row_packs = [[refs.pop(0) for _ in range(chunks)] for chunks in row_counts]
    strengths = [refs.pop(0) for _ in row_counts]
    totals = [refs.pop(0) for _ in strides]
    col_packs = [[refs.pop(0) for _ in range(CHUNKS)] for _ in range(count)]
    size = strengths[0].shape[0]
    for at, (row_pack, row_strength) in enumerate(zip(row_packs, strengths, strict=True)):
        total, pieces = None, {}
        for col_refs in col_packs:
            strength, _, _, _ = statistics(col_refs[0])
            cols = joined(col_refs)
            raised = jnp.exp2(scores_of(joined(row_pack), cols) * SCALE - OFFSET)
            value = (raised * (wide(row_strength[...], size) + strength)).astype(jnp.bfloat16)
            term = jnp.dot(value, cols, preferred_element_type=jnp.float32)
            total = term if total is None else total + term
        for total_ref, (row, begin, offset) in zip(totals, strides, strict=True):
            if row == at and total_ref.shape[0] >= size:
                total = total + total_ref[offset : offset + size, :]
            elif row == at:
                pieces.setdefault(begin, []).append(total_ref[...].astype(jnp.float32))
        if pieces:
            total = total + jnp.concatenate([pieces[begin][0] for begin in sorted(pieces)], axis=0)
        first = 0
        for out_ref in refs:
            begin, end = max(first, at * size), min(first + out_ref.shape[0], (at + 1) * size)
            if begin < end:
                piece = total[begin - at * size : end - at * size, :]
                out_ref[begin - first : end - first, :] = piece.astype(out_ref.dtype)
            first += out_ref.shape[0]


def window_terms(row_packs, strengths, totals, col_packs, dtype=jnp.float32, alias=False, pieces=1):
    size, width = strengths[0].shape[0], col_packs[0][0].shape[1]
    strides = []
    arrays = []
    for row, array, offset in totals:
        for i, piece in enumerate(array if offset is None else [array]):
            strides.append((row, i * piece.shape[0] if offset is None else 0, offset or 0))
            arrays.append(piece)
    at = sum(len(pack) for pack in row_packs) + len(row_packs)
    return pl.pallas_call(
        functools.partial(window_kernel, tuple(len(pack) for pack in row_packs), tuple(strides), len(col_packs)),
        out_shape=[jax.ShapeDtypeStruct((len(row_packs) * size // pieces, width), dtype)] * pieces,
        in_specs=[WHOLE] * (at + len(arrays) + CHUNKS * len(col_packs)),
        out_specs=[WHOLE] * pieces,
        input_output_aliases={at: 0} if alias else {},
        compiler_params=pltpu.CompilerParams(vmem_limit_bytes=VMEM),
        cost_estimate=pl.CostEstimate(
            flops=4 * len(row_packs) * len(col_packs) * size**2 * width,
            bytes_accessed=len(row_packs) * size * width * 10,
            transcendentals=0,
        ),
        name="window",
    )(*sum(row_packs, []), *strengths, *arrays, *sum(col_packs, []))


def finish_kernel(here_ref, *refs):
    rows = here_ref.shape[0]
    away_ref, out_ref = refs[-2:]
    count = len(refs) - 2
    for i, piece_ref in enumerate(refs[:count]):
        part = slice(i * rows // count, (i + 1) * rows // count)
        total = here_ref[part, :] + piece_ref[...].astype(jnp.float32) + away_ref[part, :].astype(jnp.float32)
        out_ref[part, :] = total * (1.0 / TEMPER)


def finish(here, pieces, away):
    return pl.pallas_call(
        finish_kernel,
        out_shape=jax.ShapeDtypeStruct(here.shape, jnp.float32),
        in_specs=[WHOLE] * (2 + len(pieces)),
        out_specs=WHOLE,
        compiler_params=pltpu.CompilerParams(vmem_limit_bytes=VMEM),
        name="finish",
    )(here, *pieces, away)


def per_device(lines, views, log_sum_exp, loss_weight, partner):
    dp_place, sub_place = lax.axis_index("dp"), lax.axis_index("sub")
    loop_size = lax.axis_size("dp")
    chips = loop_size // 2

    onward = []
    for place in range(chips):
        turn = 1 if (place + 1) % (chips // lines) == 0 else 0
        later = (place + 1) % chips
        for sub in range(2):
            onward.append(((2 * place) * 2 + sub, (2 * later) * 2 + (sub ^ turn)))
            onward.append(((2 * later + 1) * 2 + (sub ^ turn), (2 * place + 1) * 2 + sub))
    cores = [(place, place ^ 1) for place in range(loop_size)]

    def chip_next(value):
        return lax.ppermute(value, ("dp", "sub"), onward)

    def core_swap(value):
        return lax.ppermute(value, "dp", cores)

    def sub_swap(value):
        return lax.ppermute(value, "sub", [(0, 1), (1, 0)])

    def every(move, pack):
        return [move(chunk) for chunk in pack]

    place = ((dp_place % 2) * 2 + sub_place).astype(jnp.int32).reshape(1)
    whole, *own = pack_views(place, views, log_sum_exp, loss_weight, partner)
    core = every(core_swap, own)
    coming = {"core": every(chip_next, core), "own": every(chip_next, own)}
    other = sub_swap(whole)
    size = views.shape[0]
    own_strength, own_total = own_terms(True, whole, whole, core)
    token = own_total

    reach = STEPS // 2
    legs = [(kind, step) for step in range(1, reach) for kind in ("core", "own")] + [("core", reach)]
    plan = PLAN
    packs, strengths, totals, columns = {}, {}, {}, {}
    arrivals, back = 0, None
    for kind, step in legs:
        arrived, sent = [], []
        columns[f"{kind}{step}"] = arrived
        for chunk in coming[kind]:
            chunk = hold(chunk, token)
            arrived.append(chunk)
            if step < reach - (kind == "own"):
                sent.append(chip_next(chunk))
            arrivals += 1
            if arrivals == ROWS_AT:
                other = hold(other, chunk)
                other_strength, other_total = own_terms(False, other, whole, core)
                far = core_swap(other)
                packs = {"mine": [[whole], [other]], "theirs": [core, [far]]}
                strengths["mine"] = [own_strength, other_strength]
                totals["mine"] = [(0, own_total, 0), (1, other_total, 0)]
                token = other_total
            for names, rows in plan.get(arrivals, ()):
                cols = [columns[name] for name in names]
                if rows == "theirs" and rows not in strengths:
                    strengths[rows] = spread_strengths((core, [far]))
                parts = [(row, hold(hold(array, chunk), token), offset) for row, array, offset in totals.get(rows, [])]
                alias = len(parts) > 0 and parts[0][1].shape[0] == 2 * size
                if alias:
                    parts = [(row, parts[0][1], offset) for row, _, offset in parts]
                if rows == "theirs" and names[-1] == f"own{reach - 1}":
                    everything = parts[0][1]
                    back = window_terms(
                        packs[rows][1:], strengths[rows][1:], [(0, everything, size)], cols, jnp.bfloat16, pieces=2
                    )
                    token = window_terms(
                        packs[rows][:1], strengths[rows][:1], [(0, hold(everything, back[0]), 0)], cols, jnp.bfloat16, pieces=2
                    )
                    back, back_own = every(core_swap, back), every(core_swap, token)
                    token = token[0]
                    continue
                (token,) = window_terms(packs[rows], strengths[rows], parts, cols, alias=alias)
                totals[rows] = [(0, token, 0), (1, token, size)]
        coming[kind] = sent
    mine = totals["mine"][0][1]
    (away,) = window_terms(
        packs["mine"][1:], strengths["mine"][1:], [(0, mine, size), (0, back, None)], [arrived], jnp.bfloat16
    )
    away = sub_swap(away)
    (here,) = window_terms(packs["mine"][:1], strengths["mine"][:1], [(0, mine, 0)], [arrived])
    here = finish(here, back_own, away)
    return here


def solution(mesh):
    in_specs = (P(("dp", "sub"), None), P(("dp", "sub")), P(("dp", "sub")), P(("dp", "sub")))
    out_specs = P(("dp", "sub"), None)
    return jax.shard_map(
        functools.partial(per_device, 2), mesh=mesh, in_specs=in_specs, out_specs=out_specs, check_vma=False
    )
```

time: 82.6 us -> 87 us (1.053)
  the two profiles are of different devices: /device:TPU:2 before, /device:TPU:1 now
where the time goes in v2:
time: 87 us; the launch traced here: 86.8 us
  starting transfers between devices  45.9 us (53%)
  Pallas kernels  22.1 us (25%)
  waiting for transfers between devices  13.7 us (16%)
  local copies, waits for them, and re-layouts  4.81 us (6%)
    ppermute x14, starting transfers between devices, chip_next(): return lax.ppermute(value, ('dp', 'sub'), onward)  40.1 us
    pallas_call x15, Pallas kernels, window_terms(): pl.pallas_call(functools.partial(window_kernel, tuple((len(pack) for pack...  17.6 us
    ppermute x2, waiting for transfers between devices, sub_swap(): return lax.ppermute(value, 'sub', [(0, 1), (1, 0)])  11.5 us
    unnamed x17, local copies, waits for them, and re-layouts  4.81 us
    ppermute x7, starting transfers between devices, core_swap(): return lax.ppermute(value, 'dp', cores)  3.53 us
    pallas_call x2, Pallas kernels, own_terms(): pl.pallas_call(functools.partial(own_kernel, diagonal), out_shape=(jax.Sh...  3.09 us
    ppermute x2, starting transfers between devices, sub_swap(): return lax.ppermute(value, 'sub', [(0, 1), (1, 0)])  2.22 us
  transfers between devices with their start and end apart: 23, of which 5 were waited for; matrix products, arithmetic and copies ran while one was open for 2% of the time, Pallas kernels for 23%

profile of v2, /device:TPU:1, one launch (start us, length us, event | category | flops | bytes accessed | tf_op | source)
XLA Modules:
  0.0 86.8 jit_solution(16694243882546958698)
XLA Ops:
  0.0 1.2 %copy-done = f32[512,512]{1,0:T(8,128)S(1)} copy-done((f32[512,512]{1,0:T(8,128)S(1)}, f32[512,512]{1,0:T(8,128)}, u32[]{:S(2)}) %copy-start) | copy-done | bytes 1048600
  3.4 2.1 %collective-permute-start.2 = (bf16[528,512]{1,0:T(8,128)(2,1)S(1)}, bf16[528,512]{1,0:T(8,128)(2,1)S(1)}, u32[]{:S(2)}, u32[]{:S(2)}) collective-permute-start(bf16[528,512]{1,0:T(8,128)(2,1)S(1)} %get-tuple-element.58.row_ref.own_ref.refs_0_), channel_id=1, source_target_pairs={{0,1},{1,0},{2,3},{3,2},{4,5},{5,4},{6,7},{7,6},{8,9},{9,8},{10,11... | collective-permute-start | bytes 1622024 | tf_op jit(solution)/shard_map/ppermute | solution.py:263
  5.5 1.3 %collective-permute-start = (bf16[272,512]{1,0:T(8,128)(2,1)S(1)}, bf16[272,512]{1,0:T(8,128)(2,1)S(1)}, u32[]{:S(2)}, u32[]{:S(2)}) collective-permute-start(bf16[272,512]{1,0:T(8,128)(2,1)S(1)} %get-tuple-element.59), channel_id=1, source_target_pairs={{0,2},{2,0},{4,6},{6,4},{8,10},{10,8},{12,14},{14,12},{16,18},{18,... | collective-permute-start | bytes 835592 | tf_op jit(solution)/shard_map/ppermute | solution.py:260
  6.9 9.1 %collective-permute-start.3 = (bf16[256,512]{1,0:T(8,128)(2,1)S(1)}, bf16[256,512]{1,0:T(8,128)(2,1)S(1)}, u32[]{:S(2)}, u32[]{:S(2)}) collective-permute-start(bf16[256,512]{1,0:T(8,128)(2,1)S(1)} %get-tuple-element.60), channel_id=1, source_target_pairs={{0,4},{6,2},{1,5},{7,3},{4,8},{10,6},{5,9},{11,7},{8,12},{14,10},{... | collective-permute-start | bytes 786440 | tf_op jit(solution)/shard_map/ppermute | solution.py:257
  16.0 1.2 %collective-permute-start.4 = (bf16[272,512]{1,0:T(8,128)(2,1)S(1)}, bf16[272,512]{1,0:T(8,128)(2,1)S(1)}, u32[]{:S(2)}, u32[]{:S(2)}) collective-permute-start(bf16[272,512]{1,0:T(8,128)(2,1)S(1)} %collective-permute-done.refs_0_), channel_id=1, source_target_pairs={{0,4},{6,2},{1,5},{7,3},{4,8},{10,6},{5,9},{11,7},{8,12},{14,10},{... | collective-permute-start | bytes 835592 | tf_op jit(solution)/shard_map/ppermute | solution.py:257
  17.2 0.7 collective-permute-start.8
  18.6 1.5 %own_rows.1 = (f32[512,128]{1,0:T(8,128)S(1)}, f32[512,512]{1,0:T(8,128)S(1)}) custom-call(bf16[528,512]{1,0:T(8,128)(2,1)S(1)} %get-tuple-element.58.row_ref.own_ref.refs_0_, bf16[528,512]{1,0:T(8,128)(2,1)S(1)} %get-tuple-element.58.row_ref.own_ref.refs_0_, bf16[272,512]{1,0:T(8,128)(2,1)S(1)} %collective-permute-done.refs_0_, ...), custom_call_target="tpu_custom_call" | custom-call | flops 1073741824 | bytes 3145728 | tf_op jit(solution)/shard_map/own_rows/pallas_call | solution.py:132
  20.2 0.9 %collective-permute-start.10 = (bf16[528,512]{1,0:T(8,128)(2,1)S(1)}, bf16[528,512]{1,0:T(8,128)(2,1)S(1)}, u32[]{:S(2)}, u32[]{:S(2)}) collective-permute-start(bf16[528,512]{1,0:T(8,128)(2,1)S(1)} %collective-permute-done.2.row_ref.refs_1_.refs_0_), channel_id=1, source_target_pairs={{0,2},{2,0},{4,6},{6,4},{8,10},{10,8},{12,14},{14,12},{16,18},{18,... | collective-permute-start | bytes 1622024 | tf_op jit(solution)/shard_map/ppermute | solution.py:260
  21.1 1.2 %collective-permute-done.4.refs_6_.refs_5_ = bf16[272,512]{1,0:T(8,128)(2,1)S(1)} collective-permute-done((bf16[272,512]{1,0:T(8,128)(2,1)S(1)}, bf16[272,512]{1,0:T(8,128)(2,1)S(1)}, u32[]{:S(2)}, u32[]{:S(2)}) %collective-permute-start.4) | collective-permute-done | bytes 278560 | tf_op jit(solution)/shard_map/ppermute | solution.py:257
  22.3 7.3 %collective-permute-start.5 = (bf16[272,512]{1,0:T(8,128)(2,1)S(1)}, bf16[272,512]{1,0:T(8,128)(2,1)S(1)}, u32[]{:S(2)}, u32[]{:S(2)}) collective-permute-start(bf16[272,512]{1,0:T(8,128)(2,1)S(1)} %collective-permute-done.4.refs_6_.refs_5_), channel_id=1, source_target_pairs={{0,4},{6,2},{1,5},{7,3},{4,8},{10,6},{5,9},{11,7},{8,12},{14,10},{... | collective-permute-start | bytes 835592 | tf_op jit(solution)/shard_map/ppermute | solution.py:257
  29.6 5.8 %collective-permute-start.7 = (bf16[256,512]{1,0:T(8,128)(2,1)S(1)}, bf16[256,512]{1,0:T(8,128)(2,1)S(1)}, u32[]{:S(2)}, u32[]{:S(2)}) collective-permute-start(bf16[256,512]{1,0:T(8,128)(2,1)S(1)} %collective-permute-done.6.refs_7_.refs_6_), channel_id=1, source_target_pairs={{0,4},{6,2},{1,5},{7,3},{4,8},{10,6},{5,9},{11,7},{8,12},{14,10},{... | collective-permute-start | bytes 786440 | tf_op jit(solution)/shard_map/ppermute | solution.py:257
  35.5 1.6 %other_rows.1 = (f32[512,128]{1,0:T(8,128)S(1)}, f32[512,512]{1,0:T(8,128)S(1)}) custom-call(bf16[528,512]{1,0:T(8,128)(2,1)S(1)} %collective-permute-done.2.row_ref.refs_1_.refs_0_, bf16[528,512]{1,0:T(8,128)(2,1)S(1)} %get-tuple-element.58.row_ref.own_ref.refs_0_, bf16[272,512]{1,0:T(8,128)(2,1)S(1)} %collective-permute-done.refs_0_, ...), custom_call_target="tpu_custom_call" | custom-call | flops 1073741824 | bytes 3145728 | tf_op jit(solution)/shard_map/other_rows/pallas_call | solution.py:132
  37.1 1.3 %window.15.refs_5_ = f32[1024,512]{1,0:T(8,128)S(1)} custom-call(bf16[528,512]{1,0:T(8,128)(2,1)S(1)} %get-tuple-element.58.row_ref.own_ref.refs_0_, bf16[528,512]{1,0:T(8,128)(2,1)S(1)} %collective-permute-done.2.row_ref.refs_1_.refs_0_, f32[512,128]{1,0:T(8,128)S(1)} %get-tuple-element.61.refs_2_.refs_1_, ...), custom_call_target="tpu_custom_call" | custom-call | flops 1073741824 | bytes 5242880 | tf_op jit(solution)/shard_map/window/pallas_call | solution.py:205
  38.7 7.3 %collective-permute-start.9 = (bf16[256,512]{1,0:T(8,128)(2,1)S(1)}, bf16[256,512]{1,0:T(8,128)(2,1)S(1)}, u32[]{:S(2)}, u32[]{:S(2)}) collective-permute-start(bf16[256,512]{1,0:T(8,128)(2,1)S(1)} %collective-permute-done.7.refs_8_.refs_7_), channel_id=1, source_target_pairs={{0,4},{6,2},{1,5},{7,3},{4,8},{10,6},{5,9},{11,7},{8,12},{14,10},{... | collective-permute-start | bytes 786440 | tf_op jit(solution)/shard_map/ppermute | solution.py:257
  46.3 1.3 %window.16.refs_5_ = f32[1024,512]{1,0:T(8,128)S(1)} custom-call(bf16[528,512]{1,0:T(8,128)(2,1)S(1)} %get-tuple-element.58.row_ref.own_ref.refs_0_, bf16[528,512]{1,0:T(8,128)(2,1)S(1)} %collective-permute-done.2.row_ref.refs_1_.refs_0_, f32[512,128]{1,0:T(8,128)S(1)} %get-tuple-element.61.refs_2_.refs_1_, ...), custom_call_target="tpu_custom_call", output_to_operand_aliasing={{}: (4, {})} | custom-call | flops 1073741824 | bytes 5242880 | tf_op jit(solution)/shard_map/window/pallas_call | solution.py:205
  47.6 4.2 %collective-permute-start.15 = (bf16[272,512]{1,0:T(8,128)(2,1)S(1)}, bf16[272,512]{1,0:T(8,128)(2,1)S(1)}, u32[]{:S(2)}, u32[]{:S(2)}) collective-permute-start(bf16[272,512]{1,0:T(8,128)(2,1)S(1)} %collective-permute-done.13.refs_7_.refs_6_), channel_id=1, source_target_pairs={{0,4},{6,2},{1,5},{7,3},{4,8},{10,6},{5,9},{11,7},{8,12},{14,10},{... | collective-permute-start | bytes 835592 | tf_op jit(solution)/shard_map/ppermute | solution.py:257
  52.1 1.3 %window.17.refs_6_ = f32[1024,512]{1,0:T(8,128)S(1)} custom-call(bf16[272,512]{1,0:T(8,128)(2,1)S(1)} %collective-permute-done.refs_0_, bf16[256,512]{1,0:T(8,128)(2,1)S(1)} %collective-permute-done.1.refs_1_, bf16[528,512]{1,0:T(8,128)(2,1)S(1)} %collective-permute-done.10.refs_1_.refs_2_.refs_0_, f32[512,128]{1,0:T(8,128)S(1)} %get-tuple-element.78.refs_3_.refs_2_, ...), custom_call_target="tpu_custom_call" | custom-call | flops 1073741824 | bytes 5242880 | tf_op jit(solution)/shard_map/window/pallas_call | solution.py:205
  53.7 1.3 %window.18.refs_6_ = f32[1024,512]{1,0:T(8,128)S(1)} custom-call(bf16[272,512]{1,0:T(8,128)(2,1)S(1)} %collective-permute-done.refs_0_, bf16[256,512]{1,0:T(8,128)(2,1)S(1)} %collective-permute-done.1.refs_1_, bf16[528,512]{1,0:T(8,128)(2,1)S(1)} %collective-permute-done.10.refs_1_.refs_2_.refs_0_, ...), custom_call_target="tpu_custom_call", output_to_operand_aliasing={{}: (5, {})} | custom-call | flops 1073741824 | bytes 5242880 | tf_op jit(solution)/shard_map/window/pallas_call | solution.py:205
  55.2 1.3 %window.19.refs_6_ = f32[1024,512]{1,0:T(8,128)S(1)} custom-call(bf16[272,512]{1,0:T(8,128)(2,1)S(1)} %collective-permute-done.refs_0_, bf16[256,512]{1,0:T(8,128)(2,1)S(1)} %collective-permute-done.1.refs_1_, bf16[528,512]{1,0:T(8,128)(2,1)S(1)} %collective-permute-done.10.refs_1_.refs_2_.refs_0_, ...), custom_call_target="tpu_custom_call", output_to_operand_aliasing={{}: (5, {})} | custom-call | flops 1073741824 | bytes 5242880 | tf_op jit(solution)/shard_map/window/pallas_call | solution.py:205
  56.6 3.2 %collective-permute-start.16 = (bf16[272,512]{1,0:T(8,128)(2,1)S(1)}, bf16[272,512]{1,0:T(8,128)(2,1)S(1)}, u32[]{:S(2)}, u32[]{:S(2)}) collective-permute-start(bf16[272,512]{1,0:T(8,128)(2,1)S(1)} %collective-permute-done.12.refs_7_.refs_6_), channel_id=1, source_target_pairs={{0,4},{6,2},{1,5},{7,3},{4,8},{10,6},{5,9},{11,7},{8,12},{14,10},{... | collective-permute-start | bytes 835592 | tf_op jit(solution)/shard_map/ppermute | solution.py:257
  59.9 1.3 %window.20.refs_6_ = f32[1024,512]{1,0:T(8,128)S(1)} custom-call(bf16[272,512]{1,0:T(8,128)(2,1)S(1)} %collective-permute-done.refs_0_, bf16[256,512]{1,0:T(8,128)(2,1)S(1)} %collective-permute-done.1.refs_1_, bf16[528,512]{1,0:T(8,128)(2,1)S(1)} %collective-permute-done.10.refs_1_.refs_2_.refs_0_, ...), custom_call_target="tpu_custom_call", output_to_operand_aliasing={{}: (5, {})} | custom-call | flops 1073741824 | bytes 5242880 | tf_op jit(solution)/shard_map/window/pallas_call | solution.py:205
  61.7 1.3 %window.21.refs_5_ = f32[1024,512]{1,0:T(8,128)S(1)} custom-call(bf16[528,512]{1,0:T(8,128)(2,1)S(1)} %get-tuple-element.58.row_ref.own_ref.refs_0_, bf16[528,512]{1,0:T(8,128)(2,1)S(1)} %collective-permute-done.2.row_ref.refs_1_.refs_0_, f32[512,128]{1,0:T(8,128)S(1)} %get-tuple-element.61.refs_2_.refs_1_, ...), custom_call_target="tpu_custom_call", output_to_operand_aliasing={{}: (4, {})} | custom-call | flops 1073741824 | bytes 5242880 | tf_op jit(solution)/shard_map/window/pallas_call | solution.py:205
  63.3 1.3 %window.22.refs_5_ = f32[1024,512]{1,0:T(8,128)S(1)} custom-call(bf16[528,512]{1,0:T(8,128)(2,1)S(1)} %get-tuple-element.58.row_ref.own_ref.refs_0_, bf16[528,512]{1,0:T(8,128)(2,1)S(1)} %collective-permute-done.2.row_ref.refs_1_.refs_0_, f32[512,128]{1,0:T(8,128)S(1)} %get-tuple-element.61.refs_2_.refs_1_, ...), custom_call_target="tpu_custom_call", output_to_operand_aliasing={{}: (4, {})} | custom-call | flops 1073741824 | bytes 5242880 | tf_op jit(solution)/shard_map/window/pallas_call | solution.py:205
  64.8 1.3 %window.23.refs_2_.refs_3_ = f32[1024,512]{1,0:T(8,128)S(1)} custom-call(bf16[272,512]{1,0:T(8,128)(2,1)S(1)} %collective-permute-done.refs_0_, bf16[256,512]{1,0:T(8,128)(2,1)S(1)} %collective-permute-done.1.refs_1_, bf16[528,512]{1,0:T(8,128)(2,1)S(1)} %collective-permute-done.10.refs_1_.refs_2_.refs_0_, ...), custom_call_target="tpu_custom_call", output_to_operand_aliasing={{}: (5, {})} | custom-call | flops 1073741824 | bytes 5242880 | tf_op jit(solution)/shard_map/window/pallas_call | solution.py:205
  66.1 0.8 window.24
  67.5 0.7 window.25
  68.4 1.3 %window.26.refs_5_ = f32[1024,512]{1,0:T(8,128)S(1)} custom-call(bf16[528,512]{1,0:T(8,128)(2,1)S(1)} %get-tuple-element.58.row_ref.own_ref.refs_0_, bf16[528,512]{1,0:T(8,128)(2,1)S(1)} %collective-permute-done.2.row_ref.refs_1_.refs_0_, f32[512,128]{1,0:T(8,128)S(1)} %get-tuple-element.61.refs_2_.refs_1_, ...), custom_call_target="tpu_custom_call", output_to_operand_aliasing={{}: (4, {})} | custom-call | flops 1073741824 | bytes 5242880 | tf_op jit(solution)/shard_map/window/pallas_call | solution.py:205
  69.9 1.3 %window.27.refs_2_ = f32[1024,512]{1,0:T(8,128)S(1)} custom-call(bf16[528,512]{1,0:T(8,128)(2,1)S(1)} %get-tuple-element.58.row_ref.own_ref.refs_0_, bf16[528,512]{1,0:T(8,128)(2,1)S(1)} %collective-permute-done.2.row_ref.refs_1_.refs_0_, f32[512,128]{1,0:T(8,128)S(1)} %get-tuple-element.61.refs_2_.refs_1_, ...), custom_call_target="tpu_custom_call", output_to_operand_aliasing={{}: (4, {})} | custom-call | flops 1073741824 | bytes 5242880 | tf_op jit(solution)/shard_map/window/pallas_call | solution.py:205
  71.3 0.7 window.29
  72.8 0.7 window.28.here_ref
  74.2 11.5 %collective-permute-done.22.refs_2_ = bf16[512,512]{1,0:T(8,128)(2,1)S(1)} collective-permute-done((bf16[512,512]{1,0:T(8,128)(2,1)S(1)}, bf16[512,512]{1,0:T(8,128)(2,1)S(1)}, u32[]{:S(2)}, u32[]{:S(2)}) %collective-permute-start.22) | collective-permute-done | bytes 524320 | tf_op jit(solution)/shard_map/ppermute | solution.py:263
  85.6 1.1 %finish.1 = f32[512,512]{1,0:T(8,128)} custom-call(f32[512,512]{1,0:T(8,128)S(1)} %window.28.here_ref, bf16[256,512]{1,0:T(8,128)(2,1)S(1)} %collective-permute-done.18.refs_0_, bf16[256,512]{1,0:T(8,128)(2,1)S(1)} %collective-permute-done.19.refs_1_, bf16[512,512]{1,0:T(8,128)(2,1)S(1)} %collective-permute-done.22.refs_2_), custom_call_target="tpu_custom_call" | custom-call | tf_op jit(solution)/shard_map/finish/pallas_call | solution.py:232
  (51 shorter events, 7.5 us)
Async XLA Ops:
  0.0 1.2 %copy-start = (f32[512,512]{1,0:T(8,128)S(1)}, f32[512,512]{1,0:T(8,128)}, u32[]{:S(2)}) copy-start(f32[512,512]{1,0:T(8,128)} %views_ref.1) | copy-start | bytes 3145732
  1.2 0.7 copy-start.1
  1.9 0.7 copy-start.2
  2.6 0.7 copy-start.3
  3.4 16.8 %collective-permute-start.2 = (bf16[528,512]{1,0:T(8,128)(2,1)S(1)}, bf16[528,512]{1,0:T(8,128)(2,1)S(1)}, u32[]{:S(2)}, u32[]{:S(2)}) collective-permute-start(bf16[528,512]{1,0:T(8,128)(2,1)S(1)} %get-tuple-element.58.row_ref.own_ref.refs_0_), channel_id=1, source_target_pairs={{0,1},{1,0},{2,3},{3,2},{4,5},{5,4},{6,7},{7,6},{8,9},{9,8},{10,11... | collective-permute-start | bytes 1622024 | tf_op jit(solution)/shard_map/ppermute | solution.py:263
  5.5 10.5 %collective-permute-start = (bf16[272,512]{1,0:T(8,128)(2,1)S(1)}, bf16[272,512]{1,0:T(8,128)(2,1)S(1)}, u32[]{:S(2)}, u32[]{:S(2)}) collective-permute-start(bf16[272,512]{1,0:T(8,128)(2,1)S(1)} %get-tuple-element.59), channel_id=1, source_target_pairs={{0,2},{2,0},{4,6},{6,4},{8,10},{10,8},{12,14},{14,12},{16,18},{18,... | collective-permute-start | bytes 835592 | tf_op jit(solution)/shard_map/ppermute | solution.py:260
  6.8 11.1 %collective-permute-start.1 = (bf16[256,512]{1,0:T(8,128)(2,1)S(1)}, bf16[256,512]{1,0:T(8,128)(2,1)S(1)}, u32[]{:S(2)}, u32[]{:S(2)}) collective-permute-start(bf16[256,512]{1,0:T(8,128)(2,1)S(1)} %get-tuple-element.60), channel_id=1, source_target_pairs={{0,2},{2,0},{4,6},{6,4},{8,10},{10,8},{12,14},{14,12},{16,18},{18,... | collective-permute-start | bytes 786440 | tf_op jit(solution)/shard_map/ppermute | solution.py:260
  6.9 13.3 %collective-permute-start.3 = (bf16[256,512]{1,0:T(8,128)(2,1)S(1)}, bf16[256,512]{1,0:T(8,128)(2,1)S(1)}, u32[]{:S(2)}, u32[]{:S(2)}) collective-permute-start(bf16[256,512]{1,0:T(8,128)(2,1)S(1)} %get-tuple-element.60), channel_id=1, source_target_pairs={{0,4},{6,2},{1,5},{7,3},{4,8},{10,6},{5,9},{11,7},{8,12},{14,10},{... | collective-permute-start | bytes 786440 | tf_op jit(solution)/shard_map/ppermute | solution.py:257
  16.0 6.3 %collective-permute-start.4 = (bf16[272,512]{1,0:T(8,128)(2,1)S(1)}, bf16[272,512]{1,0:T(8,128)(2,1)S(1)}, u32[]{:S(2)}, u32[]{:S(2)}) collective-permute-start(bf16[272,512]{1,0:T(8,128)(2,1)S(1)} %collective-permute-done.refs_0_), channel_id=1, source_target_pairs={{0,4},{6,2},{1,5},{7,3},{4,8},{10,6},{5,9},{11,7},{8,12},{14,10},{... | collective-permute-start | bytes 835592 | tf_op jit(solution)/shard_map/ppermute | solution.py:257
  17.2 18.3 %collective-permute-start.8 = (bf16[272,512]{1,0:T(8,128)(2,1)S(1)}, bf16[272,512]{1,0:T(8,128)(2,1)S(1)}, u32[]{:S(2)}, u32[]{:S(2)}) collective-permute-start(bf16[272,512]{1,0:T(8,128)(2,1)S(1)} %get-tuple-element.59), channel_id=1, source_target_pairs={{0,4},{6,2},{1,5},{7,3},{4,8},{10,6},{5,9},{11,7},{8,12},{14,10},{... | collective-permute-start | bytes 835592 | tf_op jit(solution)/shard_map/ppermute | solution.py:257
  17.9 11.7 %collective-permute-start.6 = (bf16[256,512]{1,0:T(8,128)(2,1)S(1)}, bf16[256,512]{1,0:T(8,128)(2,1)S(1)}, u32[]{:S(2)}, u32[]{:S(2)}) collective-permute-start(bf16[256,512]{1,0:T(8,128)(2,1)S(1)} %collective-permute-done.1.refs_1_), channel_id=1, source_target_pairs={{0,4},{6,2},{1,5},{7,3},{4,8},{10,6},{5,9},{11,7},{8,12},{14,10},{... | collective-permute-start | bytes 786440 | tf_op jit(solution)/shard_map/ppermute | solution.py:257
  20.2 31.7 %collective-permute-start.10 = (bf16[528,512]{1,0:T(8,128)(2,1)S(1)}, bf16[528,512]{1,0:T(8,128)(2,1)S(1)}, u32[]{:S(2)}, u32[]{:S(2)}) collective-permute-start(bf16[528,512]{1,0:T(8,128)(2,1)S(1)} %collective-permute-done.2.row_ref.refs_1_.refs_0_), channel_id=1, source_target_pairs={{0,2},{2,0},{4,6},{6,4},{8,10},{10,8},{12,14},{14,12},{16,18},{18,... | collective-permute-start | bytes 1622024 | tf_op jit(solution)/shard_map/ppermute | solution.py:260
  22.3 14.8 %collective-permute-start.5 = (bf16[272,512]{1,0:T(8,128)(2,1)S(1)}, bf16[272,512]{1,0:T(8,128)(2,1)S(1)}, u32[]{:S(2)}, u32[]{:S(2)}) collective-permute-start(bf16[272,512]{1,0:T(8,128)(2,1)S(1)} %collective-permute-done.4.refs_6_.refs_5_), channel_id=1, source_target_pairs={{0,4},{6,2},{1,5},{7,3},{4,8},{10,6},{5,9},{11,7},{8,12},{14,10},{... | collective-permute-start | bytes 835592 | tf_op jit(solution)/shard_map/ppermute | solution.py:257
  29.6 9.1 %collective-permute-start.7 = (bf16[256,512]{1,0:T(8,128)(2,1)S(1)}, bf16[256,512]{1,0:T(8,128)(2,1)S(1)}, u32[]{:S(2)}, u32[]{:S(2)}) collective-permute-start(bf16[256,512]{1,0:T(8,128)(2,1)S(1)} %collective-permute-done.6.refs_7_.refs_6_), channel_id=1, source_target_pairs={{0,4},{6,2},{1,5},{7,3},{4,8},{10,6},{5,9},{11,7},{8,12},{14,10},{... | collective-permute-start | bytes 786440 | tf_op jit(solution)/shard_map/ppermute | solution.py:257
  35.4 18.0 %collective-permute-start.11 = (bf16[256,512]{1,0:T(8,128)(2,1)S(1)}, bf16[256,512]{1,0:T(8,128)(2,1)S(1)}, u32[]{:S(2)}, u32[]{:S(2)}) collective-permute-start(bf16[256,512]{1,0:T(8,128)(2,1)S(1)} %collective-permute-done.3.refs_7_.refs_8_), channel_id=1, source_target_pairs={{0,4},{6,2},{1,5},{7,3},{4,8},{10,6},{5,9},{11,7},{8,12},{14,10},{... | collective-permute-start | bytes 786440 | tf_op jit(solution)/shard_map/ppermute | solution.py:257
  35.5 12.2 %collective-permute-start.13 = (bf16[272,512]{1,0:T(8,128)(2,1)S(1)}, bf16[272,512]{1,0:T(8,128)(2,1)S(1)}, u32[]{:S(2)}, u32[]{:S(2)}) collective-permute-start(bf16[272,512]{1,0:T(8,128)(2,1)S(1)} %collective-permute-done.8.refs_6_.refs_7_), channel_id=1, source_target_pairs={{0,4},{6,2},{1,5},{7,3},{4,8},{10,6},{5,9},{11,7},{8,12},{14,10},{... | collective-permute-start | bytes 835592 | tf_op jit(solution)/shard_map/ppermute | solution.py:257
  38.7 22.5 %collective-permute-start.9 = (bf16[256,512]{1,0:T(8,128)(2,1)S(1)}, bf16[256,512]{1,0:T(8,128)(2,1)S(1)}, u32[]{:S(2)}, u32[]{:S(2)}) collective-permute-start(bf16[256,512]{1,0:T(8,128)(2,1)S(1)} %collective-permute-done.7.refs_8_.refs_7_), channel_id=1, source_target_pairs={{0,4},{6,2},{1,5},{7,3},{4,8},{10,6},{5,9},{11,7},{8,12},{14,10},{... | collective-permute-start | bytes 786440 | tf_op jit(solution)/shard_map/ppermute | solution.py:257
  46.1 10.5 %collective-permute-start.12 = (bf16[272,512]{1,0:T(8,128)(2,1)S(1)}, bf16[272,512]{1,0:T(8,128)(2,1)S(1)}, u32[]{:S(2)}, u32[]{:S(2)}) collective-permute-start(bf16[272,512]{1,0:T(8,128)(2,1)S(1)} %collective-permute-done.5.refs_7_.refs_6_), channel_id=1, source_target_pairs={{0,4},{6,2},{1,5},{7,3},{4,8},{10,6},{5,9},{11,7},{8,12},{14,10},{... | collective-permute-start | bytes 835592 | tf_op jit(solution)/shard_map/ppermute | solution.py:257
  47.6 17.0 %collective-permute-start.15 = (bf16[272,512]{1,0:T(8,128)(2,1)S(1)}, bf16[272,512]{1,0:T(8,128)(2,1)S(1)}, u32[]{:S(2)}, u32[]{:S(2)}) collective-permute-start(bf16[272,512]{1,0:T(8,128)(2,1)S(1)} %collective-permute-done.13.refs_7_.refs_6_), channel_id=1, source_target_pairs={{0,4},{6,2},{1,5},{7,3},{4,8},{10,6},{5,9},{11,7},{8,12},{14,10},{... | collective-permute-start | bytes 835592 | tf_op jit(solution)/shard_map/ppermute | solution.py:257
  53.4 12.7 %collective-permute-start.14 = (bf16[256,512]{1,0:T(8,128)(2,1)S(1)}, bf16[256,512]{1,0:T(8,128)(2,1)S(1)}, u32[]{:S(2)}, u32[]{:S(2)}) collective-permute-start(bf16[256,512]{1,0:T(8,128)(2,1)S(1)} %collective-permute-done.11.refs_8_.refs_7_), channel_id=1, source_target_pairs={{0,4},{6,2},{1,5},{7,3},{4,8},{10,6},{5,9},{11,7},{8,12},{14,10},{... | collective-permute-start | bytes 786440 | tf_op jit(solution)/shard_map/ppermute | solution.py:257
  56.6 13.2 %collective-permute-start.16 = (bf16[272,512]{1,0:T(8,128)(2,1)S(1)}, bf16[272,512]{1,0:T(8,128)(2,1)S(1)}, u32[]{:S(2)}, u32[]{:S(2)}) collective-permute-start(bf16[272,512]{1,0:T(8,128)(2,1)S(1)} %collective-permute-done.12.refs_7_.refs_6_), channel_id=1, source_target_pairs={{0,4},{6,2},{1,5},{7,3},{4,8},{10,6},{5,9},{11,7},{8,12},{14,10},{... | collective-permute-start | bytes 835592 | tf_op jit(solution)/shard_map/ppermute | solution.py:257
  61.2 10.0 %collective-permute-start.17 = (bf16[256,512]{1,0:T(8,128)(2,1)S(1)}, bf16[256,512]{1,0:T(8,128)(2,1)S(1)}, u32[]{:S(2)}, u32[]{:S(2)}) collective-permute-start(bf16[256,512]{1,0:T(8,128)(2,1)S(1)} %collective-permute-done.9.refs_8_.refs_7_), channel_id=1, source_target_pairs={{0,4},{6,2},{1,5},{7,3},{4,8},{10,6},{5,9},{11,7},{8,12},{14,10},{... | collective-permute-start | bytes 786440 | tf_op jit(solution)/shard_map/ppermute | solution.py:257
  66.9 4.4 %collective-permute-start.20 = (bf16[256,512]{1,0:T(8,128)(2,1)S(1)}, bf16[256,512]{1,0:T(8,128)(2,1)S(1)}, u32[]{:S(2)}, u32[]{:S(2)}) collective-permute-start(bf16[256,512]{1,0:T(8,128)(2,1)S(1)} %get-tuple-element.101), channel_id=1, source_target_pairs={{0,2},{2,0},{4,6},{6,4},{8,10},{10,8},{12,14},{14,12},{16,18},{18,... | collective-permute-start | bytes 786440 | tf_op jit(solution)/shard_map/ppermute | solution.py:260
  67.0 4.3 %collective-permute-start.21 = (bf16[256,512]{1,0:T(8,128)(2,1)S(1)}, bf16[256,512]{1,0:T(8,128)(2,1)S(1)}, u32[]{:S(2)}, u32[]{:S(2)}) collective-permute-start(bf16[256,512]{1,0:T(8,128)(2,1)S(1)} %get-tuple-element.110), channel_id=1, source_target_pairs={{0,2},{2,0},{4,6},{6,4},{8,10},{10,8},{12,14},{14,12},{16,18},{18,... | collective-permute-start | bytes 786440 | tf_op jit(solution)/shard_map/ppermute | solution.py:260
  72.1 13.6 %collective-permute-start.22 = (bf16[512,512]{1,0:T(8,128)(2,1)S(1)}, bf16[512,512]{1,0:T(8,128)(2,1)S(1)}, u32[]{:S(2)}, u32[]{:S(2)}) collective-permute-start(bf16[512,512]{1,0:T(8,128)(2,1)S(1)} %window.29), channel_id=1, source_target_pairs={{0,1},{1,0},{2,3},{3,2},{4,5},{5,4},{6,7},{7,6},{8,9},{9,8},{10,11... | collective-permute-start | bytes 1572872 | tf_op jit(solution)/shard_map/ppermute | solution.py:263
  72.2 1.6 %collective-permute-start.18 = (bf16[256,512]{1,0:T(8,128)(2,1)S(1)}, bf16[256,512]{1,0:T(8,128)(2,1)S(1)}, u32[]{:S(2)}, u32[]{:S(2)}) collective-permute-start(bf16[256,512]{1,0:T(8,128)(2,1)S(1)} %get-tuple-element.103), channel_id=1, source_target_pairs={{0,2},{2,0},{4,6},{6,4},{8,10},{10,8},{12,14},{14,12},{16,18},{18,... | collective-permute-start | bytes 786440 | tf_op jit(solution)/shard_map/ppermute | solution.py:260
  72.4 1.8 %collective-permute-start.19 = (bf16[256,512]{1,0:T(8,128)(2,1)S(1)}, bf16[256,512]{1,0:T(8,128)(2,1)S(1)}, u32[]{:S(2)}, u32[]{:S(2)}) collective-permute-start(bf16[256,512]{1,0:T(8,128)(2,1)S(1)} %get-tuple-element.109), channel_id=1, source_target_pairs={{0,2},{2,0},{4,6},{6,4},{8,10},{10,8},{12,14},{14,12},{16,18},{18,... | collective-permute-start | bytes 786440 | tf_op jit(solution)/shard_map/ppermute | solution.py:260

commit v3 on v1

v3 whole, which is shorter than its diff:
```python
import functools
import math

import jax
import jax.numpy as jnp
from jax import lax
from jax.experimental import pallas as pl
from jax.experimental.pallas import tpu as pltpu
from jax.sharding import PartitionSpec as P

STEPS = 8
TEMPER = 0.07
SHIFT = 11.5
SCALE = math.log2(math.e) / TEMPER
OFFSET = SHIFT * math.log2(math.e)
EXTRA = 16
CHUNKS = 1
GROUPS = 2
VMEM = 8 * 2**20
WHOLE = pl.BlockSpec(memory_space=pltpu.VMEM)

PLAN = {
    1: [("core1", ("own", "core"))],
    2: [("own1", ("own", "core"))],
    3: [("core2", ("own", "core"))],
    4: [("core1", ("other", "far")), ("own1", ("other", "far")), ("core2", ("other", "far"))],
    5: [("own2", ("own", "core")), ("own2", ("other", "far")), ("core3", ("core", "far")), ("core3", ("own", "other"))],
    6: [("own3", ("far",)), ("own3", ("core",)), ("own3", ("own", "other"))],
}
ROWS_AT = 3


def hold(value, token):
    return lax.optimization_barrier((value, token))[0]


def call(kernel, shapes, args, name, aliases=None, flops=0, specs=None):
    return pl.pallas_call(
        kernel,
        out_shape=[jax.ShapeDtypeStruct(shape, dtype) for shape, dtype in shapes],
        in_specs=specs or [WHOLE] * len(args),
        out_specs=[WHOLE] * len(shapes),
        input_output_aliases=aliases or {},
        compiler_params=pltpu.CompilerParams(vmem_limit_bytes=VMEM),
        cost_estimate=pl.CostEstimate(flops=flops, bytes_accessed=0, transcendentals=0),
        name=name,
    )(*args)


def split3(value):
    high = value.astype(jnp.bfloat16)
    rest = value - high.astype(jnp.float32)
    mid = rest.astype(jnp.bfloat16)
    low = (rest - mid.astype(jnp.float32)).astype(jnp.bfloat16)
    return [high.astype(jnp.float32), mid.astype(jnp.float32), low.astype(jnp.float32)]


def pack_kernel(place_ref, views_ref, lse_ref, weight_ref, partner_ref, pack_ref):
    rows = views_ref.shape[0]
    pack_ref[:rows, :] = views_ref[...].astype(jnp.bfloat16)
    weight = weight_ref[...]
    strength = weight * jnp.exp(SHIFT - lse_ref[...])
    local = partner_ref[...] & 2047
    place = jnp.full(weight.shape, place_ref[0] * rows, jnp.int32).astype(jnp.float32)
    lines = split3(strength) + split3(weight)
    lines += [(local >> 8).astype(jnp.float32), (local & 255).astype(jnp.float32), place]
    lines += [jnp.zeros_like(weight)] * (EXTRA - len(lines))
    pack_ref[rows:, :] = jnp.concatenate(lines, axis=0).astype(jnp.bfloat16)


def pack_views(place, views, lse, weight, partner):
    rows, width = views.shape
    line = (1, rows)
    return call(
        pack_kernel,
        [((rows + EXTRA, width), jnp.bfloat16)],
        (place, views, lse.reshape(line), weight.reshape(line), partner.reshape(line)),
        "pack",
        specs=[pl.BlockSpec(memory_space=pltpu.SMEM)] + [WHOLE] * 4,
    )[0]


def statistics(first_ref):
    rows = first_ref.shape[0] - EXTRA
    lines = first_ref[rows:, :].astype(jnp.float32)
    strength = lines[0:1] + lines[1:2] + lines[2:3]
    weight = lines[3:4] + lines[4:5] + lines[5:6]
    partner = lines[6:7] * 256.0 + lines[7:8]
    return strength, weight, partner, lines[8:9]


def joined(chunk_refs):
    first = chunk_refs[0][: chunk_refs[0].shape[0] - EXTRA, :]
    rest = [ref[...] for ref in chunk_refs[1:]]
    return jnp.concatenate([first] + rest, axis=0) if rest else first


def spread(line):
    return jnp.broadcast_to(line, (128, line.shape[1])).T


def wide(column, width):
    return jnp.concatenate([column] * (width // 128), axis=1)


def scores_of(rows, cols):
    return lax.dot_general(rows, cols, (((1,), (1,)), ((), ())), preferred_element_type=jnp.float32)


def block_kernel(diagonal, row_ref, own_ref, *refs):
    core_refs, (strength_ref, total_ref) = refs[:CHUNKS], refs[CHUNKS:]
    size = total_ref.shape[0]
    row_strength, row_weight, _, row_place = statistics(row_ref)
    row_strength, row_weight = spread(row_strength), spread(row_weight)
    strength_ref[...] = row_strength
    rows = joined([row_ref])
    row_at = lax.broadcasted_iota(jnp.int32, (size, size), 0)
    total = None
    for col_refs in ([own_ref], core_refs):
        strength, weight, partner, _ = statistics(col_refs[0])
        cols = joined(col_refs)
        raised = jnp.exp2(scores_of(rows, cols) * SCALE - OFFSET)
        value = raised * (wide(row_strength, size) + strength)
        pair = partner == row_at.astype(jnp.float32) + row_place
        value = value - jnp.where(pair, wide(row_weight, size) + weight, 0.0)
        if diagonal and total is None:
            col_at = lax.broadcasted_iota(jnp.int32, (size, size), 1)
            value = jnp.where(row_at == col_at, 0.0, value)
        term = jnp.dot(value.astype(jnp.bfloat16), cols, preferred_element_type=jnp.float32)
        total = term if total is None else total + term
    total_ref[...] = total


def block_terms(diagonal, rows, own, core):
    size, width = own.shape[0] - EXTRA, own.shape[1]
    return call(
        functools.partial(block_kernel, diagonal),
        [((size, 128), jnp.float32), ((size, width), jnp.float32)],
        (rows, own, *core),
        "own_rows" if diagonal else "other_rows",
        flops=32 * size**2 * width,
    )


def spread_kernel(first_ref, out_ref):
    out_ref[...] = spread(statistics(first_ref)[0])


def strengths_of(pack, size):
    return call(spread_kernel, [((size, 128), jnp.float32)], pack[:1], "spread")[0]


def window_kernel(layout, pieces, *refs):
    refs = list(refs)
    parts = []
    for chunks, addends in layout:
        pack, strength = [refs.pop(0) for _ in range(chunks)], refs.pop(0)
        parts.append((pack, strength, [[refs.pop(0) for _ in range(count)] for count in addends]))
    cols_refs = [refs.pop(0) for _ in range(CHUNKS)]
    strength, _, _, _ = statistics(cols_refs[0])
    cols = joined(cols_refs)
    for at, (pack, row_strength, addends) in enumerate(parts):
        size = row_strength.shape[0]
        raised = jnp.exp2(scores_of(joined(pack), cols) * SCALE - OFFSET)
        value = (raised * (wide(row_strength[...], size) + strength)).astype(jnp.bfloat16)
        total = jnp.dot(value, cols, preferred_element_type=jnp.float32)
        for addend in addends:
            whole = [ref[...].astype(jnp.float32) for ref in addend]
            total = total + (jnp.concatenate(whole, axis=0) if len(whole) > 1 else whole[0])
        for i, out_ref in enumerate(refs[at * pieces : (at + 1) * pieces]):
            rows = out_ref.shape[0]
            out_ref[...] = total[i * rows : (i + 1) * rows, :].astype(out_ref.dtype)


def window_terms(row_packs, cols, dtype=jnp.float32, pieces=1, weight=0):
    size, width = row_packs[0][1].shape[0], cols[0].shape[1]
    args, layout, aliases = [], [], {}
    for at, (pack, strength, addends) in enumerate(row_packs):
        layout.append((len(pack), tuple(len(addend) for addend in addends)))
        args += [*pack, strength]
        if addends and len(addends[0]) == pieces and dtype == addends[0][0].dtype:
            aliases.update({len(args) + i: at * pieces + i for i in range(pieces)})
        args += sum(addends, [])
    return call(
        functools.partial(window_kernel, tuple(layout), pieces),
        [((size // pieces, width), dtype)] * (pieces * len(row_packs)),
        (*args, *cols),
        "window",
        aliases=aliases,
        flops=weight * len(row_packs) * size**2 * width,
    )


def finish_kernel(here_ref, *refs):
    pieces, (away_ref, out_ref) = refs[:-2], refs[-2:]
    rows = here_ref.shape[0] // len(pieces)
    for i, piece_ref in enumerate(pieces):
        part = slice(i * rows, (i + 1) * rows)
        total = here_ref[part, :] + piece_ref[...].astype(jnp.float32) + away_ref[part, :].astype(jnp.float32)
        out_ref[part, :] = total * (1.0 / TEMPER)


def per_device(views, log_sum_exp, loss_weight, partner):
    dp_place, sub_place = lax.axis_index("dp"), lax.axis_index("sub")
    loop_size = lax.axis_size("dp")
    chips = loop_size // 2
    size = views.shape[0]

    onward = []
    for place in range(chips):
        turn = 1 if (place + 1) % (chips // GROUPS) == 0 else 0
        later = (place + 1) % chips
        for sub in range(2):
            onward.append(((2 * place) * 2 + sub, (2 * later) * 2 + (sub ^ turn)))
            onward.append(((2 * later + 1) * 2 + (sub ^ turn), (2 * place + 1) * 2 + sub))
    cores = [(place, place ^ 1) for place in range(loop_size)]

    def chip_next(value):
        return lax.ppermute(value, ("dp", "sub"), onward)

    def core_swap(value):
        return lax.ppermute(value, "dp", cores)

    def sub_swap(value):
        return lax.ppermute(value, "sub", [(0, 1), (1, 0)])

    place = ((dp_place % 2) * 2 + sub_place).astype(jnp.int32).reshape(1)
    whole = pack_views(place, views, log_sum_exp, loss_weight, partner)
    core = core_swap(whole)
    coming = {"core": chip_next(core), "own": chip_next(hold(whole, core))}
    other = sub_swap(whole)

    reach = STEPS // 2
    legs = [(kind, step) for step in range(1, reach) for kind in ("core", "own")] + [("core", reach)]
    packs = {"own": [whole], "core": [core]}
    strengths, totals, columns = {}, {"core": [], "far": []}, {}
    strengths["own"], token = block_terms(True, whole, whole, [core])
    totals["own"] = [[token]]
    strengths["core"] = strengths_of([core], size)
    for arrivals, (kind, step) in enumerate(legs, 1):
        pack = hold(coming[kind], token)
        arrived = columns[f"{kind}{step}"] = [pack]
        if step < reach - (kind == "own"):
            coming[kind] = chip_next(pack)
        for name, rows in PLAN.get(arrivals, ()):
            group = [
                (packs[r], strengths[r], [[hold(hold(a, pack), token) for a in addend] for addend in totals[r]])
                for r in rows
            ]
            last = name == f"own{reach - 1}" and rows[0] in ("core", "far")
            if last:
                sums = window_terms(group, columns[name], jnp.bfloat16)
                totals[rows[0]] = [sums]
            else:
                sums = window_terms(group, columns[name], weight=16 if arrivals < 3 else 0)
                totals.update({r: [[value]] for r, value in zip(rows, sums, strict=True)})
            token = sums[0]
        if arrivals == ROWS_AT:
            other = hold(hold(other, pack), token)
            strengths["other"], token = block_terms(False, other, whole, [core])
            far = core_swap(other)
            packs["other"], packs["far"] = [other], [far]
            totals["other"] = [[token]]
            strengths["far"] = strengths_of([far], size)
    back = {r: [core_swap(piece) for piece in totals[r][0]] for r in ("far", "core")}
    (away,) = window_terms([(packs["other"], strengths["other"], totals["other"] + [back["far"]])], arrived, jnp.bfloat16)
    away = sub_swap(away)
    (here,) = window_terms([(packs["own"], strengths["own"], totals["own"])], arrived)
    return call(finish_kernel, [(here.shape, jnp.float32)], (here, *back["core"], away), "finish")[0]


def solution(mesh):
    in_specs = (P(("dp", "sub"), None), P(("dp", "sub")), P(("dp", "sub")), P(("dp", "sub")))
    out_specs = P(("dp", "sub"), None)
    return jax.shard_map(per_device, mesh=mesh, in_specs=in_specs, out_specs=out_specs, check_vma=False)
```

time: 82.6 us -> 78.9 us (0.955)
  waiting for transfers between devices: 46.4 us -> 39.4 us
  starting transfers between devices: 12.4 us -> 15.3 us
  other arithmetic: 1.15 us -> 0 us
  local copies, waits for them, and re-layouts: 1.05 us -> 1.93 us
    ppermute x7, waiting for transfers between devices: 40 us -> 28.2 us  [chip_next(): return lax.ppermute(value, ('dp', 'sub'), onward)]
    ppermute x7 -> x4, starting transfers between devices: 1.27 us -> 5.11 us  [core_swap(): return lax.ppermute(value, 'dp', cores)]
    ppermute x2, waiting for transfers between devices: 6.41 us -> 9.25 us  [sub_swap(): return lax.ppermute(value, 'sub', [(0, 1), (1, 0)])]
    ppermute x7 -> x4, waiting for transfers between devices: 0.02 us -> 1.93 us  [core_swap(): return lax.ppermute(value, 'dp', cores)]
    ppermute x2, starting transfers between devices: 7.26 us -> 6.05 us  [sub_swap(): return lax.ppermute(value, 'sub', [(0, 1), (1, 0)])]
    mul x1 -> x0, other arithmetic: 1.15 us -> none  [per_device(): return (here + away.astype(jnp.float32)) * (1.0 / TEMPER)]
    unnamed x4 -> x8, local copies, waits for them, and re-layouts: 1.05 us -> 1.93 us
    pallas_call x11 -> x21, Pallas kernels: 21.3 us -> 22 us  [call(): pl.pallas_call(kernel, out_shape=[jax.ShapeDtypeStruct(shape, dtype) for...]
  transfers between devices with their start and end apart: 16 -> 13, of which waited for: 8 -> 8; matrix products, arithmetic and copies ran while one was open for 0% -> 0% of each run, Pallas kernels for 22% -> 26%
where the time goes in v3:
time: 78.9 us; the launch traced here: 78.8 us
  waiting for transfers between devices  39.4 us (50%)
  Pallas kernels  22 us (28%)
  starting transfers between devices  15.3 us (19%)
  local copies, waits for them, and re-layouts  1.93 us (2%)
    ppermute x7, waiting for transfers between devices, chip_next(): return lax.ppermute(value, ('dp', 'sub'), onward)  28.2 us
    pallas_call x21, Pallas kernels, call(): pl.pallas_call(kernel, out_shape=[jax.ShapeDtypeStruct(shape, dtype) for...  22 us
    ppermute x2, waiting for transfers between devices, sub_swap(): return lax.ppermute(value, 'sub', [(0, 1), (1, 0)])  9.25 us
    ppermute x2, starting transfers between devices, sub_swap(): return lax.ppermute(value, 'sub', [(0, 1), (1, 0)])  6.05 us
    ppermute x4, starting transfers between devices, core_swap(): return lax.ppermute(value, 'dp', cores)  5.11 us
    ppermute x7, starting transfers between devices, chip_next(): return lax.ppermute(value, ('dp', 'sub'), onward)  4.11 us
    unnamed x8, local copies, waits for them, and re-layouts  1.93 us
    ppermute x4, waiting for transfers between devices, core_swap(): return lax.ppermute(value, 'dp', cores)  1.93 us
  transfers between devices with their start and end apart: 13, of which 8 were waited for; matrix products, arithmetic and copies ran while one was open for 0% of the time, Pallas kernels for 26%

profile of v3, /device:TPU:2, one launch (start us, length us, event | category | flops | bytes accessed | tf_op | source)
XLA Modules:
  0.0 78.8 jit_solution(15665640676212280505)
XLA Ops:
  0.7 1.2 %copy-done = f32[512,512]{1,0:T(8,128)S(1)} copy-done((f32[512,512]{1,0:T(8,128)S(1)}, f32[512,512]{1,0:T(8,128)}, u32[]{:S(2)}) %copy-start) | copy-done | bytes 1048600
  2.1 1.9 %collective-permute-done.refs_0_.first_ref.refs_3_ = bf16[528,512]{1,0:T(8,128)(2,1)S(1)} collective-permute-done((bf16[528,512]{1,0:T(8,128)(2,1)S(1)}, bf16[528,512]{1,0:T(8,128)(2,1)S(1)}, u32[]{:S(2)}, u32[]{:S(2)}) %collective-permute-start) | collective-permute-done | bytes 540704 | tf_op jit(solution)/shard_map/ppermute | solution.py:222
  4.1 1.9 %collective-permute-start.1 = (bf16[528,512]{1,0:T(8,128)(2,1)S(1)}, bf16[528,512]{1,0:T(8,128)(2,1)S(1)}, u32[]{:S(2)}, u32[]{:S(2)}) collective-permute-start(bf16[528,512]{1,0:T(8,128)(2,1)S(1)} %collective-permute-done.refs_0_.first_ref.refs_3_), channel_id=1, source_target_pairs={{0,4},{6,2},{1,5},{7,3},{4,8},{10,6},{5,9},{11,7},{8,12},{14,10},{... | collective-permute-start | bytes 1622024 | tf_op jit(solution)/shard_map/ppermute | solution.py:219
  6.5 1.9 %collective-permute-start.2 = (bf16[528,512]{1,0:T(8,128)(2,1)S(1)}, bf16[528,512]{1,0:T(8,128)(2,1)S(1)}, u32[]{:S(2)}, u32[]{:S(2)}) collective-permute-start(bf16[528,512]{1,0:T(8,128)(2,1)S(1)} %pack.1.row_ref.own_ref.refs_0_), channel_id=1, source_target_pairs={{0,4},{6,2},{1,5},{7,3},{4,8},{10,6},{5,9},{11,7},{8,12},{14,10},{... | collective-permute-start | bytes 1622024 | tf_op jit(solution)/shard_map/ppermute | solution.py:219
  8.4 1.5 %own_rows.1 = (f32[512,128]{1,0:T(8,128)S(1)}, f32[512,512]{1,0:T(8,128)S(1)}) custom-call(bf16[528,512]{1,0:T(8,128)(2,1)S(1)} %pack.1.row_ref.own_ref.refs_0_, bf16[528,512]{1,0:T(8,128)(2,1)S(1)} %pack.1.row_ref.own_ref.refs_0_, bf16[528,512]{1,0:T(8,128)(2,1)S(1)} %collective-permute-done.refs_0_.first_ref.refs_3_), custom_call_target="tpu_custom_call" | custom-call | flops 4294967296 | tf_op jit(solution)/shard_map/own_rows/pallas_call | solution.py:38
  10.1 10.5 %collective-permute-done.1.refs_5_ = bf16[528,512]{1,0:T(8,128)(2,1)S(1)} collective-permute-done((bf16[528,512]{1,0:T(8,128)(2,1)S(1)}, bf16[528,512]{1,0:T(8,128)(2,1)S(1)}, u32[]{:S(2)}, u32[]{:S(2)}) %collective-permute-start.1) | collective-permute-done | bytes 540704 | tf_op jit(solution)/shard_map/ppermute | solution.py:219
  20.6 1.3 %window.15 = (f32[512,512]{1,0:T(8,128)S(1)}, f32[512,512]{1,0:T(8,128)S(1)}) custom-call(bf16[528,512]{1,0:T(8,128)(2,1)S(1)} %pack.1.row_ref.own_ref.refs_0_, f32[512,128]{1,0:T(8,128)S(1)} %get-tuple-element.85.refs_1_, f32[512,512]{1,0:T(8,128)S(1)} %get-tuple-element.89.refs_2_, ...), custom_call_target="tpu_custom_call", output_to_operand_aliasing={{0}: (2, {})} | custom-call | flops 4294967296 | tf_op jit(solution)/shard_map/window/pallas_call | solution.py:38
  21.9 4.5 %collective-permute-done.2.refs_6_ = bf16[528,512]{1,0:T(8,128)(2,1)S(1)} collective-permute-done((bf16[528,512]{1,0:T(8,128)(2,1)S(1)}, bf16[528,512]{1,0:T(8,128)(2,1)S(1)}, u32[]{:S(2)}, u32[]{:S(2)}) %collective-permute-start.2) | collective-permute-done | bytes 540704 | tf_op jit(solution)/shard_map/ppermute | solution.py:219
  26.4 1.3 %window.16 = (f32[512,512]{1,0:T(8,128)S(1)}, f32[512,512]{1,0:T(8,128)S(1)}) custom-call(bf16[528,512]{1,0:T(8,128)(2,1)S(1)} %pack.1.row_ref.own_ref.refs_0_, f32[512,128]{1,0:T(8,128)S(1)} %get-tuple-element.85.refs_1_, f32[512,512]{1,0:T(8,128)S(1)} %get-tuple-element.94.refs_2_, ...), custom_call_target="tpu_custom_call", output_to_operand_aliasing={{0}: (2, {}), {1}: (5, {})} | custom-call | flops 4294967296 | tf_op jit(solution)/shard_map/window/pallas_call | solution.py:38
  27.7 6.5 %collective-permute-done.3.refs_6_ = bf16[528,512]{1,0:T(8,128)(2,1)S(1)} collective-permute-done((bf16[528,512]{1,0:T(8,128)(2,1)S(1)}, bf16[528,512]{1,0:T(8,128)(2,1)S(1)}, u32[]{:S(2)}, u32[]{:S(2)}) %collective-permute-start.3) | collective-permute-done | bytes 540704 | tf_op jit(solution)/shard_map/ppermute | solution.py:219
  34.2 1.3 %window.17 = (f32[512,512]{1,0:T(8,128)S(1)}, f32[512,512]{1,0:T(8,128)S(1)}) custom-call(bf16[528,512]{1,0:T(8,128)(2,1)S(1)} %pack.1.row_ref.own_ref.refs_0_, f32[512,128]{1,0:T(8,128)S(1)} %get-tuple-element.85.refs_1_, f32[512,512]{1,0:T(8,128)S(1)} %get-tuple-element.101.refs_2_, ...), custom_call_target="tpu_custom_call", output_to_operand_aliasing={{0}: (2, {}), {1}: (5, {})} | custom-call | tf_op jit(solution)/shard_map/window/pallas_call | solution.py:38
  35.5 3.9 %collective-permute-start.7 = (bf16[528,512]{1,0:T(8,128)(2,1)S(1)}, bf16[528,512]{1,0:T(8,128)(2,1)S(1)}, u32[]{:S(2)}, u32[]{:S(2)}) collective-permute-start(bf16[528,512]{1,0:T(8,128)(2,1)S(1)} %collective-permute-done.5.row_ref.refs_0_.refs_3_), channel_id=1, source_target_pairs={{0,2},{2,0},{4,6},{6,4},{8,10},{10,8},{12,14},{14,12},{16,18},{18,... | collective-permute-start | bytes 1622024 | tf_op jit(solution)/shard_map/ppermute | solution.py:222
  39.4 1.5 %other_rows.1 = (f32[512,128]{1,0:T(8,128)S(1)}, f32[512,512]{1,0:T(8,128)S(1)}) custom-call(bf16[528,512]{1,0:T(8,128)(2,1)S(1)} %collective-permute-done.5.row_ref.refs_0_.refs_3_, bf16[528,512]{1,0:T(8,128)(2,1)S(1)} %pack.1.row_ref.own_ref.refs_0_, bf16[528,512]{1,0:T(8,128)(2,1)S(1)} %collective-permute-done.refs_0_.first_ref.refs_3_), custom_call_target="tpu_custom_call" | custom-call | flops 4294967296 | tf_op jit(solution)/shard_map/other_rows/pallas_call | solution.py:38
  41.4 1.3 %window.18 = (f32[512,512]{1,0:T(8,128)S(1)}, f32[512,512]{1,0:T(8,128)S(1)}) custom-call(bf16[528,512]{1,0:T(8,128)(2,1)S(1)} %collective-permute-done.5.row_ref.refs_0_.refs_3_, f32[512,128]{1,0:T(8,128)S(1)} %get-tuple-element.108.refs_1_.refs_4_, f32[512,512]{1,0:T(8,128)S(1)} %get-tuple-element.112.refs_2_, ...), custom_call_target="tpu_custom_call", output_to_operand_aliasing={{0}: (2, {})} | custom-call | tf_op jit(solution)/shard_map/window/pallas_call | solution.py:38
  42.7 1.3 %window.19 = (f32[512,512]{1,0:T(8,128)S(1)}, f32[512,512]{1,0:T(8,128)S(1)}) custom-call(bf16[528,512]{1,0:T(8,128)(2,1)S(1)} %collective-permute-done.5.row_ref.refs_0_.refs_3_, f32[512,128]{1,0:T(8,128)S(1)} %get-tuple-element.108.refs_1_.refs_4_, f32[512,512]{1,0:T(8,128)S(1)} %get-tuple-element.115.refs_2_, ...), custom_call_target="tpu_custom_call", output_to_operand_aliasing={{0}: (2, {}), {1}: (5, {})} | custom-call | tf_op jit(solution)/shard_map/window/pallas_call | solution.py:38
  44.0 1.3 %window.20 = (f32[512,512]{1,0:T(8,128)S(1)}, f32[512,512]{1,0:T(8,128)S(1)}) custom-call(bf16[528,512]{1,0:T(8,128)(2,1)S(1)} %collective-permute-done.5.row_ref.refs_0_.refs_3_, f32[512,128]{1,0:T(8,128)S(1)} %get-tuple-element.108.refs_1_.refs_4_, f32[512,512]{1,0:T(8,128)S(1)} %get-tuple-element.121.refs_2_, ...), custom_call_target="tpu_custom_call", output_to_operand_aliasing={{0}: (2, {}), {1}: (5, {})} | custom-call | tf_op jit(solution)/shard_map/window/pallas_call | solution.py:38
  45.4 2.4 %collective-permute-done.4.refs_6_ = bf16[528,512]{1,0:T(8,128)(2,1)S(1)} collective-permute-done((bf16[528,512]{1,0:T(8,128)(2,1)S(1)}, bf16[528,512]{1,0:T(8,128)(2,1)S(1)}, u32[]{:S(2)}, u32[]{:S(2)}) %collective-permute-start.4) | collective-permute-done | bytes 540704 | tf_op jit(solution)/shard_map/ppermute | solution.py:219
  47.8 1.3 %window.21 = (f32[512,512]{1,0:T(8,128)S(1)}, f32[512,512]{1,0:T(8,128)S(1)}) custom-call(bf16[528,512]{1,0:T(8,128)(2,1)S(1)} %pack.1.row_ref.own_ref.refs_0_, f32[512,128]{1,0:T(8,128)S(1)} %get-tuple-element.85.refs_1_, f32[512,512]{1,0:T(8,128)S(1)} %get-tuple-element.128.refs_2_, ...), custom_call_target="tpu_custom_call", output_to_operand_aliasing={{0}: (2, {}), {1}: (5, {})} | custom-call | tf_op jit(solution)/shard_map/window/pallas_call | solution.py:38
  49.1 1.3 %window.22 = (f32[512,512]{1,0:T(8,128)S(1)}, f32[512,512]{1,0:T(8,128)S(1)}) custom-call(bf16[528,512]{1,0:T(8,128)(2,1)S(1)} %collective-permute-done.5.row_ref.refs_0_.refs_3_, f32[512,128]{1,0:T(8,128)S(1)} %get-tuple-element.108.refs_1_.refs_4_, f32[512,512]{1,0:T(8,128)S(1)} %get-tuple-element.137.refs_2_, ...), custom_call_target="tpu_custom_call", output_to_operand_aliasing={{0}: (2, {}), {1}: (5, {})} | custom-call | tf_op jit(solution)/shard_map/window/pallas_call | solution.py:38
  50.4 1.3 %window.23 = (f32[512,512]{1,0:T(8,128)S(1)}, f32[512,512]{1,0:T(8,128)S(1)}) custom-call(bf16[528,512]{1,0:T(8,128)(2,1)S(1)} %collective-permute-done.refs_0_.first_ref.refs_3_, f32[512,128]{1,0:T(8,128)S(1)} %spread.2.refs_4_.refs_1_, f32[512,512]{1,0:T(8,128)S(1)} %get-tuple-element.142.refs_2_, ...), custom_call_target="tpu_custom_call", output_to_operand_aliasing={{0}: (2, {}), {1}: (5, {})} | custom-call | tf_op jit(solution)/shard_map/window/pallas_call | solution.py:38
  51.8 1.3 %window.24 = (f32[512,512]{1,0:T(8,128)S(1)}, f32[512,512]{1,0:T(8,128)S(1)}) custom-call(bf16[528,512]{1,0:T(8,128)(2,1)S(1)} %pack.1.row_ref.own_ref.refs_0_, f32[512,128]{1,0:T(8,128)S(1)} %get-tuple-element.85.refs_1_, f32[512,512]{1,0:T(8,128)S(1)} %get-tuple-element.147.refs_2_, ...), custom_call_target="tpu_custom_call", output_to_operand_aliasing={{0}: (2, {}), {1}: (5, {})} | custom-call | tf_op jit(solution)/shard_map/window/pallas_call | solution.py:38
  53.1 1.7 %collective-permute-done.8.refs_3_.refs_6_ = bf16[528,512]{1,0:T(8,128)(2,1)S(1)} collective-permute-done((bf16[528,512]{1,0:T(8,128)(2,1)S(1)}, bf16[528,512]{1,0:T(8,128)(2,1)S(1)}, u32[]{:S(2)}, u32[]{:S(2)}) %collective-permute-start.8) | collective-permute-done | bytes 540704 | tf_op jit(solution)/shard_map/ppermute | solution.py:219
  54.8 0.7 window.25
  55.6 1.0 %collective-permute-start.11 = (bf16[512,512]{1,0:T(8,128)(2,1)S(1)}, bf16[512,512]{1,0:T(8,128)(2,1)S(1)}, u32[]{:S(2)}, u32[]{:S(2)}) collective-permute-start(bf16[512,512]{1,0:T(8,128)(2,1)S(1)} %window.25), channel_id=1, source_target_pairs={{0,2},{2,0},{4,6},{6,4},{8,10},{10,8},{12,14},{14,12},{16,18},{18,... | collective-permute-start | bytes 1572872 | tf_op jit(solution)/shard_map/ppermute | solution.py:222
  56.6 0.7 window.26
  57.4 1.3 %window.27 = (f32[512,512]{1,0:T(8,128)S(1)}, f32[512,512]{1,0:T(8,128)S(1)}) custom-call(bf16[528,512]{1,0:T(8,128)(2,1)S(1)} %pack.1.row_ref.own_ref.refs_0_, f32[512,128]{1,0:T(8,128)S(1)} %get-tuple-element.85.refs_1_, f32[512,512]{1,0:T(8,128)S(1)} %get-tuple-element.158.refs_2_, ...), custom_call_target="tpu_custom_call", output_to_operand_aliasing={{0}: (2, {}), {1}: (5, {})} | custom-call | tf_op jit(solution)/shard_map/window/pallas_call | solution.py:38
  58.8 2.6 %collective-permute-done.9.refs_3_.refs_4_ = bf16[528,512]{1,0:T(8,128)(2,1)S(1)} collective-permute-done((bf16[528,512]{1,0:T(8,128)(2,1)S(1)}, bf16[528,512]{1,0:T(8,128)(2,1)S(1)}, u32[]{:S(2)}, u32[]{:S(2)}) %collective-permute-start.9) | collective-permute-done | bytes 540704 | tf_op jit(solution)/shard_map/ppermute | solution.py:219
  61.4 0.7 window.29
  62.1 5.5 %collective-permute-start.12 = (bf16[512,512]{1,0:T(8,128)(2,1)S(1)}, bf16[512,512]{1,0:T(8,128)(2,1)S(1)}, u32[]{:S(2)}, u32[]{:S(2)}) collective-permute-start(bf16[512,512]{1,0:T(8,128)(2,1)S(1)} %window.29), channel_id=1, source_target_pairs={{0,1},{1,0},{2,3},{3,2},{4,5},{5,4},{6,7},{7,6},{8,9},{9,8},{10,11... | collective-permute-start | bytes 1572872 | tf_op jit(solution)/shard_map/ppermute | solution.py:225
  67.6 0.7 window.28.here_ref
  68.4 9.2 %collective-permute-done.12.refs_1_ = bf16[512,512]{1,0:T(8,128)(2,1)S(1)} collective-permute-done((bf16[512,512]{1,0:T(8,128)(2,1)S(1)}, bf16[512,512]{1,0:T(8,128)(2,1)S(1)}, u32[]{:S(2)}, u32[]{:S(2)}) %collective-permute-start.12) | collective-permute-done | bytes 524320 | tf_op jit(solution)/shard_map/ppermute | solution.py:225
  77.6 1.1 %finish.1 = f32[512,512]{1,0:T(8,128)} custom-call(f32[512,512]{1,0:T(8,128)S(1)} %window.28.here_ref, bf16[512,512]{1,0:T(8,128)(2,1)S(1)} %collective-permute-done.10.refs_0_, bf16[512,512]{1,0:T(8,128)(2,1)S(1)} %collective-permute-done.12.refs_1_), custom_call_target="tpu_custom_call" | custom-call | tf_op jit(solution)/shard_map/finish/pallas_call | solution.py:38
  (23 shorter events, 2.1 us)
Async XLA Ops:
  0.0 0.7 copy-start.3
  0.0 0.7 copy-start.2
  0.0 0.7 copy-start.1
  0.7 1.2 %copy-start = (f32[512,512]{1,0:T(8,128)S(1)}, f32[512,512]{1,0:T(8,128)}, u32[]{:S(2)}) copy-start(f32[512,512]{1,0:T(8,128)} %views_ref.1) | copy-start | bytes 3145732
  2.0 2.0 %collective-permute-start = (bf16[528,512]{1,0:T(8,128)(2,1)S(1)}, bf16[528,512]{1,0:T(8,128)(2,1)S(1)}, u32[]{:S(2)}, u32[]{:S(2)}) collective-permute-start(bf16[528,512]{1,0:T(8,128)(2,1)S(1)} %pack.1.row_ref.own_ref.refs_0_), channel_id=1, source_target_pairs={{0,2},{2,0},{4,6},{6,4},{8,10},{10,8},{12,14},{14,12},{16,18},{18,... | collective-permute-start | bytes 1622024 | tf_op jit(solution)/shard_map/ppermute | solution.py:222
  4.1 16.6 %collective-permute-start.1 = (bf16[528,512]{1,0:T(8,128)(2,1)S(1)}, bf16[528,512]{1,0:T(8,128)(2,1)S(1)}, u32[]{:S(2)}, u32[]{:S(2)}) collective-permute-start(bf16[528,512]{1,0:T(8,128)(2,1)S(1)} %collective-permute-done.refs_0_.first_ref.refs_3_), channel_id=1, source_target_pairs={{0,4},{6,2},{1,5},{7,3},{4,8},{10,6},{5,9},{11,7},{8,12},{14,10},{... | collective-permute-start | bytes 1622024 | tf_op jit(solution)/shard_map/ppermute | solution.py:219
  6.0 28.2 %collective-permute-start.5 = (bf16[528,512]{1,0:T(8,128)(2,1)S(1)}, bf16[528,512]{1,0:T(8,128)(2,1)S(1)}, u32[]{:S(2)}, u32[]{:S(2)}) collective-permute-start(bf16[528,512]{1,0:T(8,128)(2,1)S(1)} %pack.1.row_ref.own_ref.refs_0_), channel_id=1, source_target_pairs={{0,1},{1,0},{2,3},{3,2},{4,5},{5,4},{6,7},{7,6},{8,9},{9,8},{10,11... | collective-permute-start | bytes 1622024 | tf_op jit(solution)/shard_map/ppermute | solution.py:225
  6.5 19.9 %collective-permute-start.2 = (bf16[528,512]{1,0:T(8,128)(2,1)S(1)}, bf16[528,512]{1,0:T(8,128)(2,1)S(1)}, u32[]{:S(2)}, u32[]{:S(2)}) collective-permute-start(bf16[528,512]{1,0:T(8,128)(2,1)S(1)} %pack.1.row_ref.own_ref.refs_0_), channel_id=1, source_target_pairs={{0,4},{6,2},{1,5},{7,3},{4,8},{10,6},{5,9},{11,7},{8,12},{14,10},{... | collective-permute-start | bytes 1622024 | tf_op jit(solution)/shard_map/ppermute | solution.py:219
  20.6 13.6 %collective-permute-start.3 = (bf16[528,512]{1,0:T(8,128)(2,1)S(1)}, bf16[528,512]{1,0:T(8,128)(2,1)S(1)}, u32[]{:S(2)}, u32[]{:S(2)}) collective-permute-start(bf16[528,512]{1,0:T(8,128)(2,1)S(1)} %collective-permute-done.1.refs_5_), channel_id=1, source_target_pairs={{0,4},{6,2},{1,5},{7,3},{4,8},{10,6},{5,9},{11,7},{8,12},{14,10},{... | collective-permute-start | bytes 1622024 | tf_op jit(solution)/shard_map/ppermute | solution.py:219
  26.4 14.6 %collective-permute-start.6 = (bf16[528,512]{1,0:T(8,128)(2,1)S(1)}, bf16[528,512]{1,0:T(8,128)(2,1)S(1)}, u32[]{:S(2)}, u32[]{:S(2)}) collective-permute-start(bf16[528,512]{1,0:T(8,128)(2,1)S(1)} %collective-permute-done.2.refs_6_), channel_id=1, source_target_pairs={{0,4},{6,2},{1,5},{7,3},{4,8},{10,6},{5,9},{11,7},{8,12},{14,10},{... | collective-permute-start | bytes 1622024 | tf_op jit(solution)/shard_map/ppermute | solution.py:219
  34.2 13.6 %collective-permute-start.4 = (bf16[528,512]{1,0:T(8,128)(2,1)S(1)}, bf16[528,512]{1,0:T(8,128)(2,1)S(1)}, u32[]{:S(2)}, u32[]{:S(2)}) collective-permute-start(bf16[528,512]{1,0:T(8,128)(2,1)S(1)} %collective-permute-done.3.refs_6_), channel_id=1, source_target_pairs={{0,4},{6,2},{1,5},{7,3},{4,8},{10,6},{5,9},{11,7},{8,12},{14,10},{... | collective-permute-start | bytes 1622024 | tf_op jit(solution)/shard_map/ppermute | solution.py:219
  35.5 5.7 %collective-permute-start.7 = (bf16[528,512]{1,0:T(8,128)(2,1)S(1)}, bf16[528,512]{1,0:T(8,128)(2,1)S(1)}, u32[]{:S(2)}, u32[]{:S(2)}) collective-permute-start(bf16[528,512]{1,0:T(8,128)(2,1)S(1)} %collective-permute-done.5.row_ref.refs_0_.refs_3_), channel_id=1, source_target_pairs={{0,2},{2,0},{4,6},{6,4},{8,10},{10,8},{12,14},{14,12},{16,18},{18,... | collective-permute-start | bytes 1622024 | tf_op jit(solution)/shard_map/ppermute | solution.py:222
  41.0 13.8 %collective-permute-start.8 = (bf16[528,512]{1,0:T(8,128)(2,1)S(1)}, bf16[528,512]{1,0:T(8,128)(2,1)S(1)}, u32[]{:S(2)}, u32[]{:S(2)}) collective-permute-start(bf16[528,512]{1,0:T(8,128)(2,1)S(1)} %collective-permute-done.6.refs_6_), channel_id=1, source_target_pairs={{0,4},{6,2},{1,5},{7,3},{4,8},{10,6},{5,9},{11,7},{8,12},{14,10},{... | collective-permute-start | bytes 1622024 | tf_op jit(solution)/shard_map/ppermute | solution.py:219
  47.8 13.6 %collective-permute-start.9 = (bf16[528,512]{1,0:T(8,128)(2,1)S(1)}, bf16[528,512]{1,0:T(8,128)(2,1)S(1)}, u32[]{:S(2)}, u32[]{:S(2)}) collective-permute-start(bf16[528,512]{1,0:T(8,128)(2,1)S(1)} %collective-permute-done.4.refs_6_), channel_id=1, source_target_pairs={{0,4},{6,2},{1,5},{7,3},{4,8},{10,6},{5,9},{11,7},{8,12},{14,10},{... | collective-permute-start | bytes 1622024 | tf_op jit(solution)/shard_map/ppermute | solution.py:219
  55.6 5.8 %collective-permute-start.11 = (bf16[512,512]{1,0:T(8,128)(2,1)S(1)}, bf16[512,512]{1,0:T(8,128)(2,1)S(1)}, u32[]{:S(2)}, u32[]{:S(2)}) collective-permute-start(bf16[512,512]{1,0:T(8,128)(2,1)S(1)} %window.25), channel_id=1, source_target_pairs={{0,2},{2,0},{4,6},{6,4},{8,10},{10,8},{12,14},{14,12},{16,18},{18,... | collective-permute-start | bytes 1572872 | tf_op jit(solution)/shard_map/ppermute | solution.py:222
  57.3 11.0 %collective-permute-start.10 = (bf16[512,512]{1,0:T(8,128)(2,1)S(1)}, bf16[512,512]{1,0:T(8,128)(2,1)S(1)}, u32[]{:S(2)}, u32[]{:S(2)}) collective-permute-start(bf16[512,512]{1,0:T(8,128)(2,1)S(1)} %window.26), channel_id=1, source_target_pairs={{0,2},{2,0},{4,6},{6,4},{8,10},{10,8},{12,14},{14,12},{16,18},{18,... | collective-permute-start | bytes 1572872 | tf_op jit(solution)/shard_map/ppermute | solution.py:222
  62.1 15.5 %collective-permute-start.12 = (bf16[512,512]{1,0:T(8,128)(2,1)S(1)}, bf16[512,512]{1,0:T(8,128)(2,1)S(1)}, u32[]{:S(2)}, u32[]{:S(2)}) collective-permute-start(bf16[512,512]{1,0:T(8,128)(2,1)S(1)} %window.29), channel_id=1, source_target_pairs={{0,1},{1,0},{2,3},{3,2},{4,5},{5,4},{6,7},{7,6},{8,9},{9,8},{10,11... | collective-permute-start | bytes 1572872 | tf_op jit(solution)/shard_map/ppermute | solution.py:225

commit v4 on v3

--- a/solution.py
+++ b/solution.py
@@ -14,20 +14,21 @@
 SCALE = math.log2(math.e) / TEMPER
 OFFSET = SHIFT * math.log2(math.e)
 EXTRA = 16
-CHUNKS = 1
+CHUNKS = 2
 GROUPS = 2
 VMEM = 8 * 2**20
 WHOLE = pl.BlockSpec(memory_space=pltpu.VMEM)
 
 PLAN = {
-    1: [("core1", ("own", "core"))],
-    2: [("own1", ("own", "core"))],
-    3: [("core2", ("own", "core"))],
-    4: [("core1", ("other", "far")), ("own1", ("other", "far")), ("core2", ("other", "far"))],
-    5: [("own2", ("own", "core")), ("own2", ("other", "far")), ("core3", ("core", "far")), ("core3", ("own", "other"))],
-    6: [("own3", ("far",)), ("own3", ("core",)), ("own3", ("own", "other"))],
+    2: [("core1", ("own", "core"))],
+    3: [("own1", ("own", "core"))],
+    6: [("core1", ("other", "far"))],
+    7: [("own1", ("other", "far"))],
+    8: [("core2", ("other", "far")), ("own2", ("other", "far")), ("core3", ("other", "far"))],
+    9: [("own3", ("far",)), ("own3", ("other",))],
 }
-ROWS_AT = 3
+BESIDE = [(name, ("own", "core")) for name in ("core2", "own2", "core3")] + [("own3", ("core",)), ("own3", ("own",))]
+ROWS_AT = 5
 
 
 def hold(value, token):
@@ -55,29 +56,36 @@
     return [high.astype(jnp.float32), mid.astype(jnp.float32), low.astype(jnp.float32)]
 
 
-def pack_kernel(place_ref, views_ref, lse_ref, weight_ref, partner_ref, pack_ref):
-    rows = views_ref.shape[0]
-    pack_ref[:rows, :] = views_ref[...].astype(jnp.bfloat16)
+def pack_kernel(place_ref, views_ref, lse_ref, weight_ref, partner_ref, whole_ref, *chunk_refs):
+    total = views_ref.shape[0]
+    rows = total // CHUNKS
     weight = weight_ref[...]
     strength = weight * jnp.exp(SHIFT - lse_ref[...])
     local = partner_ref[...] & 2047
-    place = jnp.full(weight.shape, place_ref[0] * rows, jnp.int32).astype(jnp.float32)
+    place = jnp.full(weight.shape, place_ref[0] * total, jnp.int32).astype(jnp.float32)
     lines = split3(strength) + split3(weight)
     lines += [(local >> 8).astype(jnp.float32), (local & 255).astype(jnp.float32), place]
     lines += [jnp.zeros_like(weight)] * (EXTRA - len(lines))
-    pack_ref[rows:, :] = jnp.concatenate(lines, axis=0).astype(jnp.bfloat16)
+    extra = jnp.concatenate(lines, axis=0).astype(jnp.bfloat16)
+    chunk_refs[0][rows:, :] = extra
+    whole_ref[total:, :] = extra
+    for i, chunk_ref in enumerate(chunk_refs):
+        chunk = views_ref[i * rows : (i + 1) * rows, :].astype(jnp.bfloat16)
+        chunk_ref[:rows, :] = chunk
+        whole_ref[i * rows : (i + 1) * rows, :] = chunk
 
 
 def pack_views(place, views, lse, weight, partner):
     rows, width = views.shape
+    sizes = [rows + EXTRA] + [rows // CHUNKS + (EXTRA if i == 0 else 0) for i in range(CHUNKS)]
     line = (1, rows)
     return call(
         pack_kernel,
-        [((rows + EXTRA, width), jnp.bfloat16)],
+        [((size, width), jnp.bfloat16) for size in sizes],
         (place, views, lse.reshape(line), weight.reshape(line), partner.reshape(line)),
         "pack",
         specs=[pl.BlockSpec(memory_space=pltpu.SMEM)] + [WHOLE] * 4,
-    )[0]
+    )
 
 
 def statistics(first_ref):
@@ -107,13 +115,14 @@
     return lax.dot_general(rows, cols, (((1,), (1,)), ((), ())), preferred_element_type=jnp.float32)
 
 
-def block_kernel(diagonal, row_ref, own_ref, *refs):
+def block_kernel(count, diagonal, *refs):
+    row_refs, own_ref, refs = refs[:count], refs[count], refs[count + 1 :]
     core_refs, (strength_ref, total_ref) = refs[:CHUNKS], refs[CHUNKS:]
     size = total_ref.shape[0]
-    row_strength, row_weight, _, row_place = statistics(row_ref)
+    row_strength, row_weight, _, row_place = statistics(row_refs[0])
     row_strength, row_weight = spread(row_strength), spread(row_weight)
     strength_ref[...] = row_strength
-    rows = joined([row_ref])
+    rows = joined(row_refs)
     row_at = lax.broadcasted_iota(jnp.int32, (size, size), 0)
     total = None
     for col_refs in ([own_ref], core_refs):
@@ -134,9 +143,9 @@
 def block_terms(diagonal, rows, own, core):
     size, width = own.shape[0] - EXTRA, own.shape[1]
     return call(
-        functools.partial(block_kernel, diagonal),
+        functools.partial(block_kernel, len(rows), diagonal),
         [((size, 128), jnp.float32), ((size, width), jnp.float32)],
-        (rows, own, *core),
+        (*rows, own, *core),
         "own_rows" if diagonal else "other_rows",
         flops=32 * size**2 * width,
     )
@@ -150,13 +159,13 @@
     return call(spread_kernel, [((size, 128), jnp.float32)], pack[:1], "spread")[0]
 
 
-def window_kernel(layout, pieces, *refs):
+def window_kernel(layout, pieces, count, *refs):
     refs = list(refs)
     parts = []
     for chunks, addends in layout:
         pack, strength = [refs.pop(0) for _ in range(chunks)], refs.pop(0)
         parts.append((pack, strength, [[refs.pop(0) for _ in range(count)] for count in addends]))
-    cols_refs = [refs.pop(0) for _ in range(CHUNKS)]
+    cols_refs = [refs.pop(0) for _ in range(count)]
     strength, _, _, _ = statistics(cols_refs[0])
     cols = joined(cols_refs)
     for at, (pack, row_strength, addends) in enumerate(parts):
@@ -182,7 +191,7 @@
             aliases.update({len(args) + i: at * pieces + i for i in range(pieces)})
         args += sum(addends, [])
     return call(
-        functools.partial(window_kernel, tuple(layout), pieces),
+        functools.partial(window_kernel, tuple(layout), pieces, len(cols)),
         [((size // pieces, width), dtype)] * (pieces * len(row_packs)),
         (*args, *cols),
         "window",
@@ -225,48 +234,63 @@
         return lax.ppermute(value, "sub", [(0, 1), (1, 0)])
 
     place = ((dp_place % 2) * 2 + sub_place).astype(jnp.int32).reshape(1)
-    whole = pack_views(place, views, log_sum_exp, loss_weight, partner)
-    core = core_swap(whole)
-    coming = {"core": chip_next(core), "own": chip_next(hold(whole, core))}
-    other = sub_swap(whole)
+    whole, *own = pack_views(place, views, log_sum_exp, loss_weight, partner)
+    core = [core_swap(own[0])]
+    for chunk in own[1:]:
+        core.append(core_swap(hold(chunk, core[-1])))
+    strengths, totals, columns = {}, {"core": [], "far": []}, {}
+    strengths["own"], token = block_terms(True, [whole], whole, core)
+    totals["own"] = [[token]]
+    coming = {"core": [chip_next(chunk) for chunk in core], "own": [chip_next(hold(whole, token))]}
+    other = [sub_swap(chunk) for chunk in own]
 
     reach = STEPS // 2
     legs = [(kind, step) for step in range(1, reach) for kind in ("core", "own")] + [("core", reach)]
-    packs = {"own": [whole], "core": [core]}
-    strengths, totals, columns = {}, {"core": [], "far": []}, {}
-    strengths["own"], token = block_terms(True, whole, whole, [core])
-    totals["own"] = [[token]]
-    strengths["core"] = strengths_of([core], size)
-    for arrivals, (kind, step) in enumerate(legs, 1):
-        pack = hold(coming[kind], token)
-        arrived = columns[f"{kind}{step}"] = [pack]
-        if step < reach - (kind == "own"):
-            coming[kind] = chip_next(pack)
-        for name, rows in PLAN.get(arrivals, ()):
+    packs = {"own": [whole], "core": core}
+    strengths["core"] = strengths_of(core, size)
+
+    def run(plan, token, arrived):
+        for name, rows in plan:
             group = [
-                (packs[r], strengths[r], [[hold(hold(a, pack), token) for a in addend] for addend in totals[r]])
+                (packs[r], strengths[r], [[hold(hold(a, arrived), token) for a in addend] for addend in totals[r]])
                 for r in rows
             ]
-            last = name == f"own{reach - 1}" and rows[0] in ("core", "far")
-            if last:
-                sums = window_terms(group, columns[name], jnp.bfloat16)
+            if name == f"own{reach - 1}" and rows[0] in ("core", "far"):
+                sums = window_terms(group, columns[name], jnp.bfloat16, 2)
                 totals[rows[0]] = [sums]
             else:
-                sums = window_terms(group, columns[name], weight=16 if arrivals < 3 else 0)
+                sums = window_terms(group, columns[name], weight=16 if arrivals < 9 else 0)
                 totals.update({r: [[value]] for r, value in zip(rows, sums, strict=True)})
             token = sums[0]
-        if arrivals == ROWS_AT:
-            other = hold(hold(other, pack), token)
-            strengths["other"], token = block_terms(False, other, whole, [core])
-            far = core_swap(other)
-            packs["other"], packs["far"] = [other], [far]
-            totals["other"] = [[token]]
-            strengths["far"] = strengths_of([far], size)
-    back = {r: [core_swap(piece) for piece in totals[r][0]] for r in ("far", "core")}
-    (away,) = window_terms([(packs["other"], strengths["other"], totals["other"] + [back["far"]])], arrived, jnp.bfloat16)
+        return token
+
+    arrivals = 0
+    for kind, step in legs:
+        arrived, sent = [], []
+        columns[f"{kind}{step}"] = arrived
+        for pack in coming[kind]:
+            pack = hold(pack, token)
+            token = hold(token, pack)
+            arrived.append(pack)
+            if step < reach - (kind == "own"):
+                sent.append(chip_next(pack))
+            arrivals += 1
+            token = run(PLAN.get(arrivals, ()), token, pack)
+            if arrivals == ROWS_AT:
+                other = [hold(hold(part, pack), token) for part in other]
+                strengths["other"], token = block_terms(False, other, whole, core)
+                far = [core_swap(part) for part in other]
+                packs["other"], packs["far"] = other, far
+                totals["other"] = [[token]]
+                strengths["far"] = strengths_of(far, size)
+        coming[kind] = sent
+    back = [core_swap(piece) for piece in totals["far"][0]]
+    (away,) = window_terms([(packs["other"], strengths["other"], totals["other"] + [back])], arrived, jnp.bfloat16)
+    token = run(BESIDE, away, pack)
     away = sub_swap(away)
+    back = [core_swap(piece) for piece in totals["core"][0]]
     (here,) = window_terms([(packs["own"], strengths["own"], totals["own"])], arrived)
-    return call(finish_kernel, [(here.shape, jnp.float32)], (here, *back["core"], away), "finish")[0]
+    return call(finish_kernel, [(here.shape, jnp.float32)], (here, *back, away), "finish")[0]
 
 
 def solution(mesh):

time: 78.9 us -> 75.1 us (0.952)
  waiting for transfers between devices: 39.4 us -> 31.3 us
  starting transfers between devices: 15.3 us -> 19 us
    ppermute x2 -> x3, waiting for transfers between devices: 9.25 us -> 1.9 us  [sub_swap(): return lax.ppermute(value, 'sub', [(0, 1), (1, 0)])]
    ppermute x7 -> x11, starting transfers between devices: 4.11 us -> 5.85 us  [chip_next(): return lax.ppermute(value, ('dp', 'sub'), onward)]
    ppermute x4 -> x8, starting transfers between devices: 5.11 us -> 6.84 us  [core_swap(): return lax.ppermute(value, 'dp', cores)]
    pallas_call x21 -> x22, Pallas kernels: 22 us -> 22.5 us  [call(): pl.pallas_call(kernel, out_shape=[jax.ShapeDtypeStruct(shape, dtype) for...]
    ppermute x7 -> x11, waiting for transfers between devices: 28.2 us -> 27.8 us  [chip_next(): return lax.ppermute(value, ('dp', 'sub'), onward)]
    ppermute x4 -> x8, waiting for transfers between devices: 1.93 us -> 1.56 us  [core_swap(): return lax.ppermute(value, 'dp', cores)]
    ppermute x2 -> x3, starting transfers between devices: 6.05 us -> 6.34 us  [sub_swap(): return lax.ppermute(value, 'sub', [(0, 1), (1, 0)])]
  transfers between devices with their start and end apart: 13 -> 22, of which waited for: 8 -> 12; matrix products, arithmetic and copies ran while one was open for 0% -> 0% of each run, Pallas kernels for 26% -> 27%
where the time goes in v4:
time: 75.1 us; the launch traced here: 75 us
  waiting for transfers between devices  31.3 us (42%)
  Pallas kernels  22.5 us (30%)
  starting transfers between devices  19 us (25%)
  local copies, waits for them, and re-layouts  1.93 us (3%)
    ppermute x11, waiting for transfers between devices, chip_next(): return lax.ppermute(value, ('dp', 'sub'), onward)  27.8 us
    pallas_call x22, Pallas kernels, call(): pl.pallas_call(kernel, out_shape=[jax.ShapeDtypeStruct(shape, dtype) for...  22.5 us
    ppermute x8, starting transfers between devices, core_swap(): return lax.ppermute(value, 'dp', cores)  6.84 us
    ppermute x3, starting transfers between devices, sub_swap(): return lax.ppermute(value, 'sub', [(0, 1), (1, 0)])  6.34 us
    ppermute x11, starting transfers between devices, chip_next(): return lax.ppermute(value, ('dp', 'sub'), onward)  5.85 us
    unnamed x8, local copies, waits for them, and re-layouts  1.93 us
    ppermute x3, waiting for transfers between devices, sub_swap(): return lax.ppermute(value, 'sub', [(0, 1), (1, 0)])  1.9 us
    ppermute x8, waiting for transfers between devices, core_swap(): return lax.ppermute(value, 'dp', cores)  1.56 us
  transfers between devices with their start and end apart: 22, of which 12 were waited for; matrix products, arithmetic and copies ran while one was open for 0% of the time, Pallas kernels for 27%

profile of v4, /device:TPU:2, one launch (start us, length us, event | category | flops | bytes accessed | tf_op | source)
XLA Modules:
  0.0 75.0 jit_solution(9701777073433083609)
XLA Ops:
  0.7 1.2 %copy-done = f32[512,512]{1,0:T(8,128)S(1)} copy-done((f32[512,512]{1,0:T(8,128)S(1)}, f32[512,512]{1,0:T(8,128)}, u32[]{:S(2)}) %copy-start) | copy-done | bytes 1048600
  2.1 1.5 %collective-permute-done.refs_2_.first_ref.refs_3_.refs_0_ = bf16[272,512]{1,0:T(8,128)(2,1)S(1)} collective-permute-done((bf16[272,512]{1,0:T(8,128)(2,1)S(1)}, bf16[272,512]{1,0:T(8,128)(2,1)S(1)}, u32[]{:S(2)}, u32[]{:S(2)}) %collective-permute-start) | collective-permute-done | bytes 278560 | tf_op jit(solution)/shard_map/ppermute | solution.py:231
  3.8 1.9 %collective-permute-start.3 = (bf16[272,512]{1,0:T(8,128)(2,1)S(1)}, bf16[272,512]{1,0:T(8,128)(2,1)S(1)}, u32[]{:S(2)}, u32[]{:S(2)}) collective-permute-start(bf16[272,512]{1,0:T(8,128)(2,1)S(1)} %collective-permute-done.refs_2_.first_ref.refs_3_.refs_0_), channel_id=1, source_target_pairs={{0,4},{6,2},{1,5},{7,3},{4,8},{10,6},{5,9},{11,7},{8,12},{14,10},{... | collective-permute-start | bytes 835592 | tf_op jit(solution)/shard_map/ppermute | solution.py:228
  5.7 1.9 %collective-permute-start.2 = (bf16[256,512]{1,0:T(8,128)(2,1)S(1)}, bf16[256,512]{1,0:T(8,128)(2,1)S(1)}, u32[]{:S(2)}, u32[]{:S(2)}) collective-permute-start(bf16[256,512]{1,0:T(8,128)(2,1)S(1)} %collective-permute-done.1.refs_3_.refs_4_.refs_1_), channel_id=1, source_target_pairs={{0,4},{6,2},{1,5},{7,3},{4,8},{10,6},{5,9},{11,7},{8,12},{14,10},{... | collective-permute-start | bytes 786440 | tf_op jit(solution)/shard_map/ppermute | solution.py:228
  7.6 1.5 %own_rows.1 = (f32[512,128]{1,0:T(8,128)S(1)}, f32[512,512]{1,0:T(8,128)S(1)}) custom-call(bf16[528,512]{1,0:T(8,128)(2,1)S(1)} %get-tuple-element.104.refs_0_.refs_1_.refs_2_, bf16[528,512]{1,0:T(8,128)(2,1)S(1)} %get-tuple-element.104.refs_0_.refs_1_.refs_2_, bf16[272,512]{1,0:T(8,128)(2,1)S(1)} %collective-permute-done.refs_2_.first_ref.refs_3_.refs_0_, ...), custom_call_target="tpu_custom_call" | custom-call | flops 4294967296 | tf_op jit(solution)/shard_map/own_rows/pallas_call | solution.py:39
  9.2 2.0 %collective-permute-start.4 = (bf16[528,512]{1,0:T(8,128)(2,1)S(1)}, bf16[528,512]{1,0:T(8,128)(2,1)S(1)}, u32[]{:S(2)}, u32[]{:S(2)}) collective-permute-start(bf16[528,512]{1,0:T(8,128)(2,1)S(1)} %get-tuple-element.104.refs_0_.refs_1_.refs_2_), channel_id=1, source_target_pairs={{0,4},{6,2},{1,5},{7,3},{4,8},{10,6},{5,9},{11,7},{8,12},{14,10},{... | collective-permute-start | bytes 1622024 | tf_op jit(solution)/shard_map/ppermute | solution.py:228
  11.7 1.5 %collective-permute-start.8 = (bf16[272,512]{1,0:T(8,128)(2,1)S(1)}, bf16[272,512]{1,0:T(8,128)(2,1)S(1)}, u32[]{:S(2)}, u32[]{:S(2)}) collective-permute-start(bf16[272,512]{1,0:T(8,128)(2,1)S(1)} %get-tuple-element.96), channel_id=1, source_target_pairs={{0,1},{1,0},{2,3},{3,2},{4,5},{5,4},{6,7},{7,6},{8,9},{9,8},{10,11... | collective-permute-start | bytes 835592 | tf_op jit(solution)/shard_map/ppermute | solution.py:234
  13.3 4.2 %collective-permute-done.3.refs_6_.refs_7_ = bf16[272,512]{1,0:T(8,128)(2,1)S(1)} collective-permute-done((bf16[272,512]{1,0:T(8,128)(2,1)S(1)}, bf16[272,512]{1,0:T(8,128)(2,1)S(1)}, u32[]{:S(2)}, u32[]{:S(2)}) %collective-permute-start.3) | collective-permute-done | bytes 278560 | tf_op jit(solution)/shard_map/ppermute | solution.py:228
  17.6 2.8 %collective-permute-done.2.refs_7_.refs_8_ = bf16[256,512]{1,0:T(8,128)(2,1)S(1)} collective-permute-done((bf16[256,512]{1,0:T(8,128)(2,1)S(1)}, bf16[256,512]{1,0:T(8,128)(2,1)S(1)}, u32[]{:S(2)}, u32[]{:S(2)}) %collective-permute-start.2) | collective-permute-done | bytes 262176 | tf_op jit(solution)/shard_map/ppermute | solution.py:228
  20.4 1.3 %window.16 = (f32[512,512]{1,0:T(8,128)S(1)}, f32[512,512]{1,0:T(8,128)S(1)}) custom-call(bf16[528,512]{1,0:T(8,128)(2,1)S(1)} %get-tuple-element.104.refs_0_.refs_1_.refs_2_, f32[512,128]{1,0:T(8,128)S(1)} %get-tuple-element.99.refs_1_, f32[512,512]{1,0:T(8,128)S(1)} %get-tuple-element.101.refs_2_, ...), custom_call_target="tpu_custom_call", output_to_operand_aliasing={{0}: (2, {})} | custom-call | flops 4294967296 | tf_op jit(solution)/shard_map/window/pallas_call | solution.py:39
  21.7 4.4 %collective-permute-done.4.refs_7_.refs_8_ = bf16[528,512]{1,0:T(8,128)(2,1)S(1)} collective-permute-done((bf16[528,512]{1,0:T(8,128)(2,1)S(1)}, bf16[528,512]{1,0:T(8,128)(2,1)S(1)}, u32[]{:S(2)}, u32[]{:S(2)}) %collective-permute-start.4) | collective-permute-done | bytes 540704 | tf_op jit(solution)/shard_map/ppermute | solution.py:228
  26.2 1.3 %window.17 = (f32[512,512]{1,0:T(8,128)S(1)}, f32[512,512]{1,0:T(8,128)S(1)}) custom-call(bf16[528,512]{1,0:T(8,128)(2,1)S(1)} %get-tuple-element.104.refs_0_.refs_1_.refs_2_, f32[512,128]{1,0:T(8,128)S(1)} %get-tuple-element.99.refs_1_, f32[512,512]{1,0:T(8,128)S(1)} %get-tuple-element.107.refs_2_, ...), custom_call_target="tpu_custom_call", output_to_operand_aliasing={{0}: (2, {}), {1}: (6, {})} | custom-call | flops 4294967296 | tf_op jit(solution)/shard_map/window/pallas_call | solution.py:39
  27.5 1.6 %collective-permute-done.6.refs_8_.refs_7_ = bf16[272,512]{1,0:T(8,128)(2,1)S(1)} collective-permute-done((bf16[272,512]{1,0:T(8,128)(2,1)S(1)}, bf16[272,512]{1,0:T(8,128)(2,1)S(1)}, u32[]{:S(2)}, u32[]{:S(2)}) %collective-permute-start.6) | collective-permute-done | bytes 278560 | tf_op jit(solution)/shard_map/ppermute | solution.py:228
  29.2 2.8 %collective-permute-done.5.refs_9_.refs_8_ = bf16[256,512]{1,0:T(8,128)(2,1)S(1)} collective-permute-done((bf16[256,512]{1,0:T(8,128)(2,1)S(1)}, bf16[256,512]{1,0:T(8,128)(2,1)S(1)}, u32[]{:S(2)}, u32[]{:S(2)}) %collective-permute-start.5) | collective-permute-done | bytes 262176 | tf_op jit(solution)/shard_map/ppermute | solution.py:228
  32.0 5.2 %collective-permute-start.11 = (bf16[272,512]{1,0:T(8,128)(2,1)S(1)}, bf16[272,512]{1,0:T(8,128)(2,1)S(1)}, u32[]{:S(2)}, u32[]{:S(2)}) collective-permute-start(bf16[272,512]{1,0:T(8,128)(2,1)S(1)} %collective-permute-done.8.refs_0_), channel_id=1, source_target_pairs={{0,2},{2,0},{4,6},{6,4},{8,10},{10,8},{12,14},{14,12},{16,18},{18,... | collective-permute-start | bytes 835592 | tf_op jit(solution)/shard_map/ppermute | solution.py:231
  37.2 1.6 %other_rows.1 = (f32[512,128]{1,0:T(8,128)S(1)}, f32[512,512]{1,0:T(8,128)S(1)}) custom-call(bf16[272,512]{1,0:T(8,128)(2,1)S(1)} %collective-permute-done.8.refs_0_, bf16[256,512]{1,0:T(8,128)(2,1)S(1)} %collective-permute-done.9.refs_1_, bf16[528,512]{1,0:T(8,128)(2,1)S(1)} %get-tuple-element.104.refs_0_.refs_1_.refs_2_, ...), custom_call_target="tpu_custom_call" | custom-call | flops 4294967296 | tf_op jit(solution)/shard_map/other_rows/pallas_call | solution.py:39
  39.0 0.8 %collective-permute-done.10.refs_8_.refs_7_ = bf16[528,512]{1,0:T(8,128)(2,1)S(1)} collective-permute-done((bf16[528,512]{1,0:T(8,128)(2,1)S(1)}, bf16[528,512]{1,0:T(8,128)(2,1)S(1)}, u32[]{:S(2)}, u32[]{:S(2)}) %collective-permute-start.10) | collective-permute-done | bytes 540704 | tf_op jit(solution)/shard_map/ppermute | solution.py:228
  39.7 1.3 %window.18 = (f32[512,512]{1,0:T(8,128)S(1)}, f32[512,512]{1,0:T(8,128)S(1)}) custom-call(bf16[272,512]{1,0:T(8,128)(2,1)S(1)} %collective-permute-done.8.refs_0_, bf16[256,512]{1,0:T(8,128)(2,1)S(1)} %collective-permute-done.9.refs_1_, f32[512,128]{1,0:T(8,128)S(1)} %get-tuple-element.120.refs_2_, ...), custom_call_target="tpu_custom_call", output_to_operand_aliasing={{0}: (3, {})} | custom-call | flops 4294967296 | tf_op jit(solution)/shard_map/window/pallas_call | solution.py:39
  41.1 1.6 %collective-permute-done.13.refs_8_.refs_7_ = bf16[272,512]{1,0:T(8,128)(2,1)S(1)} collective-permute-done((bf16[272,512]{1,0:T(8,128)(2,1)S(1)}, bf16[272,512]{1,0:T(8,128)(2,1)S(1)}, u32[]{:S(2)}, u32[]{:S(2)}) %collective-permute-start.13) | collective-permute-done | bytes 278560 | tf_op jit(solution)/shard_map/ppermute | solution.py:228
  42.7 1.3 %window.19 = (f32[512,512]{1,0:T(8,128)S(1)}, f32[512,512]{1,0:T(8,128)S(1)}) custom-call(bf16[272,512]{1,0:T(8,128)(2,1)S(1)} %collective-permute-done.8.refs_0_, bf16[256,512]{1,0:T(8,128)(2,1)S(1)} %collective-permute-done.9.refs_1_, f32[512,128]{1,0:T(8,128)S(1)} %get-tuple-element.120.refs_2_, ...), custom_call_target="tpu_custom_call", output_to_operand_aliasing={{0}: (3, {}), {1}: (7, {})} | custom-call | flops 4294967296 | tf_op jit(solution)/shard_map/window/pallas_call | solution.py:39
  44.1 1.5 %collective-permute-done.7.refs_9_.refs_8_ = bf16[256,512]{1,0:T(8,128)(2,1)S(1)} collective-permute-done((bf16[256,512]{1,0:T(8,128)(2,1)S(1)}, bf16[256,512]{1,0:T(8,128)(2,1)S(1)}, u32[]{:S(2)}, u32[]{:S(2)}) %collective-permute-start.7) | collective-permute-done | bytes 262176 | tf_op jit(solution)/shard_map/ppermute | solution.py:228
  45.5 1.3 %window.20 = (f32[512,512]{1,0:T(8,128)S(1)}, f32[512,512]{1,0:T(8,128)S(1)}) custom-call(bf16[272,512]{1,0:T(8,128)(2,1)S(1)} %collective-permute-done.8.refs_0_, bf16[256,512]{1,0:T(8,128)(2,1)S(1)} %collective-permute-done.9.refs_1_, f32[512,128]{1,0:T(8,128)S(1)} %get-tuple-element.120.refs_2_, ...), custom_call_target="tpu_custom_call", output_to_operand_aliasing={{0}: (3, {}), {1}: (7, {})} | custom-call | flops 4294967296 | tf_op jit(solution)/shard_map/window/pallas_call | solution.py:39
  46.9 1.4 %window.21 = (f32[512,512]{1,0:T(8,128)S(1)}, f32[512,512]{1,0:T(8,128)S(1)}) custom-call(bf16[272,512]{1,0:T(8,128)(2,1)S(1)} %collective-permute-done.8.refs_0_, bf16[256,512]{1,0:T(8,128)(2,1)S(1)} %collective-permute-done.9.refs_1_, f32[512,128]{1,0:T(8,128)S(1)} %get-tuple-element.120.refs_2_, ...), custom_call_target="tpu_custom_call", output_to_operand_aliasing={{0}: (3, {}), {1}: (7, {})} | custom-call | flops 4294967296 | tf_op jit(solution)/shard_map/window/pallas_call | solution.py:39
  48.3 1.3 %window.22 = (f32[512,512]{1,0:T(8,128)S(1)}, f32[512,512]{1,0:T(8,128)S(1)}) custom-call(bf16[272,512]{1,0:T(8,128)(2,1)S(1)} %collective-permute-done.8.refs_0_, bf16[256,512]{1,0:T(8,128)(2,1)S(1)} %collective-permute-done.9.refs_1_, f32[512,128]{1,0:T(8,128)S(1)} %get-tuple-element.120.refs_2_, ...), custom_call_target="tpu_custom_call", output_to_operand_aliasing={{0}: (3, {}), {1}: (7, {})} | custom-call | flops 4294967296 | tf_op jit(solution)/shard_map/window/pallas_call | solution.py:39
  49.6 3.7 %collective-permute-done.15.refs_4_.refs_3_ = bf16[528,512]{1,0:T(8,128)(2,1)S(1)} collective-permute-done((bf16[528,512]{1,0:T(8,128)(2,1)S(1)}, bf16[528,512]{1,0:T(8,128)(2,1)S(1)}, u32[]{:S(2)}, u32[]{:S(2)}) %collective-permute-start.15) | collective-permute-done | bytes 540704 | tf_op jit(solution)/shard_map/ppermute | solution.py:228
  54.8 4.3 %collective-permute-done.14.refs_7_.refs_4_ = bf16[256,512]{1,0:T(8,128)(2,1)S(1)} collective-permute-done((bf16[256,512]{1,0:T(8,128)(2,1)S(1)}, bf16[256,512]{1,0:T(8,128)(2,1)S(1)}, u32[]{:S(2)}, u32[]{:S(2)}) %collective-permute-start.14) | collective-permute-done | bytes 262176 | tf_op jit(solution)/shard_map/ppermute | solution.py:228
  60.6 4.3 %collective-permute-start.21 = (bf16[512,512]{1,0:T(8,128)(2,1)S(1)}, bf16[512,512]{1,0:T(8,128)(2,1)S(1)}, u32[]{:S(2)}, u32[]{:S(2)}) collective-permute-start(bf16[512,512]{1,0:T(8,128)(2,1)S(1)} %window.25), channel_id=1, source_target_pairs={{0,1},{1,0},{2,3},{3,2},{4,5},{5,4},{6,7},{7,6},{8,9},{9,8},{10,11... | collective-permute-start | bytes 1572872 | tf_op jit(solution)/shard_map/ppermute | solution.py:234
  65.0 1.3 %window.26 = (f32[512,512]{1,0:T(8,128)S(1)}, f32[512,512]{1,0:T(8,128)S(1)}) custom-call(bf16[528,512]{1,0:T(8,128)(2,1)S(1)} %get-tuple-element.104.refs_0_.refs_1_.refs_2_, f32[512,128]{1,0:T(8,128)S(1)} %get-tuple-element.99.refs_1_, f32[512,512]{1,0:T(8,128)S(1)} %get-tuple-element.161.refs_2_, ...), custom_call_target="tpu_custom_call", output_to_operand_aliasing={{0}: (2, {}), {1}: (6, {})} | custom-call | tf_op jit(solution)/shard_map/window/pallas_call | solution.py:39
  66.3 1.4 %window.27 = (f32[512,512]{1,0:T(8,128)S(1)}, f32[512,512]{1,0:T(8,128)S(1)}) custom-call(bf16[528,512]{1,0:T(8,128)(2,1)S(1)} %get-tuple-element.104.refs_0_.refs_1_.refs_2_, f32[512,128]{1,0:T(8,128)S(1)} %get-tuple-element.99.refs_1_, f32[512,512]{1,0:T(8,128)S(1)} %get-tuple-element.167.refs_2_, ...), custom_call_target="tpu_custom_call", output_to_operand_aliasing={{0}: (2, {}), {1}: (6, {})} | custom-call | tf_op jit(solution)/shard_map/window/pallas_call | solution.py:39
  67.7 1.3 %window.28 = (f32[512,512]{1,0:T(8,128)S(1)}, f32[512,512]{1,0:T(8,128)S(1)}) custom-call(bf16[528,512]{1,0:T(8,128)(2,1)S(1)} %get-tuple-element.104.refs_0_.refs_1_.refs_2_, f32[512,128]{1,0:T(8,128)S(1)} %get-tuple-element.99.refs_1_, f32[512,512]{1,0:T(8,128)S(1)} %get-tuple-element.173.refs_2_, ...), custom_call_target="tpu_custom_call", output_to_operand_aliasing={{0}: (2, {}), {1}: (6, {})} | custom-call | tf_op jit(solution)/shard_map/window/pallas_call | solution.py:39
  71.9 1.9 %collective-permute-done.21.refs_2_ = bf16[512,512]{1,0:T(8,128)(2,1)S(1)} collective-permute-done((bf16[512,512]{1,0:T(8,128)(2,1)S(1)}, bf16[512,512]{1,0:T(8,128)(2,1)S(1)}, u32[]{:S(2)}, u32[]{:S(2)}) %collective-permute-start.21) | collective-permute-done | bytes 524320 | tf_op jit(solution)/shard_map/ppermute | solution.py:234
  73.8 1.1 %finish.1 = f32[512,512]{1,0:T(8,128)} custom-call(f32[512,512]{1,0:T(8,128)S(1)} %window.31.here_ref, bf16[256,512]{1,0:T(8,128)(2,1)S(1)} %collective-permute-done.19.refs_0_, bf16[256,512]{1,0:T(8,128)(2,1)S(1)} %collective-permute-done.20.refs_1_, bf16[512,512]{1,0:T(8,128)(2,1)S(1)} %collective-permute-done.21.refs_2_), custom_call_target="tpu_custom_call" | custom-call | tf_op jit(solution)/shard_map/finish/pallas_call | solution.py:39
  (42 shorter events, 7.8 us)
Async XLA Ops:
  0.0 0.7 copy-start.3
  0.0 0.7 copy-start.2
  0.0 0.7 copy-start.1
  0.7 1.2 %copy-start = (f32[512,512]{1,0:T(8,128)S(1)}, f32[512,512]{1,0:T(8,128)}, u32[]{:S(2)}) copy-start(f32[512,512]{1,0:T(8,128)} %views_ref.1) | copy-start | bytes 3145732
  2.0 1.6 %collective-permute-start = (bf16[272,512]{1,0:T(8,128)(2,1)S(1)}, bf16[272,512]{1,0:T(8,128)(2,1)S(1)}, u32[]{:S(2)}, u32[]{:S(2)}) collective-permute-start(bf16[272,512]{1,0:T(8,128)(2,1)S(1)} %get-tuple-element.96), channel_id=1, source_target_pairs={{0,2},{2,0},{4,6},{6,4},{8,10},{10,8},{12,14},{14,12},{16,18},{18,... | collective-permute-start | bytes 835592 | tf_op jit(solution)/shard_map/ppermute | solution.py:231
  3.7 2.1 %collective-permute-start.1 = (bf16[256,512]{1,0:T(8,128)(2,1)S(1)}, bf16[256,512]{1,0:T(8,128)(2,1)S(1)}, u32[]{:S(2)}, u32[]{:S(2)}) collective-permute-start(bf16[256,512]{1,0:T(8,128)(2,1)S(1)} %get-tuple-element.98), channel_id=1, source_target_pairs={{0,2},{2,0},{4,6},{6,4},{8,10},{10,8},{12,14},{14,12},{16,18},{18,... | collective-permute-start | bytes 786440 | tf_op jit(solution)/shard_map/ppermute | solution.py:231
  3.8 13.8 %collective-permute-start.3 = (bf16[272,512]{1,0:T(8,128)(2,1)S(1)}, bf16[272,512]{1,0:T(8,128)(2,1)S(1)}, u32[]{:S(2)}, u32[]{:S(2)}) collective-permute-start(bf16[272,512]{1,0:T(8,128)(2,1)S(1)} %collective-permute-done.refs_2_.first_ref.refs_3_.refs_0_), channel_id=1, source_target_pairs={{0,4},{6,2},{1,5},{7,3},{4,8},{10,6},{5,9},{11,7},{8,12},{14,10},{... | collective-permute-start | bytes 835592 | tf_op jit(solution)/shard_map/ppermute | solution.py:228
  5.7 14.6 %collective-permute-start.2 = (bf16[256,512]{1,0:T(8,128)(2,1)S(1)}, bf16[256,512]{1,0:T(8,128)(2,1)S(1)}, u32[]{:S(2)}, u32[]{:S(2)}) collective-permute-start(bf16[256,512]{1,0:T(8,128)(2,1)S(1)} %collective-permute-done.1.refs_3_.refs_4_.refs_1_), channel_id=1, source_target_pairs={{0,4},{6,2},{1,5},{7,3},{4,8},{10,6},{5,9},{11,7},{8,12},{14,10},{... | collective-permute-start | bytes 786440 | tf_op jit(solution)/shard_map/ppermute | solution.py:228
  9.2 17.0 %collective-permute-start.4 = (bf16[528,512]{1,0:T(8,128)(2,1)S(1)}, bf16[528,512]{1,0:T(8,128)(2,1)S(1)}, u32[]{:S(2)}, u32[]{:S(2)}) collective-permute-start(bf16[528,512]{1,0:T(8,128)(2,1)S(1)} %get-tuple-element.104.refs_0_.refs_1_.refs_2_), channel_id=1, source_target_pairs={{0,4},{6,2},{1,5},{7,3},{4,8},{10,6},{5,9},{11,7},{8,12},{14,10},{... | collective-permute-start | bytes 1622024 | tf_op jit(solution)/shard_map/ppermute | solution.py:228
  11.2 20.8 %collective-permute-start.9 = (bf16[256,512]{1,0:T(8,128)(2,1)S(1)}, bf16[256,512]{1,0:T(8,128)(2,1)S(1)}, u32[]{:S(2)}, u32[]{:S(2)}) collective-permute-start(bf16[256,512]{1,0:T(8,128)(2,1)S(1)} %get-tuple-element.98), channel_id=1, source_target_pairs={{0,1},{1,0},{2,3},{3,2},{4,5},{5,4},{6,7},{7,6},{8,9},{9,8},{10,11... | collective-permute-start | bytes 786440 | tf_op jit(solution)/shard_map/ppermute | solution.py:234
  11.7 20.3 %collective-permute-start.8 = (bf16[272,512]{1,0:T(8,128)(2,1)S(1)}, bf16[272,512]{1,0:T(8,128)(2,1)S(1)}, u32[]{:S(2)}, u32[]{:S(2)}) collective-permute-start(bf16[272,512]{1,0:T(8,128)(2,1)S(1)} %get-tuple-element.96), channel_id=1, source_target_pairs={{0,1},{1,0},{2,3},{3,2},{4,5},{5,4},{6,7},{7,6},{8,9},{9,8},{10,11... | collective-permute-start | bytes 835592 | tf_op jit(solution)/shard_map/ppermute | solution.py:234
  17.6 11.6 %collective-permute-start.6 = (bf16[272,512]{1,0:T(8,128)(2,1)S(1)}, bf16[272,512]{1,0:T(8,128)(2,1)S(1)}, u32[]{:S(2)}, u32[]{:S(2)}) collective-permute-start(bf16[272,512]{1,0:T(8,128)(2,1)S(1)} %collective-permute-done.3.refs_6_.refs_7_), channel_id=1, source_target_pairs={{0,4},{6,2},{1,5},{7,3},{4,8},{10,6},{5,9},{11,7},{8,12},{14,10},{... | collective-permute-start | bytes 835592 | tf_op jit(solution)/shard_map/ppermute | solution.py:228
  20.4 11.6 %collective-permute-start.5 = (bf16[256,512]{1,0:T(8,128)(2,1)S(1)}, bf16[256,512]{1,0:T(8,128)(2,1)S(1)}, u32[]{:S(2)}, u32[]{:S(2)}) collective-permute-start(bf16[256,512]{1,0:T(8,128)(2,1)S(1)} %collective-permute-done.2.refs_7_.refs_8_), channel_id=1, source_target_pairs={{0,4},{6,2},{1,5},{7,3},{4,8},{10,6},{5,9},{11,7},{8,12},{14,10},{... | collective-permute-start | bytes 786440 | tf_op jit(solution)/shard_map/ppermute | solution.py:228
  26.2 13.6 %collective-permute-start.10 = (bf16[528,512]{1,0:T(8,128)(2,1)S(1)}, bf16[528,512]{1,0:T(8,128)(2,1)S(1)}, u32[]{:S(2)}, u32[]{:S(2)}) collective-permute-start(bf16[528,512]{1,0:T(8,128)(2,1)S(1)} %collective-permute-done.4.refs_7_.refs_8_), channel_id=1, source_target_pairs={{0,4},{6,2},{1,5},{7,3},{4,8},{10,6},{5,9},{11,7},{8,12},{14,10},{... | collective-permute-start | bytes 1622024 | tf_op jit(solution)/shard_map/ppermute | solution.py:228
  29.1 13.6 %collective-permute-start.13 = (bf16[272,512]{1,0:T(8,128)(2,1)S(1)}, bf16[272,512]{1,0:T(8,128)(2,1)S(1)}, u32[]{:S(2)}, u32[]{:S(2)}) collective-permute-start(bf16[272,512]{1,0:T(8,128)(2,1)S(1)} %collective-permute-done.6.refs_8_.refs_7_), channel_id=1, source_target_pairs={{0,4},{6,2},{1,5},{7,3},{4,8},{10,6},{5,9},{11,7},{8,12},{14,10},{... | collective-permute-start | bytes 835592 | tf_op jit(solution)/shard_map/ppermute | solution.py:228
  32.0 13.6 %collective-permute-start.7 = (bf16[256,512]{1,0:T(8,128)(2,1)S(1)}, bf16[256,512]{1,0:T(8,128)(2,1)S(1)}, u32[]{:S(2)}, u32[]{:S(2)}) collective-permute-start(bf16[256,512]{1,0:T(8,128)(2,1)S(1)} %collective-permute-done.5.refs_9_.refs_8_), channel_id=1, source_target_pairs={{0,4},{6,2},{1,5},{7,3},{4,8},{10,6},{5,9},{11,7},{8,12},{14,10},{... | collective-permute-start | bytes 786440 | tf_op jit(solution)/shard_map/ppermute | solution.py:228
  32.0 6.8 %collective-permute-start.11 = (bf16[272,512]{1,0:T(8,128)(2,1)S(1)}, bf16[272,512]{1,0:T(8,128)(2,1)S(1)}, u32[]{:S(2)}, u32[]{:S(2)}) collective-permute-start(bf16[272,512]{1,0:T(8,128)(2,1)S(1)} %collective-permute-done.8.refs_0_), channel_id=1, source_target_pairs={{0,2},{2,0},{4,6},{6,4},{8,10},{10,8},{12,14},{14,12},{16,18},{18,... | collective-permute-start | bytes 835592 | tf_op jit(solution)/shard_map/ppermute | solution.py:231
  37.2 2.6 %collective-permute-start.12 = (bf16[256,512]{1,0:T(8,128)(2,1)S(1)}, bf16[256,512]{1,0:T(8,128)(2,1)S(1)}, u32[]{:S(2)}, u32[]{:S(2)}) collective-permute-start(bf16[256,512]{1,0:T(8,128)(2,1)S(1)} %collective-permute-done.9.refs_1_), channel_id=1, source_target_pairs={{0,2},{2,0},{4,6},{6,4},{8,10},{10,8},{12,14},{14,12},{16,18},{18,... | collective-permute-start | bytes 786440 | tf_op jit(solution)/shard_map/ppermute | solution.py:231
  39.7 13.6 %collective-permute-start.15 = (bf16[528,512]{1,0:T(8,128)(2,1)S(1)}, bf16[528,512]{1,0:T(8,128)(2,1)S(1)}, u32[]{:S(2)}, u32[]{:S(2)}) collective-permute-start(bf16[528,512]{1,0:T(8,128)(2,1)S(1)} %collective-permute-done.10.refs_8_.refs_7_), channel_id=1, source_target_pairs={{0,4},{6,2},{1,5},{7,3},{4,8},{10,6},{5,9},{11,7},{8,12},{14,10},{... | collective-permute-start | bytes 1622024 | tf_op jit(solution)/shard_map/ppermute | solution.py:228
  42.7 17.1 %collective-permute-start.18 = (bf16[272,512]{1,0:T(8,128)(2,1)S(1)}, bf16[272,512]{1,0:T(8,128)(2,1)S(1)}, u32[]{:S(2)}, u32[]{:S(2)}) collective-permute-start(bf16[272,512]{1,0:T(8,128)(2,1)S(1)} %collective-permute-done.13.refs_8_.refs_7_), channel_id=1, source_target_pairs={{0,4},{6,2},{1,5},{7,3},{4,8},{10,6},{5,9},{11,7},{8,12},{14,10},{... | collective-permute-start | bytes 835592 | tf_op jit(solution)/shard_map/ppermute | solution.py:228
  45.5 13.6 %collective-permute-start.14 = (bf16[256,512]{1,0:T(8,128)(2,1)S(1)}, bf16[256,512]{1,0:T(8,128)(2,1)S(1)}, u32[]{:S(2)}, u32[]{:S(2)}) collective-permute-start(bf16[256,512]{1,0:T(8,128)(2,1)S(1)} %collective-permute-done.7.refs_9_.refs_8_), channel_id=1, source_target_pairs={{0,4},{6,2},{1,5},{7,3},{4,8},{10,6},{5,9},{11,7},{8,12},{14,10},{... | collective-permute-start | bytes 786440 | tf_op jit(solution)/shard_map/ppermute | solution.py:228
  54.1 5.8 %collective-permute-start.16 = (bf16[256,512]{1,0:T(8,128)(2,1)S(1)}, bf16[256,512]{1,0:T(8,128)(2,1)S(1)}, u32[]{:S(2)}, u32[]{:S(2)}) collective-permute-start(bf16[256,512]{1,0:T(8,128)(2,1)S(1)} %get-tuple-element.157), channel_id=1, source_target_pairs={{0,2},{2,0},{4,6},{6,4},{8,10},{10,8},{12,14},{14,12},{16,18},{18,... | collective-permute-start | bytes 786440 | tf_op jit(solution)/shard_map/ppermute | solution.py:231
  54.5 5.4 %collective-permute-start.17 = (bf16[256,512]{1,0:T(8,128)(2,1)S(1)}, bf16[256,512]{1,0:T(8,128)(2,1)S(1)}, u32[]{:S(2)}, u32[]{:S(2)}) collective-permute-start(bf16[256,512]{1,0:T(8,128)(2,1)S(1)} %get-tuple-element.159), channel_id=1, source_target_pairs={{0,2},{2,0},{4,6},{6,4},{8,10},{10,8},{12,14},{14,12},{16,18},{18,... | collective-permute-start | bytes 786440 | tf_op jit(solution)/shard_map/ppermute | solution.py:231
  60.6 13.2 %collective-permute-start.21 = (bf16[512,512]{1,0:T(8,128)(2,1)S(1)}, bf16[512,512]{1,0:T(8,128)(2,1)S(1)}, u32[]{:S(2)}, u32[]{:S(2)}) collective-permute-start(bf16[512,512]{1,0:T(8,128)(2,1)S(1)} %window.25), channel_id=1, source_target_pairs={{0,1},{1,0},{2,3},{3,2},{4,5},{5,4},{6,7},{7,6},{8,9},{9,8},{10,11... | collective-permute-start | bytes 1572872 | tf_op jit(solution)/shard_map/ppermute | solution.py:234
  69.8 2.1 %collective-permute-start.19 = (bf16[256,512]{1,0:T(8,128)(2,1)S(1)}, bf16[256,512]{1,0:T(8,128)(2,1)S(1)}, u32[]{:S(2)}, u32[]{:S(2)}) collective-permute-start(bf16[256,512]{1,0:T(8,128)(2,1)S(1)} %get-tuple-element.182), channel_id=1, source_target_pairs={{0,2},{2,0},{4,6},{6,4},{8,10},{10,8},{12,14},{14,12},{16,18},{18,... | collective-permute-start | bytes 786440 | tf_op jit(solution)/shard_map/ppermute | solution.py:231
  69.9 2.0 %collective-permute-start.20 = (bf16[256,512]{1,0:T(8,128)(2,1)S(1)}, bf16[256,512]{1,0:T(8,128)(2,1)S(1)}, u32[]{:S(2)}, u32[]{:S(2)}) collective-permute-start(bf16[256,512]{1,0:T(8,128)(2,1)S(1)} %get-tuple-element.184), channel_id=1, source_target_pairs={{0,2},{2,0},{4,6},{6,4},{8,10},{10,8},{12,14},{14,12},{16,18},{18,... | collective-permute-start | bytes 786440 | tf_op jit(solution)/shard_map/ppermute | solution.py:231

commit v5 on v4

--- a/solution.py
+++ b/solution.py
@@ -21,12 +21,14 @@
 
 PLAN = {
     2: [("core1", ("own", "core"))],
-    3: [("own1", ("own", "core"))],
-    6: [("core1", ("other", "far"))],
-    7: [("own1", ("other", "far"))],
-    8: [("core2", ("other", "far")), ("own2", ("other", "far")), ("core3", ("other", "far"))],
-    9: [("own3", ("far",)), ("own3", ("other",))],
+    4: [("own1", ("own", "core"))],
+    6: [("core1", ("other",)), ("own1", ("other",))],
+    8: [("core1", ("far",)), ("own1", ("far",))],
+    9: [("core2", ("other", "far"))],
+    10: [("own2", ("other", "far")), ("core3", ("other", "far"))],
+    12: [("own3", ("far",)), ("own3", ("other",))],
 }
+FAR_AT = 8
 BESIDE = [(name, ("own", "core")) for name in ("core2", "own2", "core3")] + [("own3", ("core",)), ("own3", ("own",))]
 ROWS_AT = 5
 
@@ -97,6 +99,10 @@
     return strength, weight, partner, lines[8:9]
 
 
+def part_of(ref, offset):
+    return ref if offset is None else ref.at[pl.ds(offset, ref.shape[0] // 2)]
+
+
 def joined(chunk_refs):
     first = chunk_refs[0][: chunk_refs[0].shape[0] - EXTRA, :]
     rest = [ref[...] for ref in chunk_refs[1:]]
@@ -115,9 +121,9 @@
     return lax.dot_general(rows, cols, (((1,), (1,)), ((), ())), preferred_element_type=jnp.float32)
 
 
-def block_kernel(count, diagonal, *refs):
-    row_refs, own_ref, refs = refs[:count], refs[count], refs[count + 1 :]
-    core_refs, (strength_ref, total_ref) = refs[:CHUNKS], refs[CHUNKS:]
+def block_kernel(diagonal, row_ref, own_ref, *refs):
+    core_refs, (strength_ref, total_ref, *both) = refs[:CHUNKS], refs[CHUNKS:]
+    row_refs = [row_ref]
     size = total_ref.shape[0]
     row_strength, row_weight, _, row_place = statistics(row_refs[0])
     row_strength, row_weight = spread(row_strength), spread(row_weight)
@@ -138,32 +144,38 @@
         term = jnp.dot(value.astype(jnp.bfloat16), cols, preferred_element_type=jnp.float32)
         total = term if total is None else total + term
     total_ref[...] = total
+    if both:
+        both[0][:size, :] = joined(core_refs)
+        both[0][size:, :] = core_refs[0][core_refs[0].shape[0] - EXTRA :, :]
 
 
 def block_terms(diagonal, rows, own, core):
     size, width = own.shape[0] - EXTRA, own.shape[1]
+    both = [(own.shape, jnp.bfloat16)] if diagonal else []
     return call(
-        functools.partial(block_kernel, len(rows), diagonal),
-        [((size, 128), jnp.float32), ((size, width), jnp.float32)],
-        (*rows, own, *core),
+        functools.partial(block_kernel, diagonal),
+        [((size, 128), jnp.float32), ((size, width), jnp.float32)] + both,
+        (rows, own, *core),
         "own_rows" if diagonal else "other_rows",
         flops=32 * size**2 * width,
     )
 
 
-def spread_kernel(first_ref, out_ref):
-    out_ref[...] = spread(statistics(first_ref)[0])
+def spread_kernel(offset, first_ref, out_ref):
+    out_ref[...] = spread(statistics(part_of(first_ref, offset))[0])
 
 
 def strengths_of(pack, size):
-    return call(spread_kernel, [((size, 128), jnp.float32)], pack[:1], "spread")[0]
+    array, offset = pack[0]
+    kernel = functools.partial(spread_kernel, offset)
+    return call(kernel, [((size, 128), jnp.float32)], (array,), "spread")[0]
 
 
 def window_kernel(layout, pieces, count, *refs):
     refs = list(refs)
     parts = []
-    for chunks, addends in layout:
-        pack, strength = [refs.pop(0) for _ in range(chunks)], refs.pop(0)
+    for offsets, addends in layout:
+        pack, strength = [part_of(refs.pop(0), offset) for offset in offsets], refs.pop(0)
         parts.append((pack, strength, [[refs.pop(0) for _ in range(count)] for count in addends]))
     cols_refs = [refs.pop(0) for _ in range(count)]
     strength, _, _, _ = statistics(cols_refs[0])
@@ -185,8 +197,8 @@
     size, width = row_packs[0][1].shape[0], cols[0].shape[1]
     args, layout, aliases = [], [], {}
     for at, (pack, strength, addends) in enumerate(row_packs):
-        layout.append((len(pack), tuple(len(addend) for addend in addends)))
-        args += [*pack, strength]
+        layout.append((tuple(offset for _, offset in pack), tuple(len(addend) for addend in addends)))
+        args += [*[array for array, _ in pack], strength]
         if addends and len(addends[0]) == pieces and dtype == addends[0][0].dtype:
             aliases.update({len(args) + i: at * pieces + i for i in range(pieces)})
         args += sum(addends, [])
@@ -239,15 +251,16 @@
     for chunk in own[1:]:
         core.append(core_swap(hold(chunk, core[-1])))
     strengths, totals, columns = {}, {"core": [], "far": []}, {}
-    strengths["own"], token = block_terms(True, [whole], whole, core)
+    strengths["own"], token, core_whole = block_terms(True, whole, whole, core)
     totals["own"] = [[token]]
-    coming = {"core": [chip_next(chunk) for chunk in core], "own": [chip_next(hold(whole, token))]}
-    other = [sub_swap(chunk) for chunk in own]
+    coming = {"core": [chip_next(chunk) for chunk in core], "own": [chip_next(hold(chunk, token)) for chunk in own]}
+    other = sub_swap(whole)
+    far = sub_swap(hold(core_whole, other))
 
     reach = STEPS // 2
     legs = [(kind, step) for step in range(1, reach) for kind in ("core", "own")] + [("core", reach)]
-    packs = {"own": [whole], "core": core}
-    strengths["core"] = strengths_of(core, size)
+    packs = {"own": [(whole, None)], "core": [(chunk, None) for chunk in core]}
+    strengths["core"] = strengths_of(packs["core"], size)
 
     def run(plan, token, arrived):
         for name, rows in plan:
@@ -275,14 +288,16 @@
             if step < reach - (kind == "own"):
                 sent.append(chip_next(pack))
             arrivals += 1
+            if arrivals == FAR_AT:
+                far = hold(hold(far, pack), token)
+                packs["far"] = [(far, None)]
+                strengths["far"] = strengths_of(packs["far"], size)
             token = run(PLAN.get(arrivals, ()), token, pack)
             if arrivals == ROWS_AT:
-                other = [hold(hold(part, pack), token) for part in other]
+                other = hold(hold(other, pack), token)
                 strengths["other"], token = block_terms(False, other, whole, core)
-                far = [core_swap(part) for part in other]
-                packs["other"], packs["far"] = other, far
                 totals["other"] = [[token]]
-                strengths["far"] = strengths_of(far, size)
+                packs["other"] = [(other, None)]
         coming[kind] = sent
     back = [core_swap(piece) for piece in totals["far"][0]]
     (away,) = window_terms([(packs["other"], strengths["other"], totals["other"] + [back])], arrived, jnp.bfloat16)

time: 75.1 us -> 74.1 us (0.987)
  waiting for transfers between devices: 31.3 us -> 30.1 us
    ppermute x11 -> x14, waiting for transfers between devices: 27.8 us -> 21.2 us  [chip_next(): return lax.ppermute(value, ('dp', 'sub'), onward)]
    ppermute x3, waiting for transfers between devices: 1.9 us -> 7.3 us  [sub_swap(): return lax.ppermute(value, 'sub', [(0, 1), (1, 0)])]
    ppermute x11 -> x14, starting transfers between devices: 5.85 us -> 10.5 us  [chip_next(): return lax.ppermute(value, ('dp', 'sub'), onward)]
    ppermute x8 -> x6, starting transfers between devices: 6.84 us -> 2.2 us  [core_swap(): return lax.ppermute(value, 'dp', cores)]
    pallas_call x22 -> x24, Pallas kernels: 22.5 us -> 22.7 us  [call(): pl.pallas_call(kernel, out_shape=[jax.ShapeDtypeStruct(shape, dtype) for...]
    ppermute x8 -> x6, waiting for transfers between devices: 1.56 us -> 1.56 us  [core_swap(): return lax.ppermute(value, 'dp', cores)]
  transfers between devices with their start and end apart: 22 -> 23, of which waited for: 12 -> 16; matrix products, arithmetic and copies ran while one was open for 0% -> 0% of each run, Pallas kernels for 27% -> 28%
where the time goes in v5:
time: 74.1 us; the launch traced here: 73.9 us
  waiting for transfers between devices  30.1 us (41%)
  Pallas kernels  22.7 us (31%)
  starting transfers between devices  19 us (26%)
  local copies, waits for them, and re-layouts  1.93 us (3%)
    pallas_call x24, Pallas kernels, call(): pl.pallas_call(kernel, out_shape=[jax.ShapeDtypeStruct(shape, dtype) for...  22.7 us
    ppermute x14, waiting for transfers between devices, chip_next(): return lax.ppermute(value, ('dp', 'sub'), onward)  21.2 us
    ppermute x14, starting transfers between devices, chip_next(): return lax.ppermute(value, ('dp', 'sub'), onward)  10.5 us
    ppermute x3, waiting for transfers between devices, sub_swap(): return lax.ppermute(value, 'sub', [(0, 1), (1, 0)])  7.3 us
    ppermute x3, starting transfers between devices, sub_swap(): return lax.ppermute(value, 'sub', [(0, 1), (1, 0)])  6.33 us
    ppermute x6, starting transfers between devices, core_swap(): return lax.ppermute(value, 'dp', cores)  2.2 us
    unnamed x8, local copies, waits for them, and re-layouts  1.93 us
    ppermute x6, waiting for transfers between devices, core_swap(): return lax.ppermute(value, 'dp', cores)  1.56 us
  transfers between devices with their start and end apart: 23, of which 16 were waited for; matrix products, arithmetic and copies ran while one was open for 0% of the time, Pallas kernels for 28%

profile of v5, /device:TPU:2, one launch (start us, length us, event | category | flops | bytes accessed | tf_op | source)
XLA Modules:
  0.0 73.9 jit_solution(7512773745890164512)
XLA Ops:
  0.7 1.2 %copy-done = f32[512,512]{1,0:T(8,128)S(1)} copy-done((f32[512,512]{1,0:T(8,128)S(1)}, f32[512,512]{1,0:T(8,128)}, u32[]{:S(2)}) %copy-start) | copy-done | bytes 1048600
  2.1 1.5 %collective-permute-done.refs_0_.first_ref.refs_3_ = bf16[272,512]{1,0:T(8,128)(2,1)S(1)} collective-permute-done((bf16[272,512]{1,0:T(8,128)(2,1)S(1)}, bf16[272,512]{1,0:T(8,128)(2,1)S(1)}, u32[]{:S(2)}, u32[]{:S(2)}) %collective-permute-start) | collective-permute-done | bytes 278560 | tf_op jit(solution)/shard_map/ppermute | solution.py:243
  3.8 2.3 %collective-permute-start.7 = (bf16[528,512]{1,0:T(8,128)(2,1)S(1)}, bf16[528,512]{1,0:T(8,128)(2,1)S(1)}, u32[]{:S(2)}, u32[]{:S(2)}) collective-permute-start(bf16[528,512]{1,0:T(8,128)(2,1)S(1)} %get-tuple-element.92.row_ref.own_ref.refs_0_), channel_id=1, source_target_pairs={{0,1},{1,0},{2,3},{3,2},{4,5},{5,4},{6,7},{7,6},{8,9},{9,8},{10,11... | collective-permute-start | bytes 1622024 | tf_op jit(solution)/shard_map/ppermute | solution.py:246
  6.4 2.0 %collective-permute-start.2 = (bf16[256,512]{1,0:T(8,128)(2,1)S(1)}, bf16[256,512]{1,0:T(8,128)(2,1)S(1)}, u32[]{:S(2)}, u32[]{:S(2)}) collective-permute-start(bf16[256,512]{1,0:T(8,128)(2,1)S(1)} %collective-permute-done.1.refs_1_.refs_4_), channel_id=1, source_target_pairs={{0,4},{6,2},{1,5},{7,3},{4,8},{10,6},{5,9},{11,7},{8,12},{14,10},{... | collective-permute-start | bytes 786440 | tf_op jit(solution)/shard_map/ppermute | solution.py:240
  8.4 1.5 %own_rows.1 = (f32[512,128]{1,0:T(8,128)S(1)}, f32[512,512]{1,0:T(8,128)S(1)}, bf16[528,512]{1,0:T(8,128)(2,1)S(1)}) custom-call(bf16[528,512]{1,0:T(8,128)(2,1)S(1)} %get-tuple-element.92.row_ref.own_ref.refs_0_, bf16[528,512]{1,0:T(8,128)(2,1)S(1)} %get-tuple-element.92.row_ref.own_ref.refs_0_, ...), custom_call_target="tpu_custom_call" | custom-call | flops 4294967296 | tf_op jit(solution)/shard_map/own_rows/pallas_call | solution.py:41
  9.9 2.0 %collective-permute-start.5 = (bf16[272,512]{1,0:T(8,128)(2,1)S(1)}, bf16[272,512]{1,0:T(8,128)(2,1)S(1)}, u32[]{:S(2)}, u32[]{:S(2)}) collective-permute-start(bf16[272,512]{1,0:T(8,128)(2,1)S(1)} %get-tuple-element.102), channel_id=1, source_target_pairs={{0,4},{6,2},{1,5},{7,3},{4,8},{10,6},{5,9},{11,7},{8,12},{14,10},{... | collective-permute-start | bytes 835592 | tf_op jit(solution)/shard_map/ppermute | solution.py:240
  11.9 3.1 %collective-permute-start.4 = (bf16[256,512]{1,0:T(8,128)(2,1)S(1)}, bf16[256,512]{1,0:T(8,128)(2,1)S(1)}, u32[]{:S(2)}, u32[]{:S(2)}) collective-permute-start(bf16[256,512]{1,0:T(8,128)(2,1)S(1)} %get-tuple-element.101), channel_id=1, source_target_pairs={{0,4},{6,2},{1,5},{7,3},{4,8},{10,6},{5,9},{11,7},{8,12},{14,10},{... | collective-permute-start | bytes 786440 | tf_op jit(solution)/shard_map/ppermute | solution.py:240
  15.1 3.8 %collective-permute-done.7.row_ref.refs_0_ = bf16[528,512]{1,0:T(8,128)(2,1)S(1)} collective-permute-done((bf16[528,512]{1,0:T(8,128)(2,1)S(1)}, bf16[528,512]{1,0:T(8,128)(2,1)S(1)}, u32[]{:S(2)}, u32[]{:S(2)}) %collective-permute-start.7) | collective-permute-done | bytes 540704 | tf_op jit(solution)/shard_map/ppermute | solution.py:246
  18.9 1.7 %collective-permute-start.11 = (bf16[528,512]{1,0:T(8,128)(2,1)S(1)}, bf16[528,512]{1,0:T(8,128)(2,1)S(1)}, u32[]{:S(2)}, u32[]{:S(2)}) collective-permute-start(bf16[528,512]{1,0:T(8,128)(2,1)S(1)} %get-tuple-element.122), channel_id=1, source_target_pairs={{0,1},{1,0},{2,3},{3,2},{4,5},{5,4},{6,7},{7,6},{8,9},{9,8},{10,11... | collective-permute-start | bytes 1622024 | tf_op jit(solution)/shard_map/ppermute | solution.py:246
  21.6 1.2 %collective-permute-start.6 = (bf16[256,512]{1,0:T(8,128)(2,1)S(1)}, bf16[256,512]{1,0:T(8,128)(2,1)S(1)}, u32[]{:S(2)}, u32[]{:S(2)}) collective-permute-start(bf16[256,512]{1,0:T(8,128)(2,1)S(1)} %collective-permute-done.2.refs_7_.refs_4_.refs_3_), channel_id=1, source_target_pairs={{0,4},{6,2},{1,5},{7,3},{4,8},{10,6},{5,9},{11,7},{8,12},{14,10},{... | collective-permute-start | bytes 786440 | tf_op jit(solution)/shard_map/ppermute | solution.py:240
  22.7 1.3 %window.18 = (f32[512,512]{1,0:T(8,128)S(1)}, f32[512,512]{1,0:T(8,128)S(1)}) custom-call(bf16[528,512]{1,0:T(8,128)(2,1)S(1)} %get-tuple-element.92.row_ref.own_ref.refs_0_, f32[512,128]{1,0:T(8,128)S(1)} %get-tuple-element.96.refs_1_, f32[512,512]{1,0:T(8,128)S(1)} %get-tuple-element.98.refs_2_, ...), custom_call_target="tpu_custom_call", output_to_operand_aliasing={{0}: (2, {})} | custom-call | flops 4294967296 | tf_op jit(solution)/shard_map/window/pallas_call | solution.py:41
  24.6 2.8 %collective-permute-done.4.refs_8_.refs_4_ = bf16[256,512]{1,0:T(8,128)(2,1)S(1)} collective-permute-done((bf16[256,512]{1,0:T(8,128)(2,1)S(1)}, bf16[256,512]{1,0:T(8,128)(2,1)S(1)}, u32[]{:S(2)}, u32[]{:S(2)}) %collective-permute-start.4) | collective-permute-done | bytes 262176 | tf_op jit(solution)/shard_map/ppermute | solution.py:240
  27.4 1.8 %collective-permute-start.14 = (bf16[272,512]{1,0:T(8,128)(2,1)S(1)}, bf16[272,512]{1,0:T(8,128)(2,1)S(1)}, u32[]{:S(2)}, u32[]{:S(2)}) collective-permute-start(bf16[272,512]{1,0:T(8,128)(2,1)S(1)} %collective-permute-done.5.refs_7_.refs_3_), channel_id=1, source_target_pairs={{0,4},{6,2},{1,5},{7,3},{4,8},{10,6},{5,9},{11,7},{8,12},{14,10},{... | collective-permute-start | bytes 835592 | tf_op jit(solution)/shard_map/ppermute | solution.py:240
  29.2 1.3 %window.19 = (f32[512,512]{1,0:T(8,128)S(1)}, f32[512,512]{1,0:T(8,128)S(1)}) custom-call(bf16[528,512]{1,0:T(8,128)(2,1)S(1)} %get-tuple-element.92.row_ref.own_ref.refs_0_, f32[512,128]{1,0:T(8,128)S(1)} %get-tuple-element.96.refs_1_, f32[512,512]{1,0:T(8,128)S(1)} %get-tuple-element.108.refs_2_, ...), custom_call_target="tpu_custom_call", output_to_operand_aliasing={{0}: (2, {}), {1}: (6, {})} | custom-call | flops 4294967296 | tf_op jit(solution)/shard_map/window/pallas_call | solution.py:41
  30.6 2.7 %collective-permute-done.8.refs_6_.refs_7_ = bf16[272,512]{1,0:T(8,128)(2,1)S(1)} collective-permute-done((bf16[272,512]{1,0:T(8,128)(2,1)S(1)}, bf16[272,512]{1,0:T(8,128)(2,1)S(1)}, u32[]{:S(2)}, u32[]{:S(2)}) %collective-permute-start.8) | collective-permute-done | bytes 278560 | tf_op jit(solution)/shard_map/ppermute | solution.py:240
  33.3 1.6 %other_rows.1 = (f32[512,128]{1,0:T(8,128)S(1)}, f32[512,512]{1,0:T(8,128)S(1)}) custom-call(bf16[528,512]{1,0:T(8,128)(2,1)S(1)} %collective-permute-done.7.row_ref.refs_0_, bf16[528,512]{1,0:T(8,128)(2,1)S(1)} %get-tuple-element.92.row_ref.own_ref.refs_0_, bf16[272,512]{1,0:T(8,128)(2,1)S(1)} %collective-permute-done.refs_0_.first_ref.refs_3_, ...), custom_call_target="tpu_custom_call" | custom-call | flops 4294967296 | tf_op jit(solution)/shard_map/other_rows/pallas_call | solution.py:41
  34.9 1.2 %collective-permute-done.6.refs_7_.refs_8_ = bf16[256,512]{1,0:T(8,128)(2,1)S(1)} collective-permute-done((bf16[256,512]{1,0:T(8,128)(2,1)S(1)}, bf16[256,512]{1,0:T(8,128)(2,1)S(1)}, u32[]{:S(2)}, u32[]{:S(2)}) %collective-permute-start.6) | collective-permute-done | bytes 262176 | tf_op jit(solution)/shard_map/ppermute | solution.py:240
  37.6 1.3 %collective-permute-done.12.refs_7_.refs_8_ = bf16[256,512]{1,0:T(8,128)(2,1)S(1)} collective-permute-done((bf16[256,512]{1,0:T(8,128)(2,1)S(1)}, bf16[256,512]{1,0:T(8,128)(2,1)S(1)}, u32[]{:S(2)}, u32[]{:S(2)}) %collective-permute-start.12) | collective-permute-done | bytes 262176 | tf_op jit(solution)/shard_map/ppermute | solution.py:240
  39.1 2.8 %collective-permute-done.14.refs_6_.refs_7_ = bf16[272,512]{1,0:T(8,128)(2,1)S(1)} collective-permute-done((bf16[272,512]{1,0:T(8,128)(2,1)S(1)}, bf16[272,512]{1,0:T(8,128)(2,1)S(1)}, u32[]{:S(2)}, u32[]{:S(2)}) %collective-permute-start.14) | collective-permute-done | bytes 278560 | tf_op jit(solution)/shard_map/ppermute | solution.py:240
  43.4 1.5 %collective-permute-done.10.refs_6_.refs_7_ = bf16[272,512]{1,0:T(8,128)(2,1)S(1)} collective-permute-done((bf16[272,512]{1,0:T(8,128)(2,1)S(1)}, bf16[272,512]{1,0:T(8,128)(2,1)S(1)}, u32[]{:S(2)}, u32[]{:S(2)}) %collective-permute-start.10) | collective-permute-done | bytes 278560 | tf_op jit(solution)/shard_map/ppermute | solution.py:240
  44.9 1.3 %window.24 = (f32[512,512]{1,0:T(8,128)S(1)}, f32[512,512]{1,0:T(8,128)S(1)}) custom-call(bf16[528,512]{1,0:T(8,128)(2,1)S(1)} %collective-permute-done.7.row_ref.refs_0_, f32[512,128]{1,0:T(8,128)S(1)} %get-tuple-element.117.refs_1_, f32[512,512]{1,0:T(8,128)S(1)} %window.21.refs_2_, ...), custom_call_target="tpu_custom_call", output_to_operand_aliasing={{0}: (2, {}), {1}: (5, {})} | custom-call | tf_op jit(solution)/shard_map/window/pallas_call | solution.py:41
  46.2 1.5 %collective-permute-done.9.refs_7_.refs_8_ = bf16[256,512]{1,0:T(8,128)(2,1)S(1)} collective-permute-done((bf16[256,512]{1,0:T(8,128)(2,1)S(1)}, bf16[256,512]{1,0:T(8,128)(2,1)S(1)}, u32[]{:S(2)}, u32[]{:S(2)}) %collective-permute-start.9) | collective-permute-done | bytes 262176 | tf_op jit(solution)/shard_map/ppermute | solution.py:240
  47.7 1.3 %window.25 = (f32[512,512]{1,0:T(8,128)S(1)}, f32[512,512]{1,0:T(8,128)S(1)}) custom-call(bf16[528,512]{1,0:T(8,128)(2,1)S(1)} %collective-permute-done.7.row_ref.refs_0_, f32[512,128]{1,0:T(8,128)S(1)} %get-tuple-element.117.refs_1_, f32[512,512]{1,0:T(8,128)S(1)} %get-tuple-element.135.refs_2_, ...), custom_call_target="tpu_custom_call", output_to_operand_aliasing={{0}: (2, {}), {1}: (5, {})} | custom-call | tf_op jit(solution)/shard_map/window/pallas_call | solution.py:41
  49.0 1.3 %window.26 = (f32[512,512]{1,0:T(8,128)S(1)}, f32[512,512]{1,0:T(8,128)S(1)}) custom-call(bf16[528,512]{1,0:T(8,128)(2,1)S(1)} %collective-permute-done.7.row_ref.refs_0_, f32[512,128]{1,0:T(8,128)S(1)} %get-tuple-element.117.refs_1_, f32[512,512]{1,0:T(8,128)S(1)} %get-tuple-element.142.refs_2_, ...), custom_call_target="tpu_custom_call", output_to_operand_aliasing={{0}: (2, {}), {1}: (5, {})} | custom-call | tf_op jit(solution)/shard_map/window/pallas_call | solution.py:41
  50.5 3.0 %collective-permute-done.16.refs_3_.refs_4_ = bf16[272,512]{1,0:T(8,128)(2,1)S(1)} collective-permute-done((bf16[272,512]{1,0:T(8,128)(2,1)S(1)}, bf16[272,512]{1,0:T(8,128)(2,1)S(1)}, u32[]{:S(2)}, u32[]{:S(2)}) %collective-permute-start.16) | collective-permute-done | bytes 278560 | tf_op jit(solution)/shard_map/ppermute | solution.py:240
  56.5 2.8 %collective-permute-done.13.refs_6_.refs_4_ = bf16[256,512]{1,0:T(8,128)(2,1)S(1)} collective-permute-done((bf16[256,512]{1,0:T(8,128)(2,1)S(1)}, bf16[256,512]{1,0:T(8,128)(2,1)S(1)}, u32[]{:S(2)}, u32[]{:S(2)}) %collective-permute-start.13) | collective-permute-done | bytes 262176 | tf_op jit(solution)/shard_map/ppermute | solution.py:240
  60.1 2.3 %collective-permute-start.22 = (bf16[512,512]{1,0:T(8,128)(2,1)S(1)}, bf16[512,512]{1,0:T(8,128)(2,1)S(1)}, u32[]{:S(2)}, u32[]{:S(2)}) collective-permute-start(bf16[512,512]{1,0:T(8,128)(2,1)S(1)} %window.29), channel_id=1, source_target_pairs={{0,1},{1,0},{2,3},{3,2},{4,5},{5,4},{6,7},{7,6},{8,9},{9,8},{10,11... | collective-permute-start | bytes 1572872 | tf_op jit(solution)/shard_map/ppermute | solution.py:246
  62.4 1.3 %window.30 = (f32[512,512]{1,0:T(8,128)S(1)}, f32[512,512]{1,0:T(8,128)S(1)}) custom-call(bf16[528,512]{1,0:T(8,128)(2,1)S(1)} %get-tuple-element.92.row_ref.own_ref.refs_0_, f32[512,128]{1,0:T(8,128)S(1)} %get-tuple-element.96.refs_1_, f32[512,512]{1,0:T(8,128)S(1)} %get-tuple-element.155.refs_2_, ...), custom_call_target="tpu_custom_call", output_to_operand_aliasing={{0}: (2, {}), {1}: (6, {})} | custom-call | tf_op jit(solution)/shard_map/window/pallas_call | solution.py:41
  63.7 1.3 %window.31 = (f32[512,512]{1,0:T(8,128)S(1)}, f32[512,512]{1,0:T(8,128)S(1)}) custom-call(bf16[528,512]{1,0:T(8,128)(2,1)S(1)} %get-tuple-element.92.row_ref.own_ref.refs_0_, f32[512,128]{1,0:T(8,128)S(1)} %get-tuple-element.96.refs_1_, f32[512,512]{1,0:T(8,128)S(1)} %get-tuple-element.161.refs_2_, ...), custom_call_target="tpu_custom_call", output_to_operand_aliasing={{0}: (2, {}), {1}: (6, {})} | custom-call | tf_op jit(solution)/shard_map/window/pallas_call | solution.py:41
  65.1 1.3 %window.32 = (f32[512,512]{1,0:T(8,128)S(1)}, f32[512,512]{1,0:T(8,128)S(1)}) custom-call(bf16[528,512]{1,0:T(8,128)(2,1)S(1)} %get-tuple-element.92.row_ref.own_ref.refs_0_, f32[512,128]{1,0:T(8,128)S(1)} %get-tuple-element.96.refs_1_, f32[512,512]{1,0:T(8,128)S(1)} %get-tuple-element.167.refs_2_, ...), custom_call_target="tpu_custom_call", output_to_operand_aliasing={{0}: (2, {}), {1}: (6, {})} | custom-call | tf_op jit(solution)/shard_map/window/pallas_call | solution.py:41
  69.3 3.5 %collective-permute-done.22.refs_2_ = bf16[512,512]{1,0:T(8,128)(2,1)S(1)} collective-permute-done((bf16[512,512]{1,0:T(8,128)(2,1)S(1)}, bf16[512,512]{1,0:T(8,128)(2,1)S(1)}, u32[]{:S(2)}, u32[]{:S(2)}) %collective-permute-start.22) | collective-permute-done | bytes 524320 | tf_op jit(solution)/shard_map/ppermute | solution.py:246
  72.8 1.1 %finish.1 = f32[512,512]{1,0:T(8,128)} custom-call(f32[512,512]{1,0:T(8,128)S(1)} %window.35.here_ref, bf16[256,512]{1,0:T(8,128)(2,1)S(1)} %collective-permute-done.20.refs_0_, bf16[256,512]{1,0:T(8,128)(2,1)S(1)} %collective-permute-done.21.refs_1_, bf16[512,512]{1,0:T(8,128)(2,1)S(1)} %collective-permute-done.22.refs_2_), custom_call_target="tpu_custom_call" | custom-call | tf_op jit(solution)/shard_map/finish/pallas_call | solution.py:41
  (46 shorter events, 12.6 us)
Async XLA Ops:
  0.0 0.7 copy-start.3
  0.0 0.7 copy-start.2
  0.0 0.7 copy-start.1
  0.7 1.2 %copy-start = (f32[512,512]{1,0:T(8,128)S(1)}, f32[512,512]{1,0:T(8,128)}, u32[]{:S(2)}) copy-start(f32[512,512]{1,0:T(8,128)} %views_ref.1) | copy-start | bytes 3145732
  2.0 1.6 %collective-permute-start = (bf16[272,512]{1,0:T(8,128)(2,1)S(1)}, bf16[272,512]{1,0:T(8,128)(2,1)S(1)}, u32[]{:S(2)}, u32[]{:S(2)}) collective-permute-start(bf16[272,512]{1,0:T(8,128)(2,1)S(1)} %get-tuple-element.102), channel_id=1, source_target_pairs={{0,2},{2,0},{4,6},{6,4},{8,10},{10,8},{12,14},{14,12},{16,18},{18,... | collective-permute-start | bytes 835592 | tf_op jit(solution)/shard_map/ppermute | solution.py:243
  3.7 2.7 %collective-permute-start.1 = (bf16[256,512]{1,0:T(8,128)(2,1)S(1)}, bf16[256,512]{1,0:T(8,128)(2,1)S(1)}, u32[]{:S(2)}, u32[]{:S(2)}) collective-permute-start(bf16[256,512]{1,0:T(8,128)(2,1)S(1)} %get-tuple-element.101), channel_id=1, source_target_pairs={{0,2},{2,0},{4,6},{6,4},{8,10},{10,8},{12,14},{14,12},{16,18},{18,... | collective-permute-start | bytes 786440 | tf_op jit(solution)/shard_map/ppermute | solution.py:243
  3.8 15.1 %collective-permute-start.7 = (bf16[528,512]{1,0:T(8,128)(2,1)S(1)}, bf16[528,512]{1,0:T(8,128)(2,1)S(1)}, u32[]{:S(2)}, u32[]{:S(2)}) collective-permute-start(bf16[528,512]{1,0:T(8,128)(2,1)S(1)} %get-tuple-element.92.row_ref.own_ref.refs_0_), channel_id=1, source_target_pairs={{0,1},{1,0},{2,3},{3,2},{4,5},{5,4},{6,7},{7,6},{8,9},{9,8},{10,11... | collective-permute-start | bytes 1622024 | tf_op jit(solution)/shard_map/ppermute | solution.py:246
  6.1 14.5 %collective-permute-start.3 = (bf16[272,512]{1,0:T(8,128)(2,1)S(1)}, bf16[272,512]{1,0:T(8,128)(2,1)S(1)}, u32[]{:S(2)}, u32[]{:S(2)}) collective-permute-start(bf16[272,512]{1,0:T(8,128)(2,1)S(1)} %collective-permute-done.refs_0_.first_ref.refs_3_), channel_id=1, source_target_pairs={{0,4},{6,2},{1,5},{7,3},{4,8},{10,6},{5,9},{11,7},{8,12},{14,10},{... | collective-permute-start | bytes 835592 | tf_op jit(solution)/shard_map/ppermute | solution.py:240
  6.4 15.2 %collective-permute-start.2 = (bf16[256,512]{1,0:T(8,128)(2,1)S(1)}, bf16[256,512]{1,0:T(8,128)(2,1)S(1)}, u32[]{:S(2)}, u32[]{:S(2)}) collective-permute-start(bf16[256,512]{1,0:T(8,128)(2,1)S(1)} %collective-permute-done.1.refs_1_.refs_4_), channel_id=1, source_target_pairs={{0,4},{6,2},{1,5},{7,3},{4,8},{10,6},{5,9},{11,7},{8,12},{14,10},{... | collective-permute-start | bytes 786440 | tf_op jit(solution)/shard_map/ppermute | solution.py:240
  9.9 14.6 %collective-permute-start.5 = (bf16[272,512]{1,0:T(8,128)(2,1)S(1)}, bf16[272,512]{1,0:T(8,128)(2,1)S(1)}, u32[]{:S(2)}, u32[]{:S(2)}) collective-permute-start(bf16[272,512]{1,0:T(8,128)(2,1)S(1)} %get-tuple-element.102), channel_id=1, source_target_pairs={{0,4},{6,2},{1,5},{7,3},{4,8},{10,6},{5,9},{11,7},{8,12},{14,10},{... | collective-permute-start | bytes 835592 | tf_op jit(solution)/shard_map/ppermute | solution.py:240
  11.9 15.4 %collective-permute-start.4 = (bf16[256,512]{1,0:T(8,128)(2,1)S(1)}, bf16[256,512]{1,0:T(8,128)(2,1)S(1)}, u32[]{:S(2)}, u32[]{:S(2)}) collective-permute-start(bf16[256,512]{1,0:T(8,128)(2,1)S(1)} %get-tuple-element.101), channel_id=1, source_target_pairs={{0,4},{6,2},{1,5},{7,3},{4,8},{10,6},{5,9},{11,7},{8,12},{14,10},{... | collective-permute-start | bytes 786440 | tf_op jit(solution)/shard_map/ppermute | solution.py:240
  18.9 20.1 %collective-permute-start.11 = (bf16[528,512]{1,0:T(8,128)(2,1)S(1)}, bf16[528,512]{1,0:T(8,128)(2,1)S(1)}, u32[]{:S(2)}, u32[]{:S(2)}) collective-permute-start(bf16[528,512]{1,0:T(8,128)(2,1)S(1)} %get-tuple-element.122), channel_id=1, source_target_pairs={{0,1},{1,0},{2,3},{3,2},{4,5},{5,4},{6,7},{7,6},{8,9},{9,8},{10,11... | collective-permute-start | bytes 1622024 | tf_op jit(solution)/shard_map/ppermute | solution.py:246
  20.6 12.7 %collective-permute-start.8 = (bf16[272,512]{1,0:T(8,128)(2,1)S(1)}, bf16[272,512]{1,0:T(8,128)(2,1)S(1)}, u32[]{:S(2)}, u32[]{:S(2)}) collective-permute-start(bf16[272,512]{1,0:T(8,128)(2,1)S(1)} %collective-permute-done.3.refs_6_.refs_3_.refs_2_), channel_id=1, source_target_pairs={{0,4},{6,2},{1,5},{7,3},{4,8},{10,6},{5,9},{11,7},{8,12},{14,10},{... | collective-permute-start | bytes 835592 | tf_op jit(solution)/shard_map/ppermute | solution.py:240
  21.6 14.5 %collective-permute-start.6 = (bf16[256,512]{1,0:T(8,128)(2,1)S(1)}, bf16[256,512]{1,0:T(8,128)(2,1)S(1)}, u32[]{:S(2)}, u32[]{:S(2)}) collective-permute-start(bf16[256,512]{1,0:T(8,128)(2,1)S(1)} %collective-permute-done.2.refs_7_.refs_4_.refs_3_), channel_id=1, source_target_pairs={{0,4},{6,2},{1,5},{7,3},{4,8},{10,6},{5,9},{11,7},{8,12},{14,10},{... | collective-permute-start | bytes 786440 | tf_op jit(solution)/shard_map/ppermute | solution.py:240
  27.4 11.6 %collective-permute-start.12 = (bf16[256,512]{1,0:T(8,128)(2,1)S(1)}, bf16[256,512]{1,0:T(8,128)(2,1)S(1)}, u32[]{:S(2)}, u32[]{:S(2)}) collective-permute-start(bf16[256,512]{1,0:T(8,128)(2,1)S(1)} %collective-permute-done.4.refs_8_.refs_4_), channel_id=1, source_target_pairs={{0,4},{6,2},{1,5},{7,3},{4,8},{10,6},{5,9},{11,7},{8,12},{14,10},{... | collective-permute-start | bytes 786440 | tf_op jit(solution)/shard_map/ppermute | solution.py:240
  27.4 14.5 %collective-permute-start.14 = (bf16[272,512]{1,0:T(8,128)(2,1)S(1)}, bf16[272,512]{1,0:T(8,128)(2,1)S(1)}, u32[]{:S(2)}, u32[]{:S(2)}) collective-permute-start(bf16[272,512]{1,0:T(8,128)(2,1)S(1)} %collective-permute-done.5.refs_7_.refs_3_), channel_id=1, source_target_pairs={{0,4},{6,2},{1,5},{7,3},{4,8},{10,6},{5,9},{11,7},{8,12},{14,10},{... | collective-permute-start | bytes 835592 | tf_op jit(solution)/shard_map/ppermute | solution.py:240
  33.3 11.6 %collective-permute-start.10 = (bf16[272,512]{1,0:T(8,128)(2,1)S(1)}, bf16[272,512]{1,0:T(8,128)(2,1)S(1)}, u32[]{:S(2)}, u32[]{:S(2)}) collective-permute-start(bf16[272,512]{1,0:T(8,128)(2,1)S(1)} %collective-permute-done.8.refs_6_.refs_7_), channel_id=1, source_target_pairs={{0,4},{6,2},{1,5},{7,3},{4,8},{10,6},{5,9},{11,7},{8,12},{14,10},{... | collective-permute-start | bytes 835592 | tf_op jit(solution)/shard_map/ppermute | solution.py:240
  36.1 11.6 %collective-permute-start.9 = (bf16[256,512]{1,0:T(8,128)(2,1)S(1)}, bf16[256,512]{1,0:T(8,128)(2,1)S(1)}, u32[]{:S(2)}, u32[]{:S(2)}) collective-permute-start(bf16[256,512]{1,0:T(8,128)(2,1)S(1)} %collective-permute-done.6.refs_7_.refs_8_), channel_id=1, source_target_pairs={{0,4},{6,2},{1,5},{7,3},{4,8},{10,6},{5,9},{11,7},{8,12},{14,10},{... | collective-permute-start | bytes 786440 | tf_op jit(solution)/shard_map/ppermute | solution.py:240
  38.9 11.6 %collective-permute-start.15 = (bf16[256,512]{1,0:T(8,128)(2,1)S(1)}, bf16[256,512]{1,0:T(8,128)(2,1)S(1)}, u32[]{:S(2)}, u32[]{:S(2)}) collective-permute-start(bf16[256,512]{1,0:T(8,128)(2,1)S(1)} %collective-permute-done.12.refs_7_.refs_8_), channel_id=1, source_target_pairs={{0,4},{6,2},{1,5},{7,3},{4,8},{10,6},{5,9},{11,7},{8,12},{14,10},{... | collective-permute-start | bytes 786440 | tf_op jit(solution)/shard_map/ppermute | solution.py:240
  41.9 11.6 %collective-permute-start.16 = (bf16[272,512]{1,0:T(8,128)(2,1)S(1)}, bf16[272,512]{1,0:T(8,128)(2,1)S(1)}, u32[]{:S(2)}, u32[]{:S(2)}) collective-permute-start(bf16[272,512]{1,0:T(8,128)(2,1)S(1)} %collective-permute-done.14.refs_6_.refs_7_), channel_id=1, source_target_pairs={{0,4},{6,2},{1,5},{7,3},{4,8},{10,6},{5,9},{11,7},{8,12},{14,10},{... | collective-permute-start | bytes 835592 | tf_op jit(solution)/shard_map/ppermute | solution.py:240
  44.9 11.6 %collective-permute-start.19 = (bf16[272,512]{1,0:T(8,128)(2,1)S(1)}, bf16[272,512]{1,0:T(8,128)(2,1)S(1)}, u32[]{:S(2)}, u32[]{:S(2)}) collective-permute-start(bf16[272,512]{1,0:T(8,128)(2,1)S(1)} %collective-permute-done.10.refs_6_.refs_7_), channel_id=1, source_target_pairs={{0,4},{6,2},{1,5},{7,3},{4,8},{10,6},{5,9},{11,7},{8,12},{14,10},{... | collective-permute-start | bytes 835592 | tf_op jit(solution)/shard_map/ppermute | solution.py:240
  47.7 11.6 %collective-permute-start.13 = (bf16[256,512]{1,0:T(8,128)(2,1)S(1)}, bf16[256,512]{1,0:T(8,128)(2,1)S(1)}, u32[]{:S(2)}, u32[]{:S(2)}) collective-permute-start(bf16[256,512]{1,0:T(8,128)(2,1)S(1)} %collective-permute-done.9.refs_7_.refs_8_), channel_id=1, source_target_pairs={{0,4},{6,2},{1,5},{7,3},{4,8},{10,6},{5,9},{11,7},{8,12},{14,10},{... | collective-permute-start | bytes 786440 | tf_op jit(solution)/shard_map/ppermute | solution.py:240
  54.3 5.0 %collective-permute-start.17 = (bf16[256,512]{1,0:T(8,128)(2,1)S(1)}, bf16[256,512]{1,0:T(8,128)(2,1)S(1)}, u32[]{:S(2)}, u32[]{:S(2)}) collective-permute-start(bf16[256,512]{1,0:T(8,128)(2,1)S(1)} %get-tuple-element.151), channel_id=1, source_target_pairs={{0,2},{2,0},{4,6},{6,4},{8,10},{10,8},{12,14},{14,12},{16,18},{18,... | collective-permute-start | bytes 786440 | tf_op jit(solution)/shard_map/ppermute | solution.py:243
  55.3 4.0 %collective-permute-start.18 = (bf16[256,512]{1,0:T(8,128)(2,1)S(1)}, bf16[256,512]{1,0:T(8,128)(2,1)S(1)}, u32[]{:S(2)}, u32[]{:S(2)}) collective-permute-start(bf16[256,512]{1,0:T(8,128)(2,1)S(1)} %get-tuple-element.153), channel_id=1, source_target_pairs={{0,2},{2,0},{4,6},{6,4},{8,10},{10,8},{12,14},{14,12},{16,18},{18,... | collective-permute-start | bytes 786440 | tf_op jit(solution)/shard_map/ppermute | solution.py:243
  60.1 12.7 %collective-permute-start.22 = (bf16[512,512]{1,0:T(8,128)(2,1)S(1)}, bf16[512,512]{1,0:T(8,128)(2,1)S(1)}, u32[]{:S(2)}, u32[]{:S(2)}) collective-permute-start(bf16[512,512]{1,0:T(8,128)(2,1)S(1)} %window.29), channel_id=1, source_target_pairs={{0,1},{1,0},{2,3},{3,2},{4,5},{5,4},{6,7},{7,6},{8,9},{9,8},{10,11... | collective-permute-start | bytes 1572872 | tf_op jit(solution)/shard_map/ppermute | solution.py:246
  67.2 2.1 %collective-permute-start.20 = (bf16[256,512]{1,0:T(8,128)(2,1)S(1)}, bf16[256,512]{1,0:T(8,128)(2,1)S(1)}, u32[]{:S(2)}, u32[]{:S(2)}) collective-permute-start(bf16[256,512]{1,0:T(8,128)(2,1)S(1)} %get-tuple-element.176), channel_id=1, source_target_pairs={{0,2},{2,0},{4,6},{6,4},{8,10},{10,8},{12,14},{14,12},{16,18},{18,... | collective-permute-start | bytes 786440 | tf_op jit(solution)/shard_map/ppermute | solution.py:243
  67.3 2.0 %collective-permute-start.21 = (bf16[256,512]{1,0:T(8,128)(2,1)S(1)}, bf16[256,512]{1,0:T(8,128)(2,1)S(1)}, u32[]{:S(2)}, u32[]{:S(2)}) collective-permute-start(bf16[256,512]{1,0:T(8,128)(2,1)S(1)} %get-tuple-element.178), channel_id=1, source_target_pairs={{0,2},{2,0},{4,6},{6,4},{8,10},{10,8},{12,14},{14,12},{16,18},{18,... | collective-permute-start | bytes 786440 | tf_op jit(solution)/shard_map/ppermute | solution.py:243

commit v6 on v5

--- a/solution.py
+++ b/solution.py
@@ -22,10 +22,10 @@
 PLAN = {
     2: [("core1", ("own", "core"))],
     4: [("own1", ("own", "core"))],
-    6: [("core1", ("other",)), ("own1", ("other",))],
-    8: [("core1", ("far",)), ("own1", ("far",))],
-    9: [("core2", ("other", "far"))],
-    10: [("own2", ("other", "far")), ("core3", ("other", "far"))],
+    6: [("core1", ("other",)), ("own1", ("other",)), ("core2", ("other",))],
+    8: [("core1", ("far",)), ("own1", ("far",)), ("core2", ("far",))],
+    9: [("own2", ("other", "far"))],
+    10: [("core3", ("other", "far"))],
     12: [("own3", ("far",)), ("own3", ("other",))],
 }
 FAR_AT = 8
@@ -272,7 +272,7 @@
                 sums = window_terms(group, columns[name], jnp.bfloat16, 2)
                 totals[rows[0]] = [sums]
             else:
-                sums = window_terms(group, columns[name], weight=16 if arrivals < 9 else 0)
+                sums = window_terms(group, columns[name], weight=8 if arrivals < 10 else 0)
                 totals.update({r: [[value]] for r, value in zip(rows, sums, strict=True)})
             token = sums[0]
         return token

time: 74.1 us -> 73.7 us (level)
  starting transfers between devices: 19 us -> 18.2 us
    ppermute x6, starting transfers between devices: 2.2 us -> 1.41 us  [core_swap(): return lax.ppermute(value, 'dp', cores)]
    pallas_call x24 -> x25, Pallas kernels: 22.7 us -> 22.9 us  [call(): pl.pallas_call(kernel, out_shape=[jax.ShapeDtypeStruct(shape, dtype) for...]
where the time goes in v6:
time: 73.7 us; the launch traced here: 73.6 us
  waiting for transfers between devices  30.4 us (41%)
  Pallas kernels  22.9 us (31%)
  starting transfers between devices  18.2 us (25%)
  local copies, waits for them, and re-layouts  1.93 us (3%)
    pallas_call x25, Pallas kernels, call(): pl.pallas_call(kernel, out_shape=[jax.ShapeDtypeStruct(shape, dtype) for...  22.9 us
    ppermute x14, waiting for transfers between devices, chip_next(): return lax.ppermute(value, ('dp', 'sub'), onward)  21.8 us
    ppermute x14, starting transfers between devices, chip_next(): return lax.ppermute(value, ('dp', 'sub'), onward)  10.4 us
    ppermute x3, waiting for transfers between devices, sub_swap(): return lax.ppermute(value, 'sub', [(0, 1), (1, 0)])  7.04 us
    ppermute x3, starting transfers between devices, sub_swap(): return lax.ppermute(value, 'sub', [(0, 1), (1, 0)])  6.33 us
    unnamed x8, local copies, waits for them, and re-layouts  1.93 us
    ppermute x6, waiting for transfers between devices, core_swap(): return lax.ppermute(value, 'dp', cores)  1.56 us
  transfers between devices with their start and end apart: 23, of which 16 were waited for; matrix products, arithmetic and copies ran while one was open for 0% of the time, Pallas kernels for 28%

profile of v6, /device:TPU:2, one launch (start us, length us, event | category | flops | bytes accessed | tf_op | source)
XLA Modules:
  0.0 73.6 jit_solution(12538301483599484885)
XLA Ops:
  0.7 1.2 %copy-done = f32[512,512]{1,0:T(8,128)S(1)} copy-done((f32[512,512]{1,0:T(8,128)S(1)}, f32[512,512]{1,0:T(8,128)}, u32[]{:S(2)}) %copy-start) | copy-done | bytes 1048600
  2.1 1.5 %collective-permute-done.refs_0_.first_ref.refs_3_ = bf16[272,512]{1,0:T(8,128)(2,1)S(1)} collective-permute-done((bf16[272,512]{1,0:T(8,128)(2,1)S(1)}, bf16[272,512]{1,0:T(8,128)(2,1)S(1)}, u32[]{:S(2)}, u32[]{:S(2)}) %collective-permute-start) | collective-permute-done | bytes 278560 | tf_op jit(solution)/shard_map/ppermute | solution.py:243
  3.8 2.3 %collective-permute-start.7 = (bf16[528,512]{1,0:T(8,128)(2,1)S(1)}, bf16[528,512]{1,0:T(8,128)(2,1)S(1)}, u32[]{:S(2)}, u32[]{:S(2)}) collective-permute-start(bf16[528,512]{1,0:T(8,128)(2,1)S(1)} %get-tuple-element.90.row_ref.own_ref.refs_0_), channel_id=1, source_target_pairs={{0,1},{1,0},{2,3},{3,2},{4,5},{5,4},{6,7},{7,6},{8,9},{9,8},{10,11... | collective-permute-start | bytes 1622024 | tf_op jit(solution)/shard_map/ppermute | solution.py:246
  6.3 1.9 %collective-permute-start.2 = (bf16[256,512]{1,0:T(8,128)(2,1)S(1)}, bf16[256,512]{1,0:T(8,128)(2,1)S(1)}, u32[]{:S(2)}, u32[]{:S(2)}) collective-permute-start(bf16[256,512]{1,0:T(8,128)(2,1)S(1)} %collective-permute-done.1.refs_1_.refs_4_), channel_id=1, source_target_pairs={{0,4},{6,2},{1,5},{7,3},{4,8},{10,6},{5,9},{11,7},{8,12},{14,10},{... | collective-permute-start | bytes 786440 | tf_op jit(solution)/shard_map/ppermute | solution.py:240
  8.2 1.5 %own_rows.1 = (f32[512,128]{1,0:T(8,128)S(1)}, f32[512,512]{1,0:T(8,128)S(1)}, bf16[528,512]{1,0:T(8,128)(2,1)S(1)}) custom-call(bf16[528,512]{1,0:T(8,128)(2,1)S(1)} %get-tuple-element.90.row_ref.own_ref.refs_0_, bf16[528,512]{1,0:T(8,128)(2,1)S(1)} %get-tuple-element.90.row_ref.own_ref.refs_0_, ...), custom_call_target="tpu_custom_call" | custom-call | flops 4294967296 | tf_op jit(solution)/shard_map/own_rows/pallas_call | solution.py:41
  9.7 2.0 %collective-permute-start.5 = (bf16[272,512]{1,0:T(8,128)(2,1)S(1)}, bf16[272,512]{1,0:T(8,128)(2,1)S(1)}, u32[]{:S(2)}, u32[]{:S(2)}) collective-permute-start(bf16[272,512]{1,0:T(8,128)(2,1)S(1)} %get-tuple-element.100), channel_id=1, source_target_pairs={{0,4},{6,2},{1,5},{7,3},{4,8},{10,6},{5,9},{11,7},{8,12},{14,10},{... | collective-permute-start | bytes 835592 | tf_op jit(solution)/shard_map/ppermute | solution.py:240
  11.7 3.1 %collective-permute-start.4 = (bf16[256,512]{1,0:T(8,128)(2,1)S(1)}, bf16[256,512]{1,0:T(8,128)(2,1)S(1)}, u32[]{:S(2)}, u32[]{:S(2)}) collective-permute-start(bf16[256,512]{1,0:T(8,128)(2,1)S(1)} %get-tuple-element.99), channel_id=1, source_target_pairs={{0,4},{6,2},{1,5},{7,3},{4,8},{10,6},{5,9},{11,7},{8,12},{14,10},{... | collective-permute-start | bytes 786440 | tf_op jit(solution)/shard_map/ppermute | solution.py:240
  15.0 3.9 %collective-permute-done.7.row_ref.refs_0_ = bf16[528,512]{1,0:T(8,128)(2,1)S(1)} collective-permute-done((bf16[528,512]{1,0:T(8,128)(2,1)S(1)}, bf16[528,512]{1,0:T(8,128)(2,1)S(1)}, u32[]{:S(2)}, u32[]{:S(2)}) %collective-permute-start.7) | collective-permute-done | bytes 540704 | tf_op jit(solution)/shard_map/ppermute | solution.py:246
  18.9 1.7 %collective-permute-start.11 = (bf16[528,512]{1,0:T(8,128)(2,1)S(1)}, bf16[528,512]{1,0:T(8,128)(2,1)S(1)}, u32[]{:S(2)}, u32[]{:S(2)}) collective-permute-start(bf16[528,512]{1,0:T(8,128)(2,1)S(1)} %get-tuple-element.122), channel_id=1, source_target_pairs={{0,1},{1,0},{2,3},{3,2},{4,5},{5,4},{6,7},{7,6},{8,9},{9,8},{10,11... | collective-permute-start | bytes 1622024 | tf_op jit(solution)/shard_map/ppermute | solution.py:246
  21.6 1.2 %collective-permute-start.6 = (bf16[256,512]{1,0:T(8,128)(2,1)S(1)}, bf16[256,512]{1,0:T(8,128)(2,1)S(1)}, u32[]{:S(2)}, u32[]{:S(2)}) collective-permute-start(bf16[256,512]{1,0:T(8,128)(2,1)S(1)} %collective-permute-done.2.refs_7_.refs_4_.refs_3_), channel_id=1, source_target_pairs={{0,4},{6,2},{1,5},{7,3},{4,8},{10,6},{5,9},{11,7},{8,12},{14,10},{... | collective-permute-start | bytes 786440 | tf_op jit(solution)/shard_map/ppermute | solution.py:240
  22.7 1.3 %window.19 = (f32[512,512]{1,0:T(8,128)S(1)}, f32[512,512]{1,0:T(8,128)S(1)}) custom-call(bf16[528,512]{1,0:T(8,128)(2,1)S(1)} %get-tuple-element.90.row_ref.own_ref.refs_0_, f32[512,128]{1,0:T(8,128)S(1)} %get-tuple-element.94.refs_1_, f32[512,512]{1,0:T(8,128)S(1)} %get-tuple-element.96.refs_2_, ...), custom_call_target="tpu_custom_call", output_to_operand_aliasing={{0}: (2, {})} | custom-call | flops 2147483648 | tf_op jit(solution)/shard_map/window/pallas_call | solution.py:41
  24.6 2.8 %collective-permute-done.4.refs_8_.refs_4_ = bf16[256,512]{1,0:T(8,128)(2,1)S(1)} collective-permute-done((bf16[256,512]{1,0:T(8,128)(2,1)S(1)}, bf16[256,512]{1,0:T(8,128)(2,1)S(1)}, u32[]{:S(2)}, u32[]{:S(2)}) %collective-permute-start.4) | collective-permute-done | bytes 262176 | tf_op jit(solution)/shard_map/ppermute | solution.py:240
  27.4 1.8 %collective-permute-start.13 = (bf16[272,512]{1,0:T(8,128)(2,1)S(1)}, bf16[272,512]{1,0:T(8,128)(2,1)S(1)}, u32[]{:S(2)}, u32[]{:S(2)}) collective-permute-start(bf16[272,512]{1,0:T(8,128)(2,1)S(1)} %collective-permute-done.5.refs_7_.refs_3_), channel_id=1, source_target_pairs={{0,4},{6,2},{1,5},{7,3},{4,8},{10,6},{5,9},{11,7},{8,12},{14,10},{... | collective-permute-start | bytes 835592 | tf_op jit(solution)/shard_map/ppermute | solution.py:240
  29.2 1.3 %window.20 = (f32[512,512]{1,0:T(8,128)S(1)}, f32[512,512]{1,0:T(8,128)S(1)}) custom-call(bf16[528,512]{1,0:T(8,128)(2,1)S(1)} %get-tuple-element.90.row_ref.own_ref.refs_0_, f32[512,128]{1,0:T(8,128)S(1)} %get-tuple-element.94.refs_1_, f32[512,512]{1,0:T(8,128)S(1)} %get-tuple-element.106.refs_2_, ...), custom_call_target="tpu_custom_call", output_to_operand_aliasing={{0}: (2, {}), {1}: (6, {})} | custom-call | flops 2147483648 | tf_op jit(solution)/shard_map/window/pallas_call | solution.py:41
  30.6 2.7 %collective-permute-done.8.refs_3_.refs_7_ = bf16[272,512]{1,0:T(8,128)(2,1)S(1)} collective-permute-done((bf16[272,512]{1,0:T(8,128)(2,1)S(1)}, bf16[272,512]{1,0:T(8,128)(2,1)S(1)}, u32[]{:S(2)}, u32[]{:S(2)}) %collective-permute-start.8) | collective-permute-done | bytes 278560 | tf_op jit(solution)/shard_map/ppermute | solution.py:240
  33.3 1.6 %other_rows.1 = (f32[512,128]{1,0:T(8,128)S(1)}, f32[512,512]{1,0:T(8,128)S(1)}) custom-call(bf16[528,512]{1,0:T(8,128)(2,1)S(1)} %collective-permute-done.7.row_ref.refs_0_, bf16[528,512]{1,0:T(8,128)(2,1)S(1)} %get-tuple-element.90.row_ref.own_ref.refs_0_, bf16[272,512]{1,0:T(8,128)(2,1)S(1)} %collective-permute-done.refs_0_.first_ref.refs_3_, ...), custom_call_target="tpu_custom_call" | custom-call | flops 4294967296 | tf_op jit(solution)/shard_map/other_rows/pallas_call | solution.py:41
  34.9 1.2 %collective-permute-done.6.refs_4_.refs_8_ = bf16[256,512]{1,0:T(8,128)(2,1)S(1)} collective-permute-done((bf16[256,512]{1,0:T(8,128)(2,1)S(1)}, bf16[256,512]{1,0:T(8,128)(2,1)S(1)}, u32[]{:S(2)}, u32[]{:S(2)}) %collective-permute-start.6) | collective-permute-done | bytes 262176 | tf_op jit(solution)/shard_map/ppermute | solution.py:240
  40.6 1.3 %collective-permute-done.13.refs_6_.refs_7_ = bf16[272,512]{1,0:T(8,128)(2,1)S(1)} collective-permute-done((bf16[272,512]{1,0:T(8,128)(2,1)S(1)}, bf16[272,512]{1,0:T(8,128)(2,1)S(1)}, u32[]{:S(2)}, u32[]{:S(2)}) %collective-permute-start.13) | collective-permute-done | bytes 278560 | tf_op jit(solution)/shard_map/ppermute | solution.py:240
  42.7 2.2 %collective-permute-done.10.refs_6_.refs_7_ = bf16[272,512]{1,0:T(8,128)(2,1)S(1)} collective-permute-done((bf16[272,512]{1,0:T(8,128)(2,1)S(1)}, bf16[272,512]{1,0:T(8,128)(2,1)S(1)}, u32[]{:S(2)}, u32[]{:S(2)}) %collective-permute-start.10) | collective-permute-done | bytes 278560 | tf_op jit(solution)/shard_map/ppermute | solution.py:240
  44.9 1.3 %window.27 = (f32[512,512]{1,0:T(8,128)S(1)}, f32[512,512]{1,0:T(8,128)S(1)}) custom-call(bf16[528,512]{1,0:T(8,128)(2,1)S(1)} %collective-permute-done.7.row_ref.refs_0_, f32[512,128]{1,0:T(8,128)S(1)} %get-tuple-element.115.refs_1_, f32[512,512]{1,0:T(8,128)S(1)} %window.23.refs_2_, ...), custom_call_target="tpu_custom_call", output_to_operand_aliasing={{0}: (2, {}), {1}: (5, {})} | custom-call | flops 2147483648 | tf_op jit(solution)/shard_map/window/pallas_call | solution.py:41
  46.2 1.5 %collective-permute-done.9.refs_7_.refs_8_ = bf16[256,512]{1,0:T(8,128)(2,1)S(1)} collective-permute-done((bf16[256,512]{1,0:T(8,128)(2,1)S(1)}, bf16[256,512]{1,0:T(8,128)(2,1)S(1)}, u32[]{:S(2)}, u32[]{:S(2)}) %collective-permute-start.9) | collective-permute-done | bytes 262176 | tf_op jit(solution)/shard_map/ppermute | solution.py:240
  47.7 1.3 %window.28 = (f32[512,512]{1,0:T(8,128)S(1)}, f32[512,512]{1,0:T(8,128)S(1)}) custom-call(bf16[528,512]{1,0:T(8,128)(2,1)S(1)} %collective-permute-done.7.row_ref.refs_0_, f32[512,128]{1,0:T(8,128)S(1)} %get-tuple-element.115.refs_1_, f32[512,512]{1,0:T(8,128)S(1)} %get-tuple-element.138.refs_2_, ...), custom_call_target="tpu_custom_call", output_to_operand_aliasing={{0}: (2, {}), {1}: (5, {})} | custom-call | tf_op jit(solution)/shard_map/window/pallas_call | solution.py:41
  49.0 1.5 %collective-permute-done.15.refs_4_.refs_5_ = bf16[256,512]{1,0:T(8,128)(2,1)S(1)} collective-permute-done((bf16[256,512]{1,0:T(8,128)(2,1)S(1)}, bf16[256,512]{1,0:T(8,128)(2,1)S(1)}, u32[]{:S(2)}, u32[]{:S(2)}) %collective-permute-start.15) | collective-permute-done | bytes 262176 | tf_op jit(solution)/shard_map/ppermute | solution.py:240
  50.5 3.0 %collective-permute-done.16.refs_3_.refs_4_ = bf16[272,512]{1,0:T(8,128)(2,1)S(1)} collective-permute-done((bf16[272,512]{1,0:T(8,128)(2,1)S(1)}, bf16[272,512]{1,0:T(8,128)(2,1)S(1)}, u32[]{:S(2)}, u32[]{:S(2)}) %collective-permute-start.16) | collective-permute-done | bytes 278560 | tf_op jit(solution)/shard_map/ppermute | solution.py:240
  55.6 0.9 %collective-permute-done.19.refs_5_.refs_3_ = bf16[272,512]{1,0:T(8,128)(2,1)S(1)} collective-permute-done((bf16[272,512]{1,0:T(8,128)(2,1)S(1)}, bf16[272,512]{1,0:T(8,128)(2,1)S(1)}, u32[]{:S(2)}, u32[]{:S(2)}) %collective-permute-start.19) | collective-permute-done | bytes 278560 | tf_op jit(solution)/shard_map/ppermute | solution.py:240
  56.5 2.8 %collective-permute-done.14.refs_6_.refs_4_ = bf16[256,512]{1,0:T(8,128)(2,1)S(1)} collective-permute-done((bf16[256,512]{1,0:T(8,128)(2,1)S(1)}, bf16[256,512]{1,0:T(8,128)(2,1)S(1)}, u32[]{:S(2)}, u32[]{:S(2)}) %collective-permute-start.14) | collective-permute-done | bytes 262176 | tf_op jit(solution)/shard_map/ppermute | solution.py:240
  60.1 2.3 %collective-permute-start.22 = (bf16[512,512]{1,0:T(8,128)(2,1)S(1)}, bf16[512,512]{1,0:T(8,128)(2,1)S(1)}, u32[]{:S(2)}, u32[]{:S(2)}) collective-permute-start(bf16[512,512]{1,0:T(8,128)(2,1)S(1)} %window.31), channel_id=1, source_target_pairs={{0,1},{1,0},{2,3},{3,2},{4,5},{5,4},{6,7},{7,6},{8,9},{9,8},{10,11... | collective-permute-start | bytes 1572872 | tf_op jit(solution)/shard_map/ppermute | solution.py:246
  62.4 1.3 %window.32 = (f32[512,512]{1,0:T(8,128)S(1)}, f32[512,512]{1,0:T(8,128)S(1)}) custom-call(bf16[528,512]{1,0:T(8,128)(2,1)S(1)} %get-tuple-element.90.row_ref.own_ref.refs_0_, f32[512,128]{1,0:T(8,128)S(1)} %get-tuple-element.94.refs_1_, f32[512,512]{1,0:T(8,128)S(1)} %get-tuple-element.151.refs_2_, ...), custom_call_target="tpu_custom_call", output_to_operand_aliasing={{0}: (2, {}), {1}: (6, {})} | custom-call | tf_op jit(solution)/shard_map/window/pallas_call | solution.py:41
  63.7 1.3 %window.33 = (f32[512,512]{1,0:T(8,128)S(1)}, f32[512,512]{1,0:T(8,128)S(1)}) custom-call(bf16[528,512]{1,0:T(8,128)(2,1)S(1)} %get-tuple-element.90.row_ref.own_ref.refs_0_, f32[512,128]{1,0:T(8,128)S(1)} %get-tuple-element.94.refs_1_, f32[512,512]{1,0:T(8,128)S(1)} %get-tuple-element.157.refs_2_, ...), custom_call_target="tpu_custom_call", output_to_operand_aliasing={{0}: (2, {}), {1}: (6, {})} | custom-call | tf_op jit(solution)/shard_map/window/pallas_call | solution.py:41
  65.1 1.3 %window.34 = (f32[512,512]{1,0:T(8,128)S(1)}, f32[512,512]{1,0:T(8,128)S(1)}) custom-call(bf16[528,512]{1,0:T(8,128)(2,1)S(1)} %get-tuple-element.90.row_ref.own_ref.refs_0_, f32[512,128]{1,0:T(8,128)S(1)} %get-tuple-element.94.refs_1_, f32[512,512]{1,0:T(8,128)S(1)} %get-tuple-element.163.refs_2_, ...), custom_call_target="tpu_custom_call", output_to_operand_aliasing={{0}: (2, {}), {1}: (6, {})} | custom-call | tf_op jit(solution)/shard_map/window/pallas_call | solution.py:41
  69.3 3.1 %collective-permute-done.22.refs_2_ = bf16[512,512]{1,0:T(8,128)(2,1)S(1)} collective-permute-done((bf16[512,512]{1,0:T(8,128)(2,1)S(1)}, bf16[512,512]{1,0:T(8,128)(2,1)S(1)}, u32[]{:S(2)}, u32[]{:S(2)}) %collective-permute-start.22) | collective-permute-done | bytes 524320 | tf_op jit(solution)/shard_map/ppermute | solution.py:246
  72.4 1.1 %finish.1 = f32[512,512]{1,0:T(8,128)} custom-call(f32[512,512]{1,0:T(8,128)S(1)} %window.37.here_ref, bf16[256,512]{1,0:T(8,128)(2,1)S(1)} %collective-permute-done.20.refs_0_, bf16[256,512]{1,0:T(8,128)(2,1)S(1)} %collective-permute-done.21.refs_1_, bf16[512,512]{1,0:T(8,128)(2,1)S(1)} %collective-permute-done.22.refs_2_), custom_call_target="tpu_custom_call" | custom-call | tf_op jit(solution)/shard_map/finish/pallas_call | solution.py:41
  (47 shorter events, 13.6 us)
Async XLA Ops:
  0.0 0.7 copy-start.3
  0.0 0.7 copy-start.2
  0.0 0.7 copy-start.1
  0.7 1.2 %copy-start = (f32[512,512]{1,0:T(8,128)S(1)}, f32[512,512]{1,0:T(8,128)}, u32[]{:S(2)}) copy-start(f32[512,512]{1,0:T(8,128)} %views_ref.1) | copy-start | bytes 3145732
  2.0 1.6 %collective-permute-start = (bf16[272,512]{1,0:T(8,128)(2,1)S(1)}, bf16[272,512]{1,0:T(8,128)(2,1)S(1)}, u32[]{:S(2)}, u32[]{:S(2)}) collective-permute-start(bf16[272,512]{1,0:T(8,128)(2,1)S(1)} %get-tuple-element.100), channel_id=1, source_target_pairs={{0,2},{2,0},{4,6},{6,4},{8,10},{10,8},{12,14},{14,12},{16,18},{18,... | collective-permute-start | bytes 835592 | tf_op jit(solution)/shard_map/ppermute | solution.py:243
  3.7 2.6 %collective-permute-start.1 = (bf16[256,512]{1,0:T(8,128)(2,1)S(1)}, bf16[256,512]{1,0:T(8,128)(2,1)S(1)}, u32[]{:S(2)}, u32[]{:S(2)}) collective-permute-start(bf16[256,512]{1,0:T(8,128)(2,1)S(1)} %get-tuple-element.99), channel_id=1, source_target_pairs={{0,2},{2,0},{4,6},{6,4},{8,10},{10,8},{12,14},{14,12},{16,18},{18,... | collective-permute-start | bytes 786440 | tf_op jit(solution)/shard_map/ppermute | solution.py:243
  3.8 15.1 %collective-permute-start.7 = (bf16[528,512]{1,0:T(8,128)(2,1)S(1)}, bf16[528,512]{1,0:T(8,128)(2,1)S(1)}, u32[]{:S(2)}, u32[]{:S(2)}) collective-permute-start(bf16[528,512]{1,0:T(8,128)(2,1)S(1)} %get-tuple-element.90.row_ref.own_ref.refs_0_), channel_id=1, source_target_pairs={{0,1},{1,0},{2,3},{3,2},{4,5},{5,4},{6,7},{7,6},{8,9},{9,8},{10,11... | collective-permute-start | bytes 1622024 | tf_op jit(solution)/shard_map/ppermute | solution.py:246
  6.1 14.5 %collective-permute-start.3 = (bf16[272,512]{1,0:T(8,128)(2,1)S(1)}, bf16[272,512]{1,0:T(8,128)(2,1)S(1)}, u32[]{:S(2)}, u32[]{:S(2)}) collective-permute-start(bf16[272,512]{1,0:T(8,128)(2,1)S(1)} %collective-permute-done.refs_0_.first_ref.refs_3_), channel_id=1, source_target_pairs={{0,4},{6,2},{1,5},{7,3},{4,8},{10,6},{5,9},{11,7},{8,12},{14,10},{... | collective-permute-start | bytes 835592 | tf_op jit(solution)/shard_map/ppermute | solution.py:240
  6.3 15.3 %collective-permute-start.2 = (bf16[256,512]{1,0:T(8,128)(2,1)S(1)}, bf16[256,512]{1,0:T(8,128)(2,1)S(1)}, u32[]{:S(2)}, u32[]{:S(2)}) collective-permute-start(bf16[256,512]{1,0:T(8,128)(2,1)S(1)} %collective-permute-done.1.refs_1_.refs_4_), channel_id=1, source_target_pairs={{0,4},{6,2},{1,5},{7,3},{4,8},{10,6},{5,9},{11,7},{8,12},{14,10},{... | collective-permute-start | bytes 786440 | tf_op jit(solution)/shard_map/ppermute | solution.py:240
  9.7 14.8 %collective-permute-start.5 = (bf16[272,512]{1,0:T(8,128)(2,1)S(1)}, bf16[272,512]{1,0:T(8,128)(2,1)S(1)}, u32[]{:S(2)}, u32[]{:S(2)}) collective-permute-start(bf16[272,512]{1,0:T(8,128)(2,1)S(1)} %get-tuple-element.100), channel_id=1, source_target_pairs={{0,4},{6,2},{1,5},{7,3},{4,8},{10,6},{5,9},{11,7},{8,12},{14,10},{... | collective-permute-start | bytes 835592 | tf_op jit(solution)/shard_map/ppermute | solution.py:240
  11.7 15.7 %collective-permute-start.4 = (bf16[256,512]{1,0:T(8,128)(2,1)S(1)}, bf16[256,512]{1,0:T(8,128)(2,1)S(1)}, u32[]{:S(2)}, u32[]{:S(2)}) collective-permute-start(bf16[256,512]{1,0:T(8,128)(2,1)S(1)} %get-tuple-element.99), channel_id=1, source_target_pairs={{0,4},{6,2},{1,5},{7,3},{4,8},{10,6},{5,9},{11,7},{8,12},{14,10},{... | collective-permute-start | bytes 786440 | tf_op jit(solution)/shard_map/ppermute | solution.py:240
  18.9 20.1 %collective-permute-start.11 = (bf16[528,512]{1,0:T(8,128)(2,1)S(1)}, bf16[528,512]{1,0:T(8,128)(2,1)S(1)}, u32[]{:S(2)}, u32[]{:S(2)}) collective-permute-start(bf16[528,512]{1,0:T(8,128)(2,1)S(1)} %get-tuple-element.122), channel_id=1, source_target_pairs={{0,1},{1,0},{2,3},{3,2},{4,5},{5,4},{6,7},{7,6},{8,9},{9,8},{10,11... | collective-permute-start | bytes 1622024 | tf_op jit(solution)/shard_map/ppermute | solution.py:246
  20.6 12.7 %collective-permute-start.8 = (bf16[272,512]{1,0:T(8,128)(2,1)S(1)}, bf16[272,512]{1,0:T(8,128)(2,1)S(1)}, u32[]{:S(2)}, u32[]{:S(2)}) collective-permute-start(bf16[272,512]{1,0:T(8,128)(2,1)S(1)} %collective-permute-done.3.refs_6_.refs_3_.refs_2_), channel_id=1, source_target_pairs={{0,4},{6,2},{1,5},{7,3},{4,8},{10,6},{5,9},{11,7},{8,12},{14,10},{... | collective-permute-start | bytes 835592 | tf_op jit(solution)/shard_map/ppermute | solution.py:240
  21.6 14.5 %collective-permute-start.6 = (bf16[256,512]{1,0:T(8,128)(2,1)S(1)}, bf16[256,512]{1,0:T(8,128)(2,1)S(1)}, u32[]{:S(2)}, u32[]{:S(2)}) collective-permute-start(bf16[256,512]{1,0:T(8,128)(2,1)S(1)} %collective-permute-done.2.refs_7_.refs_4_.refs_3_), channel_id=1, source_target_pairs={{0,4},{6,2},{1,5},{7,3},{4,8},{10,6},{5,9},{11,7},{8,12},{14,10},{... | collective-permute-start | bytes 786440 | tf_op jit(solution)/shard_map/ppermute | solution.py:240
  27.4 11.6 %collective-permute-start.12 = (bf16[256,512]{1,0:T(8,128)(2,1)S(1)}, bf16[256,512]{1,0:T(8,128)(2,1)S(1)}, u32[]{:S(2)}, u32[]{:S(2)}) collective-permute-start(bf16[256,512]{1,0:T(8,128)(2,1)S(1)} %collective-permute-done.4.refs_8_.refs_4_), channel_id=1, source_target_pairs={{0,4},{6,2},{1,5},{7,3},{4,8},{10,6},{5,9},{11,7},{8,12},{14,10},{... | collective-permute-start | bytes 786440 | tf_op jit(solution)/shard_map/ppermute | solution.py:240
  27.4 14.5 %collective-permute-start.13 = (bf16[272,512]{1,0:T(8,128)(2,1)S(1)}, bf16[272,512]{1,0:T(8,128)(2,1)S(1)}, u32[]{:S(2)}, u32[]{:S(2)}) collective-permute-start(bf16[272,512]{1,0:T(8,128)(2,1)S(1)} %collective-permute-done.5.refs_7_.refs_3_), channel_id=1, source_target_pairs={{0,4},{6,2},{1,5},{7,3},{4,8},{10,6},{5,9},{11,7},{8,12},{14,10},{... | collective-permute-start | bytes 835592 | tf_op jit(solution)/shard_map/ppermute | solution.py:240
  33.3 11.6 %collective-permute-start.10 = (bf16[272,512]{1,0:T(8,128)(2,1)S(1)}, bf16[272,512]{1,0:T(8,128)(2,1)S(1)}, u32[]{:S(2)}, u32[]{:S(2)}) collective-permute-start(bf16[272,512]{1,0:T(8,128)(2,1)S(1)} %collective-permute-done.8.refs_3_.refs_7_), channel_id=1, source_target_pairs={{0,4},{6,2},{1,5},{7,3},{4,8},{10,6},{5,9},{11,7},{8,12},{14,10},{... | collective-permute-start | bytes 835592 | tf_op jit(solution)/shard_map/ppermute | solution.py:240
  36.1 11.6 %collective-permute-start.9 = (bf16[256,512]{1,0:T(8,128)(2,1)S(1)}, bf16[256,512]{1,0:T(8,128)(2,1)S(1)}, u32[]{:S(2)}, u32[]{:S(2)}) collective-permute-start(bf16[256,512]{1,0:T(8,128)(2,1)S(1)} %collective-permute-done.6.refs_4_.refs_8_), channel_id=1, source_target_pairs={{0,4},{6,2},{1,5},{7,3},{4,8},{10,6},{5,9},{11,7},{8,12},{14,10},{... | collective-permute-start | bytes 786440 | tf_op jit(solution)/shard_map/ppermute | solution.py:240
  38.9 11.6 %collective-permute-start.15 = (bf16[256,512]{1,0:T(8,128)(2,1)S(1)}, bf16[256,512]{1,0:T(8,128)(2,1)S(1)}, u32[]{:S(2)}, u32[]{:S(2)}) collective-permute-start(bf16[256,512]{1,0:T(8,128)(2,1)S(1)} %collective-permute-done.12.refs_7_.refs_8_), channel_id=1, source_target_pairs={{0,4},{6,2},{1,5},{7,3},{4,8},{10,6},{5,9},{11,7},{8,12},{14,10},{... | collective-permute-start | bytes 786440 | tf_op jit(solution)/shard_map/ppermute | solution.py:240
  41.9 11.6 %collective-permute-start.16 = (bf16[272,512]{1,0:T(8,128)(2,1)S(1)}, bf16[272,512]{1,0:T(8,128)(2,1)S(1)}, u32[]{:S(2)}, u32[]{:S(2)}) collective-permute-start(bf16[272,512]{1,0:T(8,128)(2,1)S(1)} %collective-permute-done.13.refs_6_.refs_7_), channel_id=1, source_target_pairs={{0,4},{6,2},{1,5},{7,3},{4,8},{10,6},{5,9},{11,7},{8,12},{14,10},{... | collective-permute-start | bytes 835592 | tf_op jit(solution)/shard_map/ppermute | solution.py:240
  44.9 11.6 %collective-permute-start.19 = (bf16[272,512]{1,0:T(8,128)(2,1)S(1)}, bf16[272,512]{1,0:T(8,128)(2,1)S(1)}, u32[]{:S(2)}, u32[]{:S(2)}) collective-permute-start(bf16[272,512]{1,0:T(8,128)(2,1)S(1)} %collective-permute-done.10.refs_6_.refs_7_), channel_id=1, source_target_pairs={{0,4},{6,2},{1,5},{7,3},{4,8},{10,6},{5,9},{11,7},{8,12},{14,10},{... | collective-permute-start | bytes 835592 | tf_op jit(solution)/shard_map/ppermute | solution.py:240
  47.7 11.6 %collective-permute-start.14 = (bf16[256,512]{1,0:T(8,128)(2,1)S(1)}, bf16[256,512]{1,0:T(8,128)(2,1)S(1)}, u32[]{:S(2)}, u32[]{:S(2)}) collective-permute-start(bf16[256,512]{1,0:T(8,128)(2,1)S(1)} %collective-permute-done.9.refs_7_.refs_8_), channel_id=1, source_target_pairs={{0,4},{6,2},{1,5},{7,3},{4,8},{10,6},{5,9},{11,7},{8,12},{14,10},{... | collective-permute-start | bytes 786440 | tf_op jit(solution)/shard_map/ppermute | solution.py:240
  54.3 5.0 %collective-permute-start.18 = (bf16[256,512]{1,0:T(8,128)(2,1)S(1)}, bf16[256,512]{1,0:T(8,128)(2,1)S(1)}, u32[]{:S(2)}, u32[]{:S(2)}) collective-permute-start(bf16[256,512]{1,0:T(8,128)(2,1)S(1)} %get-tuple-element.149), channel_id=1, source_target_pairs={{0,2},{2,0},{4,6},{6,4},{8,10},{10,8},{12,14},{14,12},{16,18},{18,... | collective-permute-start | bytes 786440 | tf_op jit(solution)/shard_map/ppermute | solution.py:243
  54.4 4.9 %collective-permute-start.17 = (bf16[256,512]{1,0:T(8,128)(2,1)S(1)}, bf16[256,512]{1,0:T(8,128)(2,1)S(1)}, u32[]{:S(2)}, u32[]{:S(2)}) collective-permute-start(bf16[256,512]{1,0:T(8,128)(2,1)S(1)} %get-tuple-element.147), channel_id=1, source_target_pairs={{0,2},{2,0},{4,6},{6,4},{8,10},{10,8},{12,14},{14,12},{16,18},{18,... | collective-permute-start | bytes 786440 | tf_op jit(solution)/shard_map/ppermute | solution.py:243
  60.1 12.4 %collective-permute-start.22 = (bf16[512,512]{1,0:T(8,128)(2,1)S(1)}, bf16[512,512]{1,0:T(8,128)(2,1)S(1)}, u32[]{:S(2)}, u32[]{:S(2)}) collective-permute-start(bf16[512,512]{1,0:T(8,128)(2,1)S(1)} %window.31), channel_id=1, source_target_pairs={{0,1},{1,0},{2,3},{3,2},{4,5},{5,4},{6,7},{7,6},{8,9},{9,8},{10,11... | collective-permute-start | bytes 1572872 | tf_op jit(solution)/shard_map/ppermute | solution.py:246
  67.2 2.1 %collective-permute-start.21 = (bf16[256,512]{1,0:T(8,128)(2,1)S(1)}, bf16[256,512]{1,0:T(8,128)(2,1)S(1)}, u32[]{:S(2)}, u32[]{:S(2)}) collective-permute-start(bf16[256,512]{1,0:T(8,128)(2,1)S(1)} %get-tuple-element.174), channel_id=1, source_target_pairs={{0,2},{2,0},{4,6},{6,4},{8,10},{10,8},{12,14},{14,12},{16,18},{18,... | collective-permute-start | bytes 786440 | tf_op jit(solution)/shard_map/ppermute | solution.py:243
  67.3 2.0 %collective-permute-start.20 = (bf16[256,512]{1,0:T(8,128)(2,1)S(1)}, bf16[256,512]{1,0:T(8,128)(2,1)S(1)}, u32[]{:S(2)}, u32[]{:S(2)}) collective-permute-start(bf16[256,512]{1,0:T(8,128)(2,1)S(1)} %get-tuple-element.172), channel_id=1, source_target_pairs={{0,2},{2,0},{4,6},{6,4},{8,10},{10,8},{12,14},{14,12},{16,18},{18,... | collective-permute-start | bytes 786440 | tf_op jit(solution)/shard_map/ppermute | solution.py:243

commit v7 on v6

--- a/solution.py
+++ b/solution.py
@@ -255,7 +255,6 @@
     totals["own"] = [[token]]
     coming = {"core": [chip_next(chunk) for chunk in core], "own": [chip_next(hold(chunk, token)) for chunk in own]}
     other = sub_swap(whole)
-    far = sub_swap(hold(core_whole, other))
 
     reach = STEPS // 2
     legs = [(kind, step) for step in range(1, reach) for kind in ("core", "own")] + [("core", reach)]
@@ -288,6 +287,9 @@
             if step < reach - (kind == "own"):
                 sent.append(chip_next(pack))
             arrivals += 1
+            if arrivals == 2:
+                other = hold(other, pack)
+                far = sub_swap(hold(core_whole, other))
             if arrivals == FAR_AT:
                 far = hold(hold(far, pack), token)
                 packs["far"] = [(far, None)]

time: 73.7 us -> 73.8 us (level)
  waiting for transfers between devices: 30.4 us -> 33.1 us
  starting transfers between devices: 18.2 us -> 15.5 us
    ppermute x14, waiting for transfers between devices: 21.8 us -> 28.2 us  [chip_next(): return lax.ppermute(value, ('dp', 'sub'), onward)]
    ppermute x3, waiting for transfers between devices: 7.04 us -> 3.32 us  [sub_swap(): return lax.ppermute(value, 'sub', [(0, 1), (1, 0)])]
    ppermute x14, starting transfers between devices: 10.4 us -> 7.25 us  [chip_next(): return lax.ppermute(value, ('dp', 'sub'), onward)]
  transfers between devices with their start and end apart: 23 -> 23, of which waited for: 16 -> 15; matrix products, arithmetic and copies ran while one was open for 0% -> 0% of each run, Pallas kernels for 28% -> 28%
where the time goes in v7:
time: 73.8 us; the launch traced here: 73.6 us
  waiting for transfers between devices  33.1 us (45%)
  Pallas kernels  22.9 us (31%)
  starting transfers between devices  15.5 us (21%)
  local copies, waits for them, and re-layouts  1.93 us (3%)
    ppermute x14, waiting for transfers between devices, chip_next(): return lax.ppermute(value, ('dp', 'sub'), onward)  28.2 us
    pallas_call x25, Pallas kernels, call(): pl.pallas_call(kernel, out_shape=[jax.ShapeDtypeStruct(shape, dtype) for...  22.9 us
    ppermute x14, starting transfers between devices, chip_next(): return lax.ppermute(value, ('dp', 'sub'), onward)  7.25 us
    ppermute x3, starting transfers between devices, sub_swap(): return lax.ppermute(value, 'sub', [(0, 1), (1, 0)])  6.84 us
    ppermute x3, waiting for transfers between devices, sub_swap(): return lax.ppermute(value, 'sub', [(0, 1), (1, 0)])  3.32 us
    unnamed x8, local copies, waits for them, and re-layouts  1.93 us
    ppermute x6, waiting for transfers between devices, core_swap(): return lax.ppermute(value, 'dp', cores)  1.56 us
  transfers between devices with their start and end apart: 23, of which 15 were waited for; matrix products, arithmetic and copies ran while one was open for 0% of the time, Pallas kernels for 28%

profile of v7, /device:TPU:2, one launch (start us, length us, event | category | flops | bytes accessed | tf_op | source)
XLA Modules:
  0.0 73.6 jit_solution(13958162590858718775)
XLA Ops:
  0.7 1.2 %copy-done = f32[512,512]{1,0:T(8,128)S(1)} copy-done((f32[512,512]{1,0:T(8,128)S(1)}, f32[512,512]{1,0:T(8,128)}, u32[]{:S(2)}) %copy-start) | copy-done | bytes 1048600
  2.1 1.5 %collective-permute-done.refs_0_.first_ref.refs_3_ = bf16[272,512]{1,0:T(8,128)(2,1)S(1)} collective-permute-done((bf16[272,512]{1,0:T(8,128)(2,1)S(1)}, bf16[272,512]{1,0:T(8,128)(2,1)S(1)}, u32[]{:S(2)}, u32[]{:S(2)}) %collective-permute-start) | collective-permute-done | bytes 278560 | tf_op jit(solution)/shard_map/ppermute | solution.py:243
  3.8 2.3 %collective-permute-start.7 = (bf16[528,512]{1,0:T(8,128)(2,1)S(1)}, bf16[528,512]{1,0:T(8,128)(2,1)S(1)}, u32[]{:S(2)}, u32[]{:S(2)}) collective-permute-start(bf16[528,512]{1,0:T(8,128)(2,1)S(1)} %get-tuple-element.91.row_ref.own_ref.refs_0_), channel_id=1, source_target_pairs={{0,1},{1,0},{2,3},{3,2},{4,5},{5,4},{6,7},{7,6},{8,9},{9,8},{10,11... | collective-permute-start | bytes 1622024 | tf_op jit(solution)/shard_map/ppermute | solution.py:246
  6.3 1.9 %collective-permute-start.2 = (bf16[256,512]{1,0:T(8,128)(2,1)S(1)}, bf16[256,512]{1,0:T(8,128)(2,1)S(1)}, u32[]{:S(2)}, u32[]{:S(2)}) collective-permute-start(bf16[256,512]{1,0:T(8,128)(2,1)S(1)} %collective-permute-done.1.refs_1_.refs_4_), channel_id=1, source_target_pairs={{0,4},{6,2},{1,5},{7,3},{4,8},{10,6},{5,9},{11,7},{8,12},{14,10},{... | collective-permute-start | bytes 786440 | tf_op jit(solution)/shard_map/ppermute | solution.py:240
  8.2 1.5 %own_rows.1 = (f32[512,128]{1,0:T(8,128)S(1)}, f32[512,512]{1,0:T(8,128)S(1)}, bf16[528,512]{1,0:T(8,128)(2,1)S(1)}) custom-call(bf16[528,512]{1,0:T(8,128)(2,1)S(1)} %get-tuple-element.91.row_ref.own_ref.refs_0_, bf16[528,512]{1,0:T(8,128)(2,1)S(1)} %get-tuple-element.91.row_ref.own_ref.refs_0_, ...), custom_call_target="tpu_custom_call" | custom-call | flops 4294967296 | tf_op jit(solution)/shard_map/own_rows/pallas_call | solution.py:41
  9.7 2.0 %collective-permute-start.5 = (bf16[272,512]{1,0:T(8,128)(2,1)S(1)}, bf16[272,512]{1,0:T(8,128)(2,1)S(1)}, u32[]{:S(2)}, u32[]{:S(2)}) collective-permute-start(bf16[272,512]{1,0:T(8,128)(2,1)S(1)} %get-tuple-element.101), channel_id=1, source_target_pairs={{0,4},{6,2},{1,5},{7,3},{4,8},{10,6},{5,9},{11,7},{8,12},{14,10},{... | collective-permute-start | bytes 835592 | tf_op jit(solution)/shard_map/ppermute | solution.py:240
  11.7 3.1 %collective-permute-start.4 = (bf16[256,512]{1,0:T(8,128)(2,1)S(1)}, bf16[256,512]{1,0:T(8,128)(2,1)S(1)}, u32[]{:S(2)}, u32[]{:S(2)}) collective-permute-start(bf16[256,512]{1,0:T(8,128)(2,1)S(1)} %get-tuple-element.100), channel_id=1, source_target_pairs={{0,4},{6,2},{1,5},{7,3},{4,8},{10,6},{5,9},{11,7},{8,12},{14,10},{... | collective-permute-start | bytes 786440 | tf_op jit(solution)/shard_map/ppermute | solution.py:240
  15.0 3.8 %collective-permute-done.3.refs_6_.refs_3_.refs_2_ = bf16[272,512]{1,0:T(8,128)(2,1)S(1)} collective-permute-done((bf16[272,512]{1,0:T(8,128)(2,1)S(1)}, bf16[272,512]{1,0:T(8,128)(2,1)S(1)}, u32[]{:S(2)}, u32[]{:S(2)}) %collective-permute-start.3) | collective-permute-done | bytes 278560 | tf_op jit(solution)/shard_map/ppermute | solution.py:240
  18.8 2.8 %collective-permute-done.2.refs_7_.refs_4_.refs_3_ = bf16[256,512]{1,0:T(8,128)(2,1)S(1)} collective-permute-done((bf16[256,512]{1,0:T(8,128)(2,1)S(1)}, bf16[256,512]{1,0:T(8,128)(2,1)S(1)}, u32[]{:S(2)}, u32[]{:S(2)}) %collective-permute-start.2) | collective-permute-done | bytes 262176 | tf_op jit(solution)/shard_map/ppermute | solution.py:240
  21.6 1.4 %collective-permute-start.11 = (bf16[528,512]{1,0:T(8,128)(2,1)S(1)}, bf16[528,512]{1,0:T(8,128)(2,1)S(1)}, u32[]{:S(2)}, u32[]{:S(2)}) collective-permute-start(bf16[528,512]{1,0:T(8,128)(2,1)S(1)} %get-tuple-element.124), channel_id=1, source_target_pairs={{0,1},{1,0},{2,3},{3,2},{4,5},{5,4},{6,7},{7,6},{8,9},{9,8},{10,11... | collective-permute-start | bytes 1622024 | tf_op jit(solution)/shard_map/ppermute | solution.py:246
  23.0 1.3 %window.19 = (f32[512,512]{1,0:T(8,128)S(1)}, f32[512,512]{1,0:T(8,128)S(1)}) custom-call(bf16[528,512]{1,0:T(8,128)(2,1)S(1)} %get-tuple-element.91.row_ref.own_ref.refs_0_, f32[512,128]{1,0:T(8,128)S(1)} %get-tuple-element.95.refs_1_, f32[512,512]{1,0:T(8,128)S(1)} %get-tuple-element.97.refs_2_, ...), custom_call_target="tpu_custom_call", output_to_operand_aliasing={{0}: (2, {})} | custom-call | flops 2147483648 | tf_op jit(solution)/shard_map/window/pallas_call | solution.py:41
  24.6 2.8 %collective-permute-done.4.refs_8_.refs_4_ = bf16[256,512]{1,0:T(8,128)(2,1)S(1)} collective-permute-done((bf16[256,512]{1,0:T(8,128)(2,1)S(1)}, bf16[256,512]{1,0:T(8,128)(2,1)S(1)}, u32[]{:S(2)}, u32[]{:S(2)}) %collective-permute-start.4) | collective-permute-done | bytes 262176 | tf_op jit(solution)/shard_map/ppermute | solution.py:240
  27.4 1.3 %window.20 = (f32[512,512]{1,0:T(8,128)S(1)}, f32[512,512]{1,0:T(8,128)S(1)}) custom-call(bf16[528,512]{1,0:T(8,128)(2,1)S(1)} %get-tuple-element.91.row_ref.own_ref.refs_0_, f32[512,128]{1,0:T(8,128)S(1)} %get-tuple-element.95.refs_1_, f32[512,512]{1,0:T(8,128)S(1)} %get-tuple-element.107.refs_2_, ...), custom_call_target="tpu_custom_call", output_to_operand_aliasing={{0}: (2, {}), {1}: (6, {})} | custom-call | flops 2147483648 | tf_op jit(solution)/shard_map/window/pallas_call | solution.py:41
  28.7 1.6 %collective-permute-done.8.refs_3_.refs_7_ = bf16[272,512]{1,0:T(8,128)(2,1)S(1)} collective-permute-done((bf16[272,512]{1,0:T(8,128)(2,1)S(1)}, bf16[272,512]{1,0:T(8,128)(2,1)S(1)}, u32[]{:S(2)}, u32[]{:S(2)}) %collective-permute-start.8) | collective-permute-done | bytes 278560 | tf_op jit(solution)/shard_map/ppermute | solution.py:240
  30.4 1.5 %other_rows.1 = (f32[512,128]{1,0:T(8,128)S(1)}, f32[512,512]{1,0:T(8,128)S(1)}) custom-call(bf16[528,512]{1,0:T(8,128)(2,1)S(1)} %collective-permute-done.7.row_ref.refs_0_, bf16[528,512]{1,0:T(8,128)(2,1)S(1)} %get-tuple-element.91.row_ref.own_ref.refs_0_, bf16[272,512]{1,0:T(8,128)(2,1)S(1)} %collective-permute-done.refs_0_.first_ref.refs_3_, ...), custom_call_target="tpu_custom_call" | custom-call | flops 4294967296 | tf_op jit(solution)/shard_map/other_rows/pallas_call | solution.py:41
  31.9 1.3 %collective-permute-done.6.refs_4_.refs_8_ = bf16[256,512]{1,0:T(8,128)(2,1)S(1)} collective-permute-done((bf16[256,512]{1,0:T(8,128)(2,1)S(1)}, bf16[256,512]{1,0:T(8,128)(2,1)S(1)}, u32[]{:S(2)}, u32[]{:S(2)}) %collective-permute-start.6) | collective-permute-done | bytes 262176 | tf_op jit(solution)/shard_map/ppermute | solution.py:240
  33.9 0.8 %window.22.refs_2_ = f32[512,512]{1,0:T(8,128)S(1)} custom-call(bf16[528,512]{1,0:T(8,128)(2,1)S(1)} %collective-permute-done.7.row_ref.refs_0_, f32[512,128]{1,0:T(8,128)S(1)} %get-tuple-element.117.refs_1_, f32[512,512]{1,0:T(8,128)S(1)} %window.21.refs_2_, ...), custom_call_target="tpu_custom_call", output_to_operand_aliasing={{}: (2, {})} | custom-call | flops 1073741824 | tf_op jit(solution)/shard_map/window/pallas_call | solution.py:41
  34.7 0.8 %window.23.refs_2_ = f32[512,512]{1,0:T(8,128)S(1)} custom-call(bf16[528,512]{1,0:T(8,128)(2,1)S(1)} %collective-permute-done.7.row_ref.refs_0_, f32[512,128]{1,0:T(8,128)S(1)} %get-tuple-element.117.refs_1_, f32[512,512]{1,0:T(8,128)S(1)} %window.22.refs_2_, ...), custom_call_target="tpu_custom_call", output_to_operand_aliasing={{}: (2, {})} | custom-call | flops 1073741824 | tf_op jit(solution)/shard_map/window/pallas_call | solution.py:41
  35.4 2.5 %collective-permute-done.12.refs_7_.refs_8_ = bf16[256,512]{1,0:T(8,128)(2,1)S(1)} collective-permute-done((bf16[256,512]{1,0:T(8,128)(2,1)S(1)}, bf16[256,512]{1,0:T(8,128)(2,1)S(1)}, u32[]{:S(2)}, u32[]{:S(2)}) %collective-permute-start.12) | collective-permute-done | bytes 262176 | tf_op jit(solution)/shard_map/ppermute | solution.py:240
  38.0 3.0 %collective-permute-done.13.refs_6_.refs_7_ = bf16[272,512]{1,0:T(8,128)(2,1)S(1)} collective-permute-done((bf16[272,512]{1,0:T(8,128)(2,1)S(1)}, bf16[272,512]{1,0:T(8,128)(2,1)S(1)}, u32[]{:S(2)}, u32[]{:S(2)}) %collective-permute-start.13) | collective-permute-done | bytes 278560 | tf_op jit(solution)/shard_map/ppermute | solution.py:240
  43.9 1.3 %window.27 = (f32[512,512]{1,0:T(8,128)S(1)}, f32[512,512]{1,0:T(8,128)S(1)}) custom-call(bf16[528,512]{1,0:T(8,128)(2,1)S(1)} %collective-permute-done.7.row_ref.refs_0_, f32[512,128]{1,0:T(8,128)S(1)} %get-tuple-element.117.refs_1_, f32[512,512]{1,0:T(8,128)S(1)} %window.23.refs_2_, ...), custom_call_target="tpu_custom_call", output_to_operand_aliasing={{0}: (2, {}), {1}: (5, {})} | custom-call | flops 2147483648 | tf_op jit(solution)/shard_map/window/pallas_call | solution.py:41
  45.3 1.5 %collective-permute-done.9.refs_7_.refs_8_ = bf16[256,512]{1,0:T(8,128)(2,1)S(1)} collective-permute-done((bf16[256,512]{1,0:T(8,128)(2,1)S(1)}, bf16[256,512]{1,0:T(8,128)(2,1)S(1)}, u32[]{:S(2)}, u32[]{:S(2)}) %collective-permute-start.9) | collective-permute-done | bytes 262176 | tf_op jit(solution)/shard_map/ppermute | solution.py:240
  46.8 1.3 %window.28 = (f32[512,512]{1,0:T(8,128)S(1)}, f32[512,512]{1,0:T(8,128)S(1)}) custom-call(bf16[528,512]{1,0:T(8,128)(2,1)S(1)} %collective-permute-done.7.row_ref.refs_0_, f32[512,128]{1,0:T(8,128)S(1)} %get-tuple-element.117.refs_1_, f32[512,512]{1,0:T(8,128)S(1)} %get-tuple-element.140.refs_2_, ...), custom_call_target="tpu_custom_call", output_to_operand_aliasing={{0}: (2, {}), {1}: (5, {})} | custom-call | tf_op jit(solution)/shard_map/window/pallas_call | solution.py:41
  48.1 1.5 %collective-permute-done.15.refs_4_.refs_5_ = bf16[256,512]{1,0:T(8,128)(2,1)S(1)} collective-permute-done((bf16[256,512]{1,0:T(8,128)(2,1)S(1)}, bf16[256,512]{1,0:T(8,128)(2,1)S(1)}, u32[]{:S(2)}, u32[]{:S(2)}) %collective-permute-start.15) | collective-permute-done | bytes 262176 | tf_op jit(solution)/shard_map/ppermute | solution.py:240
  49.6 3.0 %collective-permute-done.16.refs_3_.refs_4_ = bf16[272,512]{1,0:T(8,128)(2,1)S(1)} collective-permute-done((bf16[272,512]{1,0:T(8,128)(2,1)S(1)}, bf16[272,512]{1,0:T(8,128)(2,1)S(1)}, u32[]{:S(2)}, u32[]{:S(2)}) %collective-permute-start.16) | collective-permute-done | bytes 278560 | tf_op jit(solution)/shard_map/ppermute | solution.py:240
  54.6 3.7 %collective-permute-done.14.refs_6_.refs_4_ = bf16[256,512]{1,0:T(8,128)(2,1)S(1)} collective-permute-done((bf16[256,512]{1,0:T(8,128)(2,1)S(1)}, bf16[256,512]{1,0:T(8,128)(2,1)S(1)}, u32[]{:S(2)}, u32[]{:S(2)}) %collective-permute-start.14) | collective-permute-done | bytes 262176 | tf_op jit(solution)/shard_map/ppermute | solution.py:240
  59.1 3.1 %collective-permute-start.22 = (bf16[512,512]{1,0:T(8,128)(2,1)S(1)}, bf16[512,512]{1,0:T(8,128)(2,1)S(1)}, u32[]{:S(2)}, u32[]{:S(2)}) collective-permute-start(bf16[512,512]{1,0:T(8,128)(2,1)S(1)} %window.31), channel_id=1, source_target_pairs={{0,1},{1,0},{2,3},{3,2},{4,5},{5,4},{6,7},{7,6},{8,9},{9,8},{10,11... | collective-permute-start | bytes 1572872 | tf_op jit(solution)/shard_map/ppermute | solution.py:246
  62.2 1.3 %window.32 = (f32[512,512]{1,0:T(8,128)S(1)}, f32[512,512]{1,0:T(8,128)S(1)}) custom-call(bf16[528,512]{1,0:T(8,128)(2,1)S(1)} %get-tuple-element.91.row_ref.own_ref.refs_0_, f32[512,128]{1,0:T(8,128)S(1)} %get-tuple-element.95.refs_1_, f32[512,512]{1,0:T(8,128)S(1)} %get-tuple-element.153.refs_2_, ...), custom_call_target="tpu_custom_call", output_to_operand_aliasing={{0}: (2, {}), {1}: (6, {})} | custom-call | tf_op jit(solution)/shard_map/window/pallas_call | solution.py:41
  63.6 1.3 %window.33 = (f32[512,512]{1,0:T(8,128)S(1)}, f32[512,512]{1,0:T(8,128)S(1)}) custom-call(bf16[528,512]{1,0:T(8,128)(2,1)S(1)} %get-tuple-element.91.row_ref.own_ref.refs_0_, f32[512,128]{1,0:T(8,128)S(1)} %get-tuple-element.95.refs_1_, f32[512,512]{1,0:T(8,128)S(1)} %get-tuple-element.159.refs_2_, ...), custom_call_target="tpu_custom_call", output_to_operand_aliasing={{0}: (2, {}), {1}: (6, {})} | custom-call | tf_op jit(solution)/shard_map/window/pallas_call | solution.py:41
  64.9 1.3 %window.34 = (f32[512,512]{1,0:T(8,128)S(1)}, f32[512,512]{1,0:T(8,128)S(1)}) custom-call(bf16[528,512]{1,0:T(8,128)(2,1)S(1)} %get-tuple-element.91.row_ref.own_ref.refs_0_, f32[512,128]{1,0:T(8,128)S(1)} %get-tuple-element.95.refs_1_, f32[512,512]{1,0:T(8,128)S(1)} %get-tuple-element.165.refs_2_, ...), custom_call_target="tpu_custom_call", output_to_operand_aliasing={{0}: (2, {}), {1}: (6, {})} | custom-call | tf_op jit(solution)/shard_map/window/pallas_call | solution.py:41
  69.2 3.3 %collective-permute-done.22.refs_2_ = bf16[512,512]{1,0:T(8,128)(2,1)S(1)} collective-permute-done((bf16[512,512]{1,0:T(8,128)(2,1)S(1)}, bf16[512,512]{1,0:T(8,128)(2,1)S(1)}, u32[]{:S(2)}, u32[]{:S(2)}) %collective-permute-start.22) | collective-permute-done | bytes 524320 | tf_op jit(solution)/shard_map/ppermute | solution.py:246
  72.5 1.1 %finish.1 = f32[512,512]{1,0:T(8,128)} custom-call(f32[512,512]{1,0:T(8,128)S(1)} %window.37.here_ref, bf16[256,512]{1,0:T(8,128)(2,1)S(1)} %collective-permute-done.20.refs_0_, bf16[256,512]{1,0:T(8,128)(2,1)S(1)} %collective-permute-done.21.refs_1_, bf16[512,512]{1,0:T(8,128)(2,1)S(1)} %collective-permute-done.22.refs_2_), custom_call_target="tpu_custom_call" | custom-call | tf_op jit(solution)/shard_map/finish/pallas_call | solution.py:41
  (47 shorter events, 10.9 us)
Async XLA Ops:
  0.0 0.7 copy-start.3
  0.0 0.7 copy-start.2
  0.0 0.7 copy-start.1
  0.7 1.2 %copy-start = (f32[512,512]{1,0:T(8,128)S(1)}, f32[512,512]{1,0:T(8,128)}, u32[]{:S(2)}) copy-start(f32[512,512]{1,0:T(8,128)} %views_ref.1) | copy-start | bytes 3145732
  2.0 1.6 %collective-permute-start = (bf16[272,512]{1,0:T(8,128)(2,1)S(1)}, bf16[272,512]{1,0:T(8,128)(2,1)S(1)}, u32[]{:S(2)}, u32[]{:S(2)}) collective-permute-start(bf16[272,512]{1,0:T(8,128)(2,1)S(1)} %get-tuple-element.101), channel_id=1, source_target_pairs={{0,2},{2,0},{4,6},{6,4},{8,10},{10,8},{12,14},{14,12},{16,18},{18,... | collective-permute-start | bytes 835592 | tf_op jit(solution)/shard_map/ppermute | solution.py:243
  3.7 2.6 %collective-permute-start.1 = (bf16[256,512]{1,0:T(8,128)(2,1)S(1)}, bf16[256,512]{1,0:T(8,128)(2,1)S(1)}, u32[]{:S(2)}, u32[]{:S(2)}) collective-permute-start(bf16[256,512]{1,0:T(8,128)(2,1)S(1)} %get-tuple-element.100), channel_id=1, source_target_pairs={{0,2},{2,0},{4,6},{6,4},{8,10},{10,8},{12,14},{14,12},{16,18},{18,... | collective-permute-start | bytes 786440 | tf_op jit(solution)/shard_map/ppermute | solution.py:243
  3.8 17.8 %collective-permute-start.7 = (bf16[528,512]{1,0:T(8,128)(2,1)S(1)}, bf16[528,512]{1,0:T(8,128)(2,1)S(1)}, u32[]{:S(2)}, u32[]{:S(2)}) collective-permute-start(bf16[528,512]{1,0:T(8,128)(2,1)S(1)} %get-tuple-element.91.row_ref.own_ref.refs_0_), channel_id=1, source_target_pairs={{0,1},{1,0},{2,3},{3,2},{4,5},{5,4},{6,7},{7,6},{8,9},{9,8},{10,11... | collective-permute-start | bytes 1622024 | tf_op jit(solution)/shard_map/ppermute | solution.py:246
  6.1 12.7 %collective-permute-start.3 = (bf16[272,512]{1,0:T(8,128)(2,1)S(1)}, bf16[272,512]{1,0:T(8,128)(2,1)S(1)}, u32[]{:S(2)}, u32[]{:S(2)}) collective-permute-start(bf16[272,512]{1,0:T(8,128)(2,1)S(1)} %collective-permute-done.refs_0_.first_ref.refs_3_), channel_id=1, source_target_pairs={{0,4},{6,2},{1,5},{7,3},{4,8},{10,6},{5,9},{11,7},{8,12},{14,10},{... | collective-permute-start | bytes 835592 | tf_op jit(solution)/shard_map/ppermute | solution.py:240
  6.3 15.3 %collective-permute-start.2 = (bf16[256,512]{1,0:T(8,128)(2,1)S(1)}, bf16[256,512]{1,0:T(8,128)(2,1)S(1)}, u32[]{:S(2)}, u32[]{:S(2)}) collective-permute-start(bf16[256,512]{1,0:T(8,128)(2,1)S(1)} %collective-permute-done.1.refs_1_.refs_4_), channel_id=1, source_target_pairs={{0,4},{6,2},{1,5},{7,3},{4,8},{10,6},{5,9},{11,7},{8,12},{14,10},{... | collective-permute-start | bytes 786440 | tf_op jit(solution)/shard_map/ppermute | solution.py:240
  9.7 14.8 %collective-permute-start.5 = (bf16[272,512]{1,0:T(8,128)(2,1)S(1)}, bf16[272,512]{1,0:T(8,128)(2,1)S(1)}, u32[]{:S(2)}, u32[]{:S(2)}) collective-permute-start(bf16[272,512]{1,0:T(8,128)(2,1)S(1)} %get-tuple-element.101), channel_id=1, source_target_pairs={{0,4},{6,2},{1,5},{7,3},{4,8},{10,6},{5,9},{11,7},{8,12},{14,10},{... | collective-permute-start | bytes 835592 | tf_op jit(solution)/shard_map/ppermute | solution.py:240
  11.7 15.7 %collective-permute-start.4 = (bf16[256,512]{1,0:T(8,128)(2,1)S(1)}, bf16[256,512]{1,0:T(8,128)(2,1)S(1)}, u32[]{:S(2)}, u32[]{:S(2)}) collective-permute-start(bf16[256,512]{1,0:T(8,128)(2,1)S(1)} %get-tuple-element.100), channel_id=1, source_target_pairs={{0,4},{6,2},{1,5},{7,3},{4,8},{10,6},{5,9},{11,7},{8,12},{14,10},{... | collective-permute-start | bytes 786440 | tf_op jit(solution)/shard_map/ppermute | solution.py:240
  18.8 11.6 %collective-permute-start.8 = (bf16[272,512]{1,0:T(8,128)(2,1)S(1)}, bf16[272,512]{1,0:T(8,128)(2,1)S(1)}, u32[]{:S(2)}, u32[]{:S(2)}) collective-permute-start(bf16[272,512]{1,0:T(8,128)(2,1)S(1)} %collective-permute-done.3.refs_6_.refs_3_.refs_2_), channel_id=1, source_target_pairs={{0,4},{6,2},{1,5},{7,3},{4,8},{10,6},{5,9},{11,7},{8,12},{14,10},{... | collective-permute-start | bytes 835592 | tf_op jit(solution)/shard_map/ppermute | solution.py:240
  21.6 11.6 %collective-permute-start.6 = (bf16[256,512]{1,0:T(8,128)(2,1)S(1)}, bf16[256,512]{1,0:T(8,128)(2,1)S(1)}, u32[]{:S(2)}, u32[]{:S(2)}) collective-permute-start(bf16[256,512]{1,0:T(8,128)(2,1)S(1)} %collective-permute-done.2.refs_7_.refs_4_.refs_3_), channel_id=1, source_target_pairs={{0,4},{6,2},{1,5},{7,3},{4,8},{10,6},{5,9},{11,7},{8,12},{14,10},{... | collective-permute-start | bytes 786440 | tf_op jit(solution)/shard_map/ppermute | solution.py:240
  21.6 19.4 %collective-permute-start.11 = (bf16[528,512]{1,0:T(8,128)(2,1)S(1)}, bf16[528,512]{1,0:T(8,128)(2,1)S(1)}, u32[]{:S(2)}, u32[]{:S(2)}) collective-permute-start(bf16[528,512]{1,0:T(8,128)(2,1)S(1)} %get-tuple-element.124), channel_id=1, source_target_pairs={{0,1},{1,0},{2,3},{3,2},{4,5},{5,4},{6,7},{7,6},{8,9},{9,8},{10,11... | collective-permute-start | bytes 1622024 | tf_op jit(solution)/shard_map/ppermute | solution.py:246
  27.4 10.6 %collective-permute-start.12 = (bf16[256,512]{1,0:T(8,128)(2,1)S(1)}, bf16[256,512]{1,0:T(8,128)(2,1)S(1)}, u32[]{:S(2)}, u32[]{:S(2)}) collective-permute-start(bf16[256,512]{1,0:T(8,128)(2,1)S(1)} %collective-permute-done.4.refs_8_.refs_4_), channel_id=1, source_target_pairs={{0,4},{6,2},{1,5},{7,3},{4,8},{10,6},{5,9},{11,7},{8,12},{14,10},{... | collective-permute-start | bytes 786440 | tf_op jit(solution)/shard_map/ppermute | solution.py:240
  27.4 13.6 %collective-permute-start.13 = (bf16[272,512]{1,0:T(8,128)(2,1)S(1)}, bf16[272,512]{1,0:T(8,128)(2,1)S(1)}, u32[]{:S(2)}, u32[]{:S(2)}) collective-permute-start(bf16[272,512]{1,0:T(8,128)(2,1)S(1)} %collective-permute-done.5.refs_7_.refs_3_), channel_id=1, source_target_pairs={{0,4},{6,2},{1,5},{7,3},{4,8},{10,6},{5,9},{11,7},{8,12},{14,10},{... | collective-permute-start | bytes 835592 | tf_op jit(solution)/shard_map/ppermute | solution.py:240
  30.4 13.6 %collective-permute-start.10 = (bf16[272,512]{1,0:T(8,128)(2,1)S(1)}, bf16[272,512]{1,0:T(8,128)(2,1)S(1)}, u32[]{:S(2)}, u32[]{:S(2)}) collective-permute-start(bf16[272,512]{1,0:T(8,128)(2,1)S(1)} %collective-permute-done.8.refs_3_.refs_7_), channel_id=1, source_target_pairs={{0,4},{6,2},{1,5},{7,3},{4,8},{10,6},{5,9},{11,7},{8,12},{14,10},{... | collective-permute-start | bytes 835592 | tf_op jit(solution)/shard_map/ppermute | solution.py:240
  33.2 13.6 %collective-permute-start.9 = (bf16[256,512]{1,0:T(8,128)(2,1)S(1)}, bf16[256,512]{1,0:T(8,128)(2,1)S(1)}, u32[]{:S(2)}, u32[]{:S(2)}) collective-permute-start(bf16[256,512]{1,0:T(8,128)(2,1)S(1)} %collective-permute-done.6.refs_4_.refs_8_), channel_id=1, source_target_pairs={{0,4},{6,2},{1,5},{7,3},{4,8},{10,6},{5,9},{11,7},{8,12},{14,10},{... | collective-permute-start | bytes 786440 | tf_op jit(solution)/shard_map/ppermute | solution.py:240
  38.0 11.6 %collective-permute-start.15 = (bf16[256,512]{1,0:T(8,128)(2,1)S(1)}, bf16[256,512]{1,0:T(8,128)(2,1)S(1)}, u32[]{:S(2)}, u32[]{:S(2)}) collective-permute-start(bf16[256,512]{1,0:T(8,128)(2,1)S(1)} %collective-permute-done.12.refs_7_.refs_8_), channel_id=1, source_target_pairs={{0,4},{6,2},{1,5},{7,3},{4,8},{10,6},{5,9},{11,7},{8,12},{14,10},{... | collective-permute-start | bytes 786440 | tf_op jit(solution)/shard_map/ppermute | solution.py:240
  41.0 11.6 %collective-permute-start.16 = (bf16[272,512]{1,0:T(8,128)(2,1)S(1)}, bf16[272,512]{1,0:T(8,128)(2,1)S(1)}, u32[]{:S(2)}, u32[]{:S(2)}) collective-permute-start(bf16[272,512]{1,0:T(8,128)(2,1)S(1)} %collective-permute-done.13.refs_6_.refs_7_), channel_id=1, source_target_pairs={{0,4},{6,2},{1,5},{7,3},{4,8},{10,6},{5,9},{11,7},{8,12},{14,10},{... | collective-permute-start | bytes 835592 | tf_op jit(solution)/shard_map/ppermute | solution.py:240
  43.9 14.4 %collective-permute-start.19 = (bf16[272,512]{1,0:T(8,128)(2,1)S(1)}, bf16[272,512]{1,0:T(8,128)(2,1)S(1)}, u32[]{:S(2)}, u32[]{:S(2)}) collective-permute-start(bf16[272,512]{1,0:T(8,128)(2,1)S(1)} %collective-permute-done.10.refs_6_.refs_7_), channel_id=1, source_target_pairs={{0,4},{6,2},{1,5},{7,3},{4,8},{10,6},{5,9},{11,7},{8,12},{14,10},{... | collective-permute-start | bytes 835592 | tf_op jit(solution)/shard_map/ppermute | solution.py:240
  46.7 11.6 %collective-permute-start.14 = (bf16[256,512]{1,0:T(8,128)(2,1)S(1)}, bf16[256,512]{1,0:T(8,128)(2,1)S(1)}, u32[]{:S(2)}, u32[]{:S(2)}) collective-permute-start(bf16[256,512]{1,0:T(8,128)(2,1)S(1)} %collective-permute-done.9.refs_7_.refs_8_), channel_id=1, source_target_pairs={{0,4},{6,2},{1,5},{7,3},{4,8},{10,6},{5,9},{11,7},{8,12},{14,10},{... | collective-permute-start | bytes 786440 | tf_op jit(solution)/shard_map/ppermute | solution.py:240
  53.3 5.1 %collective-permute-start.18 = (bf16[256,512]{1,0:T(8,128)(2,1)S(1)}, bf16[256,512]{1,0:T(8,128)(2,1)S(1)}, u32[]{:S(2)}, u32[]{:S(2)}) collective-permute-start(bf16[256,512]{1,0:T(8,128)(2,1)S(1)} %get-tuple-element.151), channel_id=1, source_target_pairs={{0,2},{2,0},{4,6},{6,4},{8,10},{10,8},{12,14},{14,12},{16,18},{18,... | collective-permute-start | bytes 786440 | tf_op jit(solution)/shard_map/ppermute | solution.py:243
  53.4 5.0 %collective-permute-start.17 = (bf16[256,512]{1,0:T(8,128)(2,1)S(1)}, bf16[256,512]{1,0:T(8,128)(2,1)S(1)}, u32[]{:S(2)}, u32[]{:S(2)}) collective-permute-start(bf16[256,512]{1,0:T(8,128)(2,1)S(1)} %get-tuple-element.149), channel_id=1, source_target_pairs={{0,2},{2,0},{4,6},{6,4},{8,10},{10,8},{12,14},{14,12},{16,18},{18,... | collective-permute-start | bytes 786440 | tf_op jit(solution)/shard_map/ppermute | solution.py:243
  59.1 13.4 %collective-permute-start.22 = (bf16[512,512]{1,0:T(8,128)(2,1)S(1)}, bf16[512,512]{1,0:T(8,128)(2,1)S(1)}, u32[]{:S(2)}, u32[]{:S(2)}) collective-permute-start(bf16[512,512]{1,0:T(8,128)(2,1)S(1)} %window.31), channel_id=1, source_target_pairs={{0,1},{1,0},{2,3},{3,2},{4,5},{5,4},{6,7},{7,6},{8,9},{9,8},{10,11... | collective-permute-start | bytes 1572872 | tf_op jit(solution)/shard_map/ppermute | solution.py:246
  67.0 2.1 %collective-permute-start.21 = (bf16[256,512]{1,0:T(8,128)(2,1)S(1)}, bf16[256,512]{1,0:T(8,128)(2,1)S(1)}, u32[]{:S(2)}, u32[]{:S(2)}) collective-permute-start(bf16[256,512]{1,0:T(8,128)(2,1)S(1)} %get-tuple-element.176), channel_id=1, source_target_pairs={{0,2},{2,0},{4,6},{6,4},{8,10},{10,8},{12,14},{14,12},{16,18},{18,... | collective-permute-start | bytes 786440 | tf_op jit(solution)/shard_map/ppermute | solution.py:243
  67.1 2.0 %collective-permute-start.20 = (bf16[256,512]{1,0:T(8,128)(2,1)S(1)}, bf16[256,512]{1,0:T(8,128)(2,1)S(1)}, u32[]{:S(2)}, u32[]{:S(2)}) collective-permute-start(bf16[256,512]{1,0:T(8,128)(2,1)S(1)} %get-tuple-element.174), channel_id=1, source_target_pairs={{0,2},{2,0},{4,6},{6,4},{8,10},{10,8},{12,14},{14,12},{16,18},{18,... | collective-permute-start | bytes 786440 | tf_op jit(solution)/shard_map/ppermute | solution.py:243
